TPU v7x, 512 devices: a whole 4x8x8 slice. The times are simulated.
512 devices in a mesh: dp: 64 (over y_lo, z, core), graph: 8 (over x, y_hi).
Axes of the slice: x: 4, y: 8 (y_hi: 2, y_lo: 4; y = y_hi * 4 + y_lo), z: 8, core: 2. Of those that a mesh axis runs over, the one named last changes fastest.
Arguments:
- positions: float32 [64, 8, 3, 128], P('dp', 'graph'), as said below
- species: int32 [64, 8, 128], P('dp', 'graph'), may hold values from 0 to 99
- counts: int32 [64, 8], P('dp', 'graph'), may hold values from 64 to 128, as said below
- source: int32 [64, 8, 2048], P('dp', 'graph'), may hold values from 0 to 191, as said below
- target: int32 [64, 8, 2048], P('dp', 'graph'), may hold values from 0 to 127, as said below
- send_left: int32 [64, 8, 32], P('dp', 'graph'), may hold values from 0 to 31, as said below
- send_right: int32 [64, 8, 32], P('dp', 'graph'), may hold values from 32 to 127, as said below
- energy_ref: float32 [64], P('dp'), may hold values from -32 to 32
- force_ref: float32 [64, 8, 3, 128], P('dp', 'graph'), may hold values from -6 to 6
- stress_ref: float32 [64, 3, 3], P('dp'), may hold values from -3 to 3
- params: float32 [122880], P('dp')
- moment_one: float32 [122880], P('dp'), may hold values from -0.15625 to 0.15625
- moment_two: float32 [122880], P('dp'), may hold values from 1e-06 to 0.001
Outputs:
- new_params: float32 [122880], P('dp')
- new_moment_one: float32 [122880], P('dp')
- new_moment_two: float32 [122880], P('dp')
- forces: float32 [64, 8, 3, 128], P('dp', 'graph')
- energy: float32 [64], P('dp')
- stress: float32 [64, 3, 3], P('dp')
Inputs may be any that keep to these rules, and one draw needn't show every extreme that they name: Slot i of a slab holds a live atom if i < counts. Some slab is full and some slab holds exactly half. Every slot is the target of exactly 16 edges; the edges of a live atom are distinct pairs with sources within 32 slots of it in the order of the cell's atoms along the first coordinate, through ghosts across slab bounds; the sources of edges to slots that are not live lie in the slab. `source`: indices into the extended list of the target's slab; a live edge never joins an atom to itself. `send_left`: A permutation of slots 0 to 31. `send_right`: A permutation of the last 32 live slots. `positions`: live atoms of a slab are ordered along the first coordinate with spacing at least half a mean spacing, slabs are 20 wide and adjacent, a cell is periodic with period 20 * 8 along it, and the other two coordinates lie in a 6 by 6 cross-section.
All inputs are finite; a program needn't handle non-finite values.
Results may differ from a plain program's by a relative error of at most 0.0003.
Values sent between devices are 32-bit elements; how exact they have to be, the bound alone decides.
No kernel may reach another device: no remote copies, remote signals or barrier semaphores. Data moves between devices by JAX's collectives and lax.ppermute only.
A program may use at most 64 MiB of HBM per device.

v0:
```python
import jax
import jax.numpy as jnp
from jax import lax
from jax.sharding import PartitionSpec as P

C = 128
FF = 512
K = 64
NS = 100
A_DEV = 128
G = 32
DEG = 16
STEP = 100


highest = lax.Precision.HIGHEST
cutoff = 6.0
slab_width = 20.0
cross_area = 36.0
force_weight = 10.0
stress_weight = 100.0


def with_halo(cells, sides, width):
    for axis, dim in sides:
        count = lax.axis_size(axis)
        head = lax.slice_in_dim(cells, 0, width, axis=dim)
        tail = lax.slice_in_dim(cells, cells.shape[dim] - width, cells.shape[dim], axis=dim)
        cells = jnp.concatenate(
            [
                lax.ppermute(tail, axis, [(i, (i + 1) % count) for i in range(count)]),
                cells,
                lax.ppermute(head, axis, [((i + 1) % count, i) for i in range(count)]),
            ],
            axis=dim,
        )
    return cells


def split_weights(flat):
    offset = 0
    table = flat[offset : offset + NS * C].reshape(NS, C)
    offset = offset + NS * C
    radial_one = flat[offset : offset + K * C].reshape(K, C)
    offset = offset + K * C
    radial_two = flat[offset : offset + C * C].reshape(C, C)
    offset = offset + C * C
    message_weight = flat[offset : offset + C * C].reshape(C, C)
    offset = offset + C * C
    update_weight = flat[offset : offset + C * FF].reshape(C, FF)
    offset = offset + C * FF
    readout_weight = flat[offset : offset + FF]
    return (table, radial_one, radial_two, message_weight, update_weight, readout_weight)


def slab_energy(flat, vectors, ext_species, source, target, count):
    table, radial_one, radial_two, message_weight, update_weight, readout_weight = split_weights(
        flat
    )
    onehot = (ext_species[:, None] == jnp.arange(NS, dtype=jnp.int32)[None, :]).astype(jnp.float32)
    embedded = jnp.dot(onehot, table, precision=highest)
    dist = jnp.sqrt(jnp.sum(vectors * vectors, axis=0))
    centers = jnp.arange(K, dtype=jnp.float32) * (cutoff / (K - 1))
    spread = 0.5 * ((K - 1) / cutoff) ** 2
    basis = jnp.exp(-spread * (dist[:, None] - centers[None, :]) ** 2)
    ratio = jnp.minimum(dist / cutoff, 1.0)
    envelope = (1.0 - ratio * ratio) ** 2
    live_edge = (target < count).astype(jnp.float32)
    inner = jax.nn.silu(jnp.dot(basis, radial_one, precision=highest))
    filtered = jnp.dot(inner, radial_two, precision=highest) * (envelope * live_edge)[:, None]
    projected = jnp.dot(embedded, message_weight, precision=highest)
    messages = filtered * projected[source]
    summed = jax.ops.segment_sum(messages, target, num_segments=A_DEV)
    hidden = embedded[G : G + A_DEV] + summed * (1.0 / DEG)
    normed = hidden * lax.rsqrt(jnp.mean(hidden * hidden, axis=-1, keepdims=True) + 1e-05)
    activated = jax.nn.silu(jnp.dot(normed, update_weight, precision=highest))
    atom_energy = jnp.dot(activated, readout_weight, precision=highest)
    live_atom = (jnp.arange(A_DEV, dtype=jnp.int32) < count).astype(jnp.float32)
    return jnp.sum(atom_energy * live_atom)


def body(
    positions,
    species,
    counts,
    source,
    target,
    send_left,
    send_right,
    energy_ref,
    force_ref,
    stress_ref,
    params,
    moment_one,
    moment_two,
):
    shards = lax.axis_size("dp")
    gathered = lax.all_gather(params, "dp", axis=0, tiled=True)
    flat = gathered.reshape(shards, -1).T.reshape(-1)
    place = positions[0, 0]
    kinds = species[0, 0]
    count = counts[0, 0]
    src = source[0, 0]
    dst = target[0, 0]
    left_list = send_left[0, 0]
    right_list = send_right[0, 0]
    ghosts = left_list.shape[0]
    slots = place.shape[1]
    rank = lax.axis_index("graph")
    slabs = lax.axis_size("graph")
    box = slabs * slab_width
    volume = box * cross_area
    packed = jnp.concatenate([place, kinds[None, :].astype(jnp.float32)], axis=0)
    outgoing = jnp.concatenate([packed[:, left_list], packed[:, right_list]], axis=1)
    extended = with_halo(outgoing, (("graph", 1),), ghosts)
    row_mask = (jnp.arange(4) == 0).astype(jnp.float32)[:, None]
    from_left = extended[:, :ghosts] + row_mask * jnp.where(rank == 0, -box, 0.0)
    from_right = extended[:, 3 * ghosts :] + row_mask * jnp.where(rank == slabs - 1, box, 0.0)
    ext_pos = jnp.concatenate([from_left[:3], place, from_right[:3]], axis=1)
    ext_species = jnp.concatenate([from_left[3], kinds.astype(jnp.float32), from_right[3]]).astype(
        jnp.int32
    )
    vectors = ext_pos[:, src] - ext_pos[:, dst + ghosts]

    def slope_fn(weights):
        return jax.value_and_grad(slab_energy, argnums=1)(
            weights, vectors, ext_species, src, dst, count
        )

    (energy_part, slopes), pull = jax.vjp(slope_fn, flat)
    stress_part = jnp.einsum("ie,je->ij", slopes, vectors, precision=highest)
    energy, stress_total = lax.psum((energy_part, stress_part), "graph")
    stress = stress_total / volume
    contrib = (
        jnp.zeros((3, slots + 2 * ghosts), jnp.float32)
        .at[:, src]
        .add(slopes)
        .at[:, dst + ghosts]
        .add(-slopes)
    )
    back = jnp.concatenate([contrib[:, :ghosts], contrib[:, ghosts + slots :]], axis=1)
    returned = with_halo(back, (("graph", 1),), ghosts)
    grad_pos = contrib[:, ghosts : ghosts + slots].at[:, left_list].add(returned[:, :ghosts])
    grad_pos = grad_pos.at[:, right_list].add(returned[:, 3 * ghosts :])
    forces = -grad_pos
    scale = 2.0 / (slabs * slots)
    live = jnp.arange(slots, dtype=jnp.int32) < count
    force_cot = jnp.where(live[None, :], force_weight * scale * (forces - force_ref[0, 0]), 0.0)
    sent_cot = jnp.concatenate([force_cot[:, left_list], force_cot[:, right_list]], axis=1)
    beside_all = with_halo(sent_cot, (("graph", 1),), ghosts)
    ext_cot = jnp.concatenate(
        [beside_all[:, :ghosts], force_cot, beside_all[:, 3 * ghosts :]], axis=1
    )
    stress_cot = 2.0 * stress_weight * (stress - stress_ref[0])
    slope_cot = -(ext_cot[:, src] - ext_cot[:, dst + ghosts])
    slope_cot = slope_cot + jnp.dot(stress_cot, vectors, precision=highest) / volume
    energy_cot = (energy - energy_ref[0]) * scale
    grad_model = pull((energy_cot, slope_cot))[0]
    grad_flat = grad_model.reshape(-1, shards).T.reshape(-1)
    within = lax.psum(grad_flat, "graph")
    grad = lax.psum_scatter(within, "dp", scatter_dimension=0, tiled=True)
    new_moment_one = 0.9 * moment_one + 0.1 * grad
    new_moment_two = 0.999 * moment_two + 0.001 * grad * grad
    corrected_one = new_moment_one / (1.0 - 0.9**STEP)
    corrected_two = new_moment_two / (1.0 - 0.999**STEP)
    new_params = params - 0.001 * (
        corrected_one / (jnp.sqrt(corrected_two) + 1e-08) + 0.01 * params
    )
    return (
        new_params,
        new_moment_one,
        new_moment_two,
        forces[None, None],
        energy[None],
        stress[None],
    )


def solution(mesh):
    in_specs = (
        P("dp", "graph", None, None),
        P("dp", "graph", None),
        P("dp", "graph"),
        P("dp", "graph", None),
        P("dp", "graph", None),
        P("dp", "graph", None),
        P("dp", "graph", None),
        P("dp"),
        P("dp", "graph", None, None),
        P("dp", None, None),
        P("dp"),
        P("dp"),
        P("dp"),
    )
    out_specs = (
        P("dp"),
        P("dp"),
        P("dp"),
        P("dp", "graph", None, None),
        P("dp"),
        P("dp", None, None),
    )
    return jax.shard_map(body, mesh=mesh, in_specs=in_specs, out_specs=out_specs, check_vma=False)
```

profile of v0, /device:TPU:1, one launch (start us, length us, event | category | flops | bytes accessed | tf_op | source)
XLA Modules:
  0.0 919.7 jit_solution(11401112860215823149)
XLA Ops:
  9.9 10.5 %collective-permute-start.1 = (f32[4,32]{0,1:T(8,128)S(1)}, f32[4,32]{0,1:T(8,128)S(1)}, u32[]{:S(2)}, u32[]{:S(2)}) collective-permute-start(f32[4,32]{0,1:T(8,128)S(1)} %bitcast.162), channel_id=1, source_target_pairs={{1,0},{2,1},{3,2},{4,3},{5,4},{6,5},{7,6},{0,7},{9,8},{10,9},{11,1... | collective-permute-start | bytes 1544 | tf_op jit(solution)/shard_map/ppermute | solution.py:33
  24.1 85.7 %all-gather = f32[64,1,1920]{2,1,0:T(1,128)S(1)} all-gather(f32[1,1,1920]{2,1,0:T(1,128)S(1)} %reshape.474), channel_id=1, replica_groups=mesh['dp'=64,'graph'=8] {'dp'}, dimensions={0}, use_global_device_ids=true | all-gather | bytes 499200 | tf_op jit(solution)/shard_map/all_gather | solution.py:98
  119.9 5.5 gather_fusion.4
  125.7 5.5 gather_fusion.2
  131.2 5.5 gather_fusion.3
  140.1 2.3 multiply_multiply_fusion
  142.4 2.9 copy.164
  145.3 12.2 %scatter_custom_fusion = f32[128,128]{1,0:T(8,128)S(1)} fusion(s32[2048]{0:T(1024)S(1)} %bitcast.155, f32[2048,128]{1,0:T(8,128)} %copy.164, f32[]{:T(128)} %constant.35.clone.1), kind=kCustom, calls=%fused_computation.169 | custom fusion | flops 262144 | bytes 66048 | tf_op jit(solution)/shard_map/jvp(jvp())/scatter-add | solution.py:73
  160.9 7.5 gather_fusion.5
  172.0 3.2 multiply_add_fusion.3
  180.9 11.8 %scatter_custom_fusion.1 = f32[3,192]{0,1:T(8,128)S(1)} fusion(s32[2048]{0:T(1024)} %bitcast.157, f32[2048,3]{1,0:T(8,128)} %copy.168, f32[]{:T(128)} %constant.35.clone.1), kind=kCustom, calls=%fused_computation.151 | custom fusion | flops 6144 | bytes 2816 | tf_op jit(solution)/shard_map/scatter-add | solution.py:137
  192.8 11.9 %scatter_fusion = f32[3,192]{0,1:T(8,128)S(1)} fusion(f32[3,192]{0,1:T(8,128)S(1)} %scatter_custom_fusion.1, s32[2048]{0:T(1024)} %bitcast.152, f32[2048,3]{1,0:T(8,128)} %copy.169), kind=kCustom, calls=%fused_computation.13 | custom fusion | flops 6144 | bytes 81920 | tf_op jit(solution)/shard_map/scatter-add | solution.py:139
  205.3 9.2 collective-permute-start.3
  216.4 2.0 fusion.32
  219.0 6.0 collective-permute-done.2
  225.1 2.3 scatter_custom_fusion.3
  227.4 2.3 scatter_custom_fusion.4
  233.8 2.0 collective-permute-start.4
  235.8 9.4 %collective-permute-start.5 = (f32[3,32]{0,1:T(8,128)}, f32[3,32]{0,1:T(8,128)}, u32[]{:S(2)}, u32[]{:S(2)}) collective-permute-start(f32[3,32]{0,1:T(8,128)} %bitcast.163), channel_id=1, source_target_pairs={{1,0},{2,1},{3,2},{4,3},{5,4},{6,5},{7,6},{0,7},{9,8},{10,9},{11,1... | collective-permute-start | bytes 1160 | tf_op jit(solution)/shard_map/ppermute | solution.py:33
  245.9 21.9 %all-reduce.8 = (f32[3,3]{1,0:T(4,128)}, f32[]{:T(128)}) all-reduce(f32[3,3]{1,0:T(4,128)S(1)} %copy-done.49, f32[]{:T(128)} %fusion.32), channel_id=1, replica_groups=mesh['dp'=64,'graph'=8] {'graph'}, use_global_device_ids=true, to_apply=%region_10.11 | all-reduce | flops 10 | bytes 80 | tf_op jit(solution)/shard_map/psum | solution.py:132
  270.0 8.3 gather_fusion.9
  278.3 7.6 gather_fusion.8
  291.3 2.9 fusion.40
  296.2 2.8 fusion.26
  299.0 3.0 fusion.157
  303.5 11.8 %scatter_custom_fusion.5 = f32[128,128]{1,0:T(8,128)S(1)} fusion(s32[2048]{0:T(1024)} %bitcast.153, f32[2048,128]{1,0:T(8,128)S(1)} %copy.175, f32[]{:T(128)} %constant.35.clone.1), kind=kCustom, calls=%fused_computation.167 | custom fusion | flops 262144 | bytes 66048 | tf_op jit(solution)/shard_map/transpose(jvp(transpose(jvp())))/scatter-add | solution.py:73
  324.7 5.5 gather_fusion.10
  331.6 3.8 multiply_add_fusion
  336.9 11.8 %scatter_custom_fusion.6 = f32[192,128]{1,0:T(8,128)S(1)} fusion(s32[2048]{0:T(1024)} %bitcast.158, f32[2048,128]{1,0:T(8,128)S(1)} %copy.177, f32[]{:T(128)} %constant.35.clone.1), kind=kCustom, calls=%fused_computation.147 | custom fusion | flops 262144 | bytes 98816 | tf_op jit(solution)/shard_map/transpose(jvp(jvp()))/scatter-add | solution.py:72
  353.0 1.9 fusion.8
  362.9 522.4 %all-reduce.11.cloned.1.call-done = f32[122880]{0:T(1024)} async-done(((f32[122880]{0:T(1024)}), f32[122880]{0:T(1024)}) %all-reduce.11.cloned.1.call-update) | async-done | bytes 491536
  886.1 25.9 %psum.24 = f32[1920]{0:T(1024)S(1)} all-reduce(f32[1920]{0:T(1024)S(1)} %dynamic-slice.1), channel_id=1, replica_groups=mesh['dp'=64,'graph'=8] {'graph'}, use_global_device_ids=true, to_apply=%region_19.20 | all-reduce | flops 1920 | bytes 15360 | tf_op jit(solution)/shard_map/psum | solution.py:160
  (301 shorter events, 74.4 us)
Async XLA Ops:
  7.2 878.1 %all-reduce.11.cloned.1.call-start = ((), (), s32[]{:S(2)}) async-start(), calls=%async_computation | async-start | bytes 983040
  9.9 10.5 %copy-start.79 = (s32[1,1,32]{2,1,0:T(1,128)S(1)}, s32[1,1,32]{2,1,0:T(1,128)}, u32[]{:S(2)}) copy-start(s32[1,1,32]{2,1,0:T(1,128)} %param.19) | copy-start | bytes 388
  9.9 108.7 %collective-permute-start.1 = (f32[4,32]{0,1:T(8,128)S(1)}, f32[4,32]{0,1:T(8,128)S(1)}, u32[]{:S(2)}, u32[]{:S(2)}) collective-permute-start(f32[4,32]{0,1:T(8,128)S(1)} %bitcast.162), channel_id=1, source_target_pairs={{1,0},{2,1},{3,2},{4,3},{5,4},{6,5},{7,6},{0,7},{9,8},{10,9},{11,1... | collective-permute-start | bytes 1544 | tf_op jit(solution)/shard_map/ppermute | solution.py:33
  20.9 3.1 copy-start.36
  21.5 97.3 %collective-permute-start = (f32[4,32]{0,1:T(8,128)S(1)}, f32[4,32]{0,1:T(8,128)S(1)}, u32[]{:S(2)}, u32[]{:S(2)}) collective-permute-start(f32[4,32]{0,1:T(8,128)S(1)} %bitcast.161), channel_id=1, source_target_pairs={{0,1},{1,2},{2,3},{3,4},{4,5},{5,6},{6,7},{7,0},{8,9},{9,10},{10,1... | collective-permute-start | bytes 1544 | tf_op jit(solution)/shard_map/ppermute | solution.py:31
  114.1 23.3 %copy-start.39 = (pred[2048]{0:T(1024)(128)(4,1)}, pred[2048]{0:T(1024)(128)(4,1)S(1)}, u32[]{:S(2)}) copy-start(pred[2048]{0:T(1024)(128)(4,1)S(1)} %get-tuple-element.45) | copy-start | bytes 6148
  116.1 15.1 %copy-start.26 = (s32[2048]{0:T(1024)}, s32[2048]{0:T(1024)S(1)}, u32[]{:S(2)}) copy-start(s32[2048]{0:T(1024)S(1)} %broadcast_clamp_fusion.1) | copy-start | bytes 24580
  117.0 20.5 %copy-start.22 = (f32[64,128]{1,0:T(8,128)}, f32[64,128]{1,0:T(8,128)S(1)}, u32[]{:S(2)}) copy-start(f32[64,128]{1,0:T(8,128)S(1)} %reshape.310) | copy-start | bytes 98308
  117.5 22.5 %copy-start.13 = (f32[128,128]{1,0:T(8,128)}, f32[128,128]{1,0:T(8,128)S(1)}, u32[]{:S(2)}) copy-start(f32[128,128]{1,0:T(8,128)S(1)} %reshape.311) | copy-start | bytes 196612
  137.4 40.7 %copy-start.10 = (f32[2048,3]{0,1:T(4,128)}, f32[2048,3]{0,1:T(4,128)S(1)}, u32[]{:S(2)}) copy-start(f32[2048,3]{0,1:T(4,128)S(1)} %get-tuple-element.62) | copy-start | bytes 73732
  142.4 156.5 %copy-start = (f32[2048,128]{0,1:T(8,128)}, f32[2048,128]{0,1:T(8,128)S(1)}, u32[]{:S(2)}) copy-start(f32[2048,128]{0,1:T(8,128)S(1)} %get-tuple-element.81) | copy-start | bytes 3145732
  145.3 12.3 %copy-start.3 = (f32[128,512]{1,0:T(8,128)S(1)}, f32[128,512]{1,0:T(8,128)}, u32[]{:S(2)}) copy-start(f32[128,512]{1,0:T(8,128)} %reshape.314) | copy-start | bytes 786436
  170.9 4.3 copy-start.1
  172.0 3.3 copy-start.23
  172.0 3.3 copy-start.31
  175.2 2.9 copy-start.82
  205.3 11.1 %copy-start.62 = (f32[512,1]{0,1:T(1,128)S(1)}, f32[512,1]{0,1:T(1,128)}, u32[]{:S(2)}) copy-start(f32[512,1]{0,1:T(1,128)} %reshape.479) | copy-start | bytes 6148
  205.3 22.1 %collective-permute-start.3 = (f32[3,32]{0,1:T(8,128)}, f32[3,32]{0,1:T(8,128)}, u32[]{:S(2)}, u32[]{:S(2)}) collective-permute-start(f32[3,32]{0,1:T(8,128)} %get-tuple-element.67), channel_id=1, source_target_pairs={{1,0},{2,1},{3,2},{4,3},{5,4},{6,5},{7,6},{0,7},{9,8},{10,9},{11,1... | collective-permute-start | bytes 1160 | tf_op jit(solution)/shard_map/ppermute | solution.py:33
  214.5 10.6 %collective-permute-start.2 = (f32[3,32]{0,1:T(8,128)S(1)}, f32[3,32]{0,1:T(8,128)}, u32[]{:S(2)}, u32[]{:S(2)}) collective-permute-start(f32[3,32]{0,1:T(8,128)S(1)} %get-tuple-element.68), channel_id=1, source_target_pairs={{0,1},{1,2},{2,3},{3,4},{4,5},{5,6},{6,7},{7,0},{8,9},{9,10},{10,1... | collective-permute-start | bytes 1160 | tf_op jit(solution)/shard_map/ppermute | solution.py:31
  231.2 37.3 %copy-start.12 = (f32[3,128]{0,1:T(8,128)}, f32[3,128]{0,1:T(8,128)S(1)}, u32[]{:S(2)}) copy-start(f32[3,128]{0,1:T(8,128)S(1)} %get-tuple-element.70) | copy-start | bytes 4612
  233.8 12.1 %copy-start.49 = (f32[3,3]{1,0:T(4,128)S(1)}, f32[3,3]{1,0:T(4,128)}, u32[]{:S(2)}) copy-start(f32[3,3]{1,0:T(4,128)} %fusion.99) | copy-start | bytes 112
  233.8 34.7 %collective-permute-start.4 = (f32[3,32]{0,1:T(8,128)}, f32[3,32]{0,1:T(8,128)S(1)}, u32[]{:S(2)}, u32[]{:S(2)}) collective-permute-start(f32[3,32]{0,1:T(8,128)} %bitcast.164), channel_id=1, source_target_pairs={{0,1},{1,2},{2,3},{3,4},{4,5},{5,6},{6,7},{7,0},{8,9},{9,10},{10,1... | collective-permute-start | bytes 1160 | tf_op jit(solution)/shard_map/ppermute | solution.py:31
  235.8 33.3 %collective-permute-start.5 = (f32[3,32]{0,1:T(8,128)}, f32[3,32]{0,1:T(8,128)}, u32[]{:S(2)}, u32[]{:S(2)}) collective-permute-start(f32[3,32]{0,1:T(8,128)} %bitcast.163), channel_id=1, source_target_pairs={{1,0},{2,1},{3,2},{4,3},{5,4},{6,5},{7,6},{0,7},{9,8},{10,9},{11,1... | collective-permute-start | bytes 1160 | tf_op jit(solution)/shard_map/ppermute | solution.py:33
  290.6 3.6 copy-start.24
  291.3 4.8 copy-start.2
  291.3 4.8 copy-start.7
  296.2 2.8 copy-start.83
  353.0 3.0 copy-start.85
  353.0 3.0 copy-start.86
  358.9 553.1 %copy-start.48 = (f32[1920]{0:T(1024)S(1)}, f32[1920]{0:T(1024)}, u32[]{:S(2)}) copy-start(f32[1920]{0:T(1024)} %param.25) | copy-start | bytes 23044
  886.1 25.9 %copy-start.37 = (f32[1920]{0:T(1024)S(1)}, f32[1920]{0:T(1024)}, u32[]{:S(2)}) copy-start(f32[1920]{0:T(1024)} %param.23) | copy-start | bytes 23044
  886.1 25.9 %copy-start.47 = (f32[1920]{0:T(1024)S(1)}, f32[1920]{0:T(1024)}, u32[]{:S(2)}) copy-start(f32[1920]{0:T(1024)} %param.24) | copy-start | bytes 23044
  (65 other events, 73.8 us)
Sparse Core Ops, SparseCore 0:
  359.9 525.3 all-reduce.10
where the time goes:
time: 933 us; the launch traced here: 920 us
  waiting for transfers between devices  528 us (57%)
  blocking collectives  134 us (14%)
  local copies, waits for them, and re-layouts  92.1 us (10%)
  other arithmetic  76.9 us (8%)
  matrix products  35.8 us (4%)
  starting transfers between devices  35 us (4%)
  between operations  18 us (2%)
    unnamed x2, waiting for transfers between devices  522 us
    all_gather x1, blocking collectives, body(): gathered = lax.all_gather(params, 'dp', axis=0, tiled=True)  85.7 us
    ppermute x3, starting transfers between devices, with_halo(): lax.ppermute(head, axis, [((i + 1) % count, i) for i in range(count)])  29 us
    psum x1, blocking collectives, body(): within = lax.psum(grad_flat, 'graph')  25.9 us
    scatter-add x2, other arithmetic, slab_energy(): summed = jax.ops.segment_sum(messages, target, num_segments=A_DEV)  24 us
    scatter-add x2, other arithmetic, body(): contrib = jnp.zeros((3, slots + 2 * ghosts), jnp.float32).at[:, src].add(...  23.8 us
    psum x1, blocking collectives, body(): energy, stress_total = lax.psum((energy_part, stress_part), 'graph')  21.9 us
    unnamed x189, local copies, waits for them, and re-layouts  20.8 us
  transfers between devices with their start and end apart: 7, of which 2 were waited for; matrix products, arithmetic and copies ran while one was open for 2% of the time, Pallas kernels for 0%

commit v1 on v0

v1 whole, which is shorter than its diff:
```python
import functools
import jax
import jax.numpy as jnp
from jax import lax
from jax.experimental import pallas as pl
from jax.experimental.pallas import tpu as pltpu
from jax.sharding import PartitionSpec as P

C = 128
FF = 512
K = 64
NS = 100
A = 128
G = 32
DEG = 16
STEP = 100
E = A * DEG
N = A + 2 * G
EC = 512
CHUNKS = E // EC
BLOCKS = 16

highest = lax.Precision.HIGHEST
cutoff = 6.0
slab_width = 20.0
cross_area = 36.0
force_weight = 10.0
stress_weight = 100.0
spread = 0.5 * ((K - 1) / cutoff) ** 2

f32 = jnp.float32
bf16 = jnp.bfloat16
NN = ((1,), (0,))
NT = ((1,), (1,))


def split(x):
    high = x.astype(bf16)
    return high, (x - high.astype(f32)).astype(bf16)


def mm(a, b, dims):
    return lax.dot_general(a, b, (dims, ((), ())), preferred_element_type=f32)


def dot3(a, b, dims):
    return mm(a[0], b[0], dims) + mm(a[0], b[1], dims) + mm(a[1], b[0], dims)


def dot2(a, onehot, dims):
    return mm(a[0], onehot, dims) + mm(a[1], onehot, dims)


def exact(x):
    one = x.astype(bf16).astype(f32)
    two = (x - one).astype(bf16).astype(f32)
    return jnp.concatenate([one, two, x - one - two], axis=0).astype(bf16)


def whole(x):
    return x[0:8] + x[8:16] + x[16:24]


def full_dot(a, b, dims):
    return lax.dot_general(a, b, (dims, ((), ())), precision=highest, preferred_element_type=f32)


def iota(shape, dim):
    return lax.broadcasted_iota(jnp.int32, shape, dim)


def select_lists(lists):
    return (iota((A, 128), 0) == lists).astype(f32)


def send_kernel(own, lists, out):
    out[...] = full_dot(own[...], select_lists(lists[...]), NN)


def weight(wg, first):
    return jnp.concatenate([wg[:, first, :], wg[:, first + 1, :]], axis=0)


def update_weight_t(wg):
    return jnp.concatenate([wg[:, 7 + h, :] for h in range(8)], axis=0)


def readout_column(wg):
    block = wg[:, 15, :]
    return jnp.concatenate([block[:, h : h + 1] for h in range(8)], axis=0)


def radial_one_t(wg):
    block = wg[:, 2, :]
    return jnp.concatenate([block[:, :K], block[:, K:]], axis=0)


def silu_parts(a):
    sig = 1.0 / (1.0 + jnp.exp(-a))
    first = sig * (1.0 + a * (1.0 - sig))
    return sig, first


def silu_second(a, sig):
    return sig * (1.0 - sig) * (2.0 + a * (1.0 - 2.0 * sig))


def forward_kernel(
    scalars, wg, own, ghost, src, dst, lists,
    message, contrib_out, a_out, da_out, filt_out, dfilt_out, q_out, h_out, dn_out, dh_out,
    z_out, emb_out, vec_out, rows_out, src_hot, dst_hot, total, force_total,
):
    count = scalars[0]
    rank = scalars[1]
    slabs = scalars[2]
    box = slab_width * slabs.astype(f32)
    table_t = weight(wg, 0)
    one_t = split(radial_one_t(wg))
    two_t = split(weight(wg, 3))
    message_t = split(weight(wg, 5))
    update_f = update_weight_t(wg)
    update_t = split(update_f)
    update = split(update_f.T)
    readout = readout_column(wg)

    own_rows = own[...]
    ghost_rows = ghost[...]
    lane = iota((8, 128), 1)
    row = iota((8, 128), 0)
    shift = jnp.where(lane < G, jnp.where(rank == 0, -box, 0.0), 0.0)
    shift = shift + jnp.where((lane >= G) & (lane < 2 * G), jnp.where(rank == slabs - 1, box, 0.0), 0.0)
    ghost_pos = ghost_rows + jnp.where(row == 0, shift, 0.0)
    ext = jnp.concatenate([own_rows, ghost_pos], axis=1)
    pieces = exact(jnp.where(iota((8, 256), 0) < 3, ext, 0.0))
    kinds = ext[3:4, :].astype(jnp.int32)
    kind_hot = (iota((128, 256), 0) == kinds).astype(f32)
    table_hi, table_rest = split(table_t)
    table_lo = (table_t - table_hi.astype(f32) - table_rest.astype(f32)).astype(bf16)
    kind_bf = kind_hot.astype(bf16)
    emb = mm(table_hi, kind_bf, NN) + mm(table_rest, kind_bf, NN) + mm(table_lo, kind_bf, NN)
    emb_out[...] = emb
    projected = split(dot3(message_t, split(emb), NN))
    projected = (projected[0][:, :N], projected[1][:, :N])
    total[...] = jnp.zeros_like(total)
    centers = iota((K, EC), 0).astype(f32) * (cutoff / (K - 1))

    def first_pass(i, carry):
        at = pl.ds(pl.multiple_of(i * EC, EC), EC)
        s = src[:, at]
        t = dst[:, at]
        s = jnp.where(s < G, s + A, jnp.where(s < G + A, s - G, s))
        hot_s = (iota((N, EC), 0) == s).astype(f32).astype(bf16)
        hot_t = (iota((A, EC), 0) == t).astype(f32).astype(bf16)
        src_hot[:, at] = hot_s
        dst_hot[:, at] = hot_t
        vec = whole(mm(pieces[:, :N], hot_s, NN) - mm(pieces[:, :A], hot_t, NN))
        vec_out[:, at] = vec
        square = jnp.sum(vec * vec, axis=0, keepdims=True)
        dist = jnp.sqrt(square)
        inverse = jnp.where(square > 0.0, 1.0 / jnp.where(square > 0.0, dist, 1.0), 0.0)
        ratio = jnp.minimum(dist / cutoff, 1.0)
        live = (t < count).astype(f32)
        inside = 1.0 - ratio * ratio
        gate = inside * inside * live
        dgate = inside * ratio * (-4.0 / cutoff) * live
        rows_out[0:1, at] = dist
        rows_out[1:2, at] = inverse
        rows_out[2:3, at] = gate
        rows_out[3:4, at] = dgate
        delta = dist - centers
        basis = jnp.exp(-spread * delta * delta)
        dbasis = (-2.0 * spread) * delta * basis
        a = dot3(one_t, split(basis), NN)
        da = dot3(one_t, split(dbasis), NN)
        a_out[:, at] = a
        da_out[:, at] = da
        sig, slope = silu_parts(a)
        f = dot3(two_t, split(a * sig), NN)
        df = dot3(two_t, split(slope * da), NN)
        filt = f * gate
        dfilt = df * gate + f * dgate
        q = dot2(projected, hot_s, NN)
        filt_out[:, at] = filt
        dfilt_out[:, at] = dfilt
        q_out[:, at] = q
        total[...] += dot2(split(filt * q), hot_t, NT)
        return carry

    lax.fori_loop(0, CHUNKS, first_pass, 0)

    hidden = emb[:, :A] + total[...] * (1.0 / DEG)
    h_out[...] = hidden
    rms = lax.rsqrt(jnp.mean(hidden * hidden, axis=0, keepdims=True) + 1e-05)
    z = dot3(update_t, split(hidden * rms), NN)
    z_out[...] = z
    sig, slope = silu_parts(z)
    live_atom = (iota((1, A), 1) < count).astype(f32)
    weighted = readout * live_atom
    energy = jnp.sum(jnp.sum(weighted * (z * sig), axis=0, keepdims=True), axis=1, keepdims=True)
    dn = dot3(update, split(weighted * slope), NN)
    dn_out[...] = dn
    cube = rms * rms * rms * (1.0 / C)
    dh = rms * dn - hidden * (cube * jnp.sum(dn * hidden, axis=0, keepdims=True))
    dh_out[...] = dh
    dh_pieces = split(dh * (1.0 / DEG))
    force_total[...] = jnp.zeros_like(force_total)

    def second_pass(i, stress):
        at = pl.ds(pl.multiple_of(i * EC, EC), EC)
        hot_s = src_hot[:, at]
        hot_t = dst_hot[:, at]
        back = dot2(dh_pieces, hot_t, NN)
        along = jnp.sum(back * (dfilt_out[:, at] * q_out[:, at]), axis=0, keepdims=True)
        vec = vec_out[:, at]
        slopes = vec * (along * rows_out[1:2, at])
        three = exact(slopes)
        force_total[:, :N] += mm(three, hot_s, NT)
        force_total[:, :A] -= mm(three, hot_t, NT)
        return stress + full_dot(slopes, vec, NT)

    stress = lax.fori_loop(0, CHUNKS, second_pass, jnp.zeros((8, 8), f32))
    contrib = whole(force_total[...])
    contrib_out[...] = contrib
    lists_hot = select_lists(lists[...])
    outgoing = full_dot(contrib[:, :A], lists_hot, NN) + pltpu.roll(contrib[:, A:], 64, 1)
    to_right = (lane < G) | (lane >= 96)
    sums = jnp.zeros((8, 128), f32)
    for i in range(3):
        for j in range(3):
            sums = sums + jnp.where(lane == 3 * i + j, stress[i : i + 1, j : j + 1], 0.0)
    sums = sums + jnp.where(lane == 9, energy, 0.0)
    right = lax.rem(rank + 1, slabs)
    left = lax.rem(rank + slabs - 1, slabs)
    for d in range(8):
        keep = (to_right & (right == d)) | (jnp.logical_not(to_right) & (left == d))
        message[d] = jnp.where(row == 3, sums, jnp.where(keep, outgoing, 0.0))[:4]


def backward_kernel(
    scalars, refs, wg, own, ghost, lists, received, contrib_in, a_in, da_in, filt_in, dfilt_in,
    q_in, h_in, dn_in, dh_in, z_in, emb_in, vec_in, rows_in, src_hot, dst_hot,
    forces_out, sums_out, grad, step_row, total, source_total, one_total, two_total,
):
    count = scalars[0]
    slabs = scalars[2]
    volume = slab_width * cross_area * slabs.astype(f32)
    scale = 2.0 / (slabs.astype(f32) * A)
    two_f = weight(wg, 3)
    two = split(two_f.T)
    message_w = split(weight(wg, 5).T)
    update_f = update_weight_t(wg)
    update_t = split(update_f)
    update = split(update_f.T)
    readout = readout_column(wg)
    lists_hot = select_lists(lists[...])
    lane = iota((8, 128), 1)
    row = iota((8, 128), 0)

    got = jnp.sum(received[...], axis=0)
    got = jnp.concatenate([got, jnp.zeros_like(got)], axis=0)
    moved = jnp.where(row < 3, got, 0.0)
    energy = got[3:4, 9:10]
    inner = jnp.where(lane < 2 * G, pltpu.roll(moved, 64, 1), 0.0)
    contrib = contrib_in[...]
    force_own = -(contrib[:, :A] + full_dot(inner, lists_hot, NT))
    force_ghost = -(contrib[:, A:] + jnp.where(lane < 2 * G, moved, 0.0))
    forces_out[...] = force_own
    sums_out[...] = got
    own_ref = jnp.concatenate([own[4:8], jnp.zeros((4, 128), f32)], axis=0)
    ghost_ref = jnp.concatenate([ghost[4:8], jnp.zeros((4, 128), f32)], axis=0)
    factor = force_weight * scale
    cot_own = jnp.where((lane < count) & (row < 3), factor * (force_own - own_ref), 0.0)
    cot_ghost = jnp.where((lane < 2 * G) & (row < 3), factor * (force_ghost - ghost_ref), 0.0)
    cot = exact(jnp.concatenate([cot_own, cot_ghost], axis=1))
    stress_cot = [
        [
            (2.0 * stress_weight / volume) * (got[3:4, 3 * i + j : 3 * i + j + 1] / volume - refs[1 + 3 * i + j])
            for j in range(3)
        ]
        for i in range(3)
    ]
    energy_cot = (energy - refs[0]) * scale
    total[...] = jnp.zeros_like(total)

    def first_pass(i, carry):
        at = pl.ds(pl.multiple_of(i * EC, EC), EC)
        hot_t = dst_hot[:, at]
        vec = vec_in[:, at]
        delta = whole(mm(cot[:, :A], hot_t, NN) - mm(cot[:, :N], src_hot[:, at], NN))
        along = jnp.sum(vec * delta, axis=0, keepdims=True)
        for r in range(3):
            inner_row = sum(stress_cot[r][j] * vec[j : j + 1] for j in range(3))
            along = along + vec[r : r + 1] * inner_row
        step = along * rows_in[1:2, at]
        step_row[:, at] = step
        total[...] += dot2(split(dfilt_in[:, at] * q_in[:, at] * step), hot_t, NT)
        return carry

    lax.fori_loop(0, CHUNKS, first_pass, 0)

    hidden = h_in[...]
    dn = dn_in[...]
    dh = dh_in[...]
    z = z_in[...]
    moved_h = total[...] * (1.0 / DEG)
    rms = lax.rsqrt(jnp.mean(hidden * hidden, axis=0, keepdims=True) + 1e-05)
    cube = rms * rms * rms
    cross = jnp.mean(hidden * moved_h, axis=0, keepdims=True)
    normed = hidden * rms
    moved_n = rms * moved_h - (cube * cross) * hidden
    moved_z = dot3(update_t, split(moved_n), NN)
    sig, slope = silu_parts(z)
    live_atom = (iota((1, A), 1) < count).astype(f32)
    weighted = readout * live_atom
    z_bar = weighted * (energy_cot * slope + silu_second(z, sig) * moved_z)
    z_bar = split(z_bar)
    moved_z_bar = split(weighted * slope)
    update_grad = dot3(z_bar, split(normed), NT) + dot3(moved_z_bar, split(moved_n), NT)
    readout_grad = jnp.sum(live_atom * (energy_cot * (z * sig) + slope * moved_z), axis=1, keepdims=True)
    n_bar = dot3(update, z_bar, NN)
    dn_h = jnp.sum(dn * hidden, axis=0, keepdims=True) * (1.0 / C)
    mix = (jnp.sum(n_bar * hidden, axis=0, keepdims=True) + jnp.sum(dn * moved_h, axis=0, keepdims=True)) * (1.0 / C)
    h_bar = (
        rms * n_bar
        + hidden * (3.0 * cube * rms * rms * cross * dn_h - cube * mix)
        - moved_h * (cube * dn_h)
        - dn * (cube * cross)
    )
    for h in range(8):
        grad[:, 7 + h, :] = update_grad[64 * h : 64 * h + 64]
    lane64 = iota((64, 128), 1)
    block = jnp.zeros((64, 128), f32)
    for h in range(8):
        block = block + jnp.where(lane64 == h, readout_grad[64 * h : 64 * h + 64], 0.0)
    grad[:, 15, :] = block

    h_pieces = split(h_bar * (1.0 / DEG))
    dh_pieces = split(dh * (1.0 / DEG))
    source_total[...] = jnp.zeros_like(source_total)
    one_total[...] = jnp.zeros_like(one_total)
    two_total[...] = jnp.zeros_like(two_total)
    centers = iota((K, EC), 0).astype(f32) * (cutoff / (K - 1))

    def second_pass(i, carry):
        at = pl.ds(pl.multiple_of(i * EC, EC), EC)
        hot_s = src_hot[:, at]
        hot_t = dst_hot[:, at]
        step = step_row[:, at]
        gate = rows_in[2:3, at]
        dgate = rows_in[3:4, at]
        m_bar = dot2(h_pieces, hot_t, NN)
        dm_bar = dot2(dh_pieces, hot_t, NN)
        q = q_in[:, at]
        source_total[...] += dot2(
            split(m_bar * filt_in[:, at] + dm_bar * (dfilt_in[:, at] * step)), hot_s, NT
        )
        dq = dm_bar * q
        f_bar = split(m_bar * q * gate + dq * (dgate * step))
        df_bar = split(dq * gate)
        s_bar = dot3(two, f_bar, NN)
        ds_bar = dot3(two, df_bar, NN)
        a = a_in[:, at]
        moved_a = da_in[:, at] * step
        sig, slope = silu_parts(a)
        two_total[...] += dot3(f_bar, split(a * sig), NT) + dot3(df_bar, split(slope * moved_a), NT)
        a_bar = split(s_bar * slope + ds_bar * (silu_second(a, sig) * moved_a))
        da_bar = split(ds_bar * slope)
        delta = rows_in[0:1, at] - centers
        basis = jnp.exp(-spread * delta * delta)
        moved_basis = (-2.0 * spread) * delta * basis * step
        one_total[...] += dot3(a_bar, split(basis), NT) + dot3(da_bar, split(moved_basis), NT)
        return carry

    lax.fori_loop(0, CHUNKS, second_pass, 0)

    one_grad = one_total[...]
    grad[:, 2, :] = jnp.concatenate([one_grad[:64], one_grad[64:]], axis=1)
    two_grad = two_total[...]
    grad[:, 3, :] = two_grad[:64]
    grad[:, 4, :] = two_grad[64:]
    p_bar = source_total[...]
    p_bar = jnp.concatenate([p_bar, jnp.zeros((C, 256 - N), f32)], axis=1)
    p_pieces = split(p_bar)
    emb = emb_in[...]
    message_grad = dot3(p_pieces, split(emb), NT)
    grad[:, 5, :] = message_grad[:64]
    grad[:, 6, :] = message_grad[64:]
    emb_bar = dot3(message_w, p_pieces, NN)
    emb_bar = jnp.concatenate([emb_bar[:, :A] + h_bar, emb_bar[:, A:]], axis=1)
    kinds = jnp.concatenate([own[3:4], ghost[3:4]], axis=1).astype(jnp.int32)
    kind_hot = (iota((128, 256), 0) == kinds).astype(f32).astype(bf16)
    table_grad = dot2(split(emb_bar), kind_hot, NT)
    grad[:, 0, :] = table_grad[:64]
    grad[:, 1, :] = table_grad[64:]


vmem = pl.BlockSpec(memory_space=pltpu.VMEM)
smem = pl.BlockSpec(memory_space=pltpu.SMEM)
params_vmem = pltpu.CompilerParams(vmem_limit_bytes=56 * 1024 * 1024)


def shape(*dims, dtype=jnp.float32):
    return jax.ShapeDtypeStruct(dims, dtype)


def send(own, lists):
    return pl.pallas_call(
        send_kernel, out_shape=shape(8, 128), in_specs=[vmem] * 2, out_specs=vmem, name="halo_send"
    )(own, lists)


def forward(scalars, wg, own, ghost, src, dst, lists):
    outs = [
        shape(8, 4, 128), shape(8, 256), shape(C, E), shape(C, E), shape(C, E), shape(C, E),
        shape(C, E), shape(C, A), shape(C, A), shape(C, A), shape(FF, A), shape(C, 256),
        shape(8, E), shape(8, E), shape(N, E, dtype=bf16), shape(A, E, dtype=bf16),
    ]
    return pl.pallas_call(
        forward_kernel,
        out_shape=outs,
        in_specs=[smem] + [vmem] * 6,
        out_specs=[vmem] * len(outs),
        scratch_shapes=[pltpu.VMEM((C, A), f32), pltpu.VMEM((24, 256), f32)],
        compiler_params=params_vmem,
        name="energy_slopes",
    )(scalars, wg, own, ghost, src, dst, lists)


def backward(scalars, refs, wg, own, ghost, lists, received, kept):
    outs = [shape(8, 128), shape(8, 128), shape(64, BLOCKS, 128)]
    return pl.pallas_call(
        backward_kernel,
        out_shape=outs,
        in_specs=[smem] * 2 + [vmem] * (5 + len(kept)),
        out_specs=[vmem] * 3,
        scratch_shapes=[
            pltpu.VMEM((1, E), f32),
            pltpu.VMEM((C, A), f32),
            pltpu.VMEM((C, N), f32),
            pltpu.VMEM((C, K), f32),
            pltpu.VMEM((C, C), f32),
        ],
        compiler_params=params_vmem,
        name="weight_gradients",
    )(scalars, refs, wg, own, ghost, lists, received, *kept)


def to_blocks(x):
    two = x[:840].reshape(420, 2).T
    table = jnp.pad(two[:, :100], ((0, 0), (0, 28)))
    one = two[:, 100:164].reshape(1, 128)
    rest = jnp.pad(x[1864:], (0, 72)).reshape(1, 128)
    return jnp.concatenate(
        [table, one, two[:, 164:292], two[:, 292:420], x[840:1864].reshape(128, 8).T, rest], axis=0
    )


def from_blocks(y):
    two = jnp.concatenate([y[0:2, :100], y[2].reshape(2, 64), y[3:5], y[5:7]], axis=1)
    return jnp.concatenate([two.T.reshape(-1), y[7:15].T.reshape(-1), y[15, :56]])


def pack_own(positions, species, force_ref):
    return jnp.concatenate(
        [positions, species[None].astype(f32), force_ref, jnp.zeros((1, A), f32)], axis=0
    )


def pack_lists(send_left, send_right):
    return jnp.concatenate([send_right, send_left, jnp.full((64,), -1, jnp.int32)])[None]


def adam(params, moment_one, moment_two, grad):
    new_moment_one = 0.9 * moment_one + 0.1 * grad
    new_moment_two = 0.999 * moment_two + 0.001 * grad * grad
    corrected_one = new_moment_one / (1.0 - 0.9**STEP)
    corrected_two = new_moment_two / (1.0 - 0.999**STEP)
    new_params = params - 0.001 * (
        corrected_one / (jnp.sqrt(corrected_two) + 1e-08) + 0.01 * params
    )
    return new_params, new_moment_one, new_moment_two


def body(
    positions,
    species,
    counts,
    source,
    target,
    send_left,
    send_right,
    energy_ref,
    force_ref,
    stress_ref,
    params,
    moment_one,
    moment_two,
):
    shards = lax.axis_size("dp")
    slabs = lax.axis_size("graph")
    rank = lax.axis_index("graph")
    own = pack_own(positions[0, 0], species[0, 0], force_ref[0, 0])
    lists = pack_lists(send_left[0, 0], send_right[0, 0])
    outgoing = send(own, lists)
    lane = jnp.arange(128)[None]
    from_left = lax.ppermute(outgoing, "graph", [(i, (i + 1) % slabs) for i in range(slabs)])
    from_right = lax.ppermute(outgoing, "graph", [((i + 1) % slabs, i) for i in range(slabs)])
    blocks = jnp.broadcast_to(to_blocks(params)[None], (shards, BLOCKS, 128))
    wg = lax.all_to_all(blocks, "dp", 0, 0, tiled=True)
    ghost = jnp.where(lane < G, from_left, from_right)
    scalars = jnp.stack([counts[0, 0], rank, jnp.int32(slabs)]).astype(jnp.int32)
    refs = jnp.concatenate([energy_ref, stress_ref[0].reshape(-1)])
    message, *kept = forward(scalars, wg, own, ghost, source[0], target[0], lists)
    received = lax.all_to_all(message, "graph", 0, 0, tiled=True)
    forces, sums, grad_blocks = backward(scalars, refs, wg, own, ghost, lists, received, kept)
    volume = slabs * slab_width * cross_area
    within = jnp.sum(lax.all_to_all(grad_blocks, "dp", 0, 0, tiled=True), axis=0)
    wide = jnp.broadcast_to(within[None], (slabs, BLOCKS, 128))
    grad = from_blocks(jnp.sum(lax.all_to_all(wide, "graph", 0, 0, tiled=True), axis=0))
    new_params, new_moment_one, new_moment_two = adam(params, moment_one, moment_two, grad)
    return (
        new_params,
        new_moment_one,
        new_moment_two,
        forces[:3][None, None],
        sums[3, 9][None],
        (sums[3, :9] / volume).reshape(1, 3, 3),
    )


def solution(mesh):
    in_specs = (
        P("dp", "graph", None, None),
        P("dp", "graph", None),
        P("dp", "graph"),
        P("dp", "graph", None),
        P("dp", "graph", None),
        P("dp", "graph", None),
        P("dp", "graph", None),
        P("dp"),
        P("dp", "graph", None, None),
        P("dp", None, None),
        P("dp"),
        P("dp"),
        P("dp"),
    )
    out_specs = (
        P("dp"),
        P("dp"),
        P("dp"),
        P("dp", "graph", None, None),
        P("dp"),
        P("dp", None, None),
    )
    return jax.shard_map(body, mesh=mesh, in_specs=in_specs, out_specs=out_specs, check_vma=False)
```

time: 933 us -> 127 us (0.14); the launches traced: 920 us -> 126 us
  waiting for transfers between devices: 528 us -> 37.6 us
  blocking collectives: 134 us -> 0 us
  local copies, waits for them, and re-layouts: 92.1 us -> 10.3 us
  other arithmetic: 76.9 us -> 4.62 us
  matrix products: 35.8 us -> 0 us
  Pallas kernels: 0 us -> 26.2 us
  between operations: 18 us -> 2.17 us
  starting transfers between devices: 35 us -> 44.8 us
    unnamed x2 -> x0, waiting for transfers between devices: 522 us -> none
    all_gather x1 -> x0, blocking collectives: 85.7 us -> none  [body(): gathered = lax.all_gather(params, 'dp', axis=0, tiled=True)]
    scatter-add x7 -> x0, other arithmetic: 64.2 us -> none  [the longest x2 24 us: slab_energy(): summed = jax.ops.segment_sum(messages, target, num_segments=A_DEV)]
    gather x18 -> x0, local copies, waits for them, and re-layouts: 56 us -> none  [the longest x4 19 us: body(): slope_cot = -(ext_cot[:, src] - ext_cot[:, dst + ghosts])]
    psum x2 -> x0, blocking collectives: 47.8 us -> none  [the longest x1 25.9 us: body(): within = lax.psum(grad_flat, 'graph')]
    dot_general x27 -> x0, matrix products: 35.8 us -> none  [the longest x6 15 us: slab_energy(): jnp.dot(inner, radial_two, precision=highest)]
    all_to_all x0 -> x4, starting transfers between devices: none -> 35.7 us  [the longest x1 15.5 us: body(): wg = lax.all_to_all(blocks, 'dp', 0, 0, tiled=True)]
    all_to_all x0 -> x4, waiting for transfers between devices: none -> 31.3 us  [the longest x1 14.5 us: body(): lax.all_to_all(grad_blocks, 'dp', 0, 0, tiled=True)]
  transfers between devices with their start and end apart: 7 -> 6, of which waited for: 2 -> 4; matrix products, arithmetic and copies ran while one was open for 2% -> 5% of each run, Pallas kernels for 0% -> 1%
where the time goes in v1:
time: 127 us; the launch traced here: 126 us
  starting transfers between devices  44.8 us (35%)
  waiting for transfers between devices  37.6 us (30%)
  Pallas kernels  26.2 us (21%)
  local copies, waits for them, and re-layouts  10.3 us (8%)
  other arithmetic  4.62 us (4%)
  between operations  2.17 us (2%)
    all_to_all x1, starting transfers between devices, body(): wg = lax.all_to_all(blocks, 'dp', 0, 0, tiled=True)  15.5 us
    all_to_all x1, waiting for transfers between devices, body(): lax.all_to_all(grad_blocks, 'dp', 0, 0, tiled=True)  14.5 us
    all_to_all x1, starting transfers between devices, body(): lax.all_to_all(grad_blocks, 'dp', 0, 0, tiled=True)  13.3 us
    pallas_call x1, Pallas kernels, backward(): pl.pallas_call(backward_kernel, out_shape=outs, in_specs=[smem] * 2 + [vm...  12.7 us
    pallas_call x1, Pallas kernels, forward(): pl.pallas_call(forward_kernel, out_shape=outs, in_specs=[smem] + [vmem] *...  12.1 us
    all_to_all x1, waiting for transfers between devices, body(): lax.all_to_all(wide, 'graph', 0, 0, tiled=True)  8.46 us
    all_to_all x1, waiting for transfers between devices, body(): received = lax.all_to_all(message, 'graph', 0, 0, tiled=True)  8.31 us
    ppermute x1, starting transfers between devices, body(): lax.ppermute(outgoing, 'graph', [((i + 1) % slabs, i) for i in range(slab...  6.94 us
  transfers between devices with their start and end apart: 6, of which 4 were waited for; matrix products, arithmetic and copies ran while one was open for 5% of the time, Pallas kernels for 1%

profile of v1, /device:TPU:1, one launch (start us, length us, event | category | flops | bytes accessed | tf_op | source)
XLA Modules:
  0.0 125.8 jit_solution(9015072633200497157)
XLA Ops:
  0.6 0.8 slice.71
  1.4 0.8 slice.70
  2.3 0.6 slice-done
  3.3 0.6 copy-done.11
  4.2 0.8 broadcast_in_dim.33
  5.0 15.5 %all-to-all-start = ((f32[64,16,128]{2,1,0:T(8,128)}), f32[64,16,128]{2,1,0:T(8,128)S(1)}, u32[]{:S(2)}, u32[]{:S(2)}) async-start(f32[64,16,128]{2,1,0:T(8,128)} %broadcast_in_dim.33), calls=%async_computation | async-start | bytes 1048576 | tf_op jit(solution)/shard_map/all_to_all | solution.py:509
  20.7 0.6 add_bitcast_fusion.lists
  21.4 0.7 maximum_maximum_fusion.own
  22.0 1.4 %halo_send.1 = f32[8,128]{1,0:T(8,128)} custom-call(f32[8,128]{1,0:T(8,128)} %maximum_maximum_fusion.own, s32[1,128]{1,0:T(1,128)} %add_bitcast_fusion.lists), custom_call_target="tpu_custom_call" | custom-call | tf_op jit(solution)/shard_map/halo_send/pallas_call | solution.py:407
  23.5 6.9 %collective-permute-start.1 = (f32[8,128]{1,0:T(8,128)}, f32[8,128]{1,0:T(8,128)S(1)}, u32[]{:S(2)}, u32[]{:S(2)}) collective-permute-start(f32[8,128]{1,0:T(8,128)} %halo_send.1), channel_id=1, source_target_pairs={{1,0},{2,1},{3,2},{4,3},{5,4},{6,5},{7,6},{0,7},{9,8},{10,9},{11,1... | collective-permute-start | bytes 12296 | tf_op jit(solution)/shard_map/ppermute | solution.py:507
  30.4 2.2 %collective-permute-start = (f32[8,128]{1,0:T(8,128)}, f32[8,128]{1,0:T(8,128)S(1)}, u32[]{:S(2)}, u32[]{:S(2)}) collective-permute-start(f32[8,128]{1,0:T(8,128)} %halo_send.1), channel_id=1, source_target_pairs={{0,1},{1,2},{2,3},{3,4},{4,5},{5,6},{6,7},{7,0},{8,9},{9,10},{10,1... | collective-permute-start | bytes 12296 | tf_op jit(solution)/shard_map/ppermute | solution.py:506
  33.3 0.6 pad_add_fusion.scalars
  34.7 6.3 %collective-permute-done = f32[8,128]{1,0:T(8,128)S(1)} collective-permute-done((f32[8,128]{1,0:T(8,128)}, f32[8,128]{1,0:T(8,128)S(1)}, u32[]{:S(2)}, u32[]{:S(2)}) %collective-permute-start) | collective-permute-done | bytes 4128 | tf_op jit(solution)/shard_map/ppermute | solution.py:506
  41.0 0.6 broadcast_select_fusion.ghost
  41.6 0.8 copy-done
  42.4 12.1 %energy_slopes.1 = (f32[8,4,128]{2,1,0:T(4,128)}, f32[8,256]{1,0:T(8,128)}, f32[128,2048]{1,0:T(8,128)}, f32[128,2048]{1,0:T(8,128)}, f32[128,2048]{1,0:T(8,128)...) custom-call(s32[3]{0:T(128)} %pad_add_fusion.scalars, ...), custom_call_target="tpu_custom_call" | custom-call | tf_op jit(solution)/shard_map/energy_slopes/pallas_call | solution.py:418
  54.5 3.3 %all-to-all-start.1 = ((f32[8,4,128]{2,1,0:T(4,128)}), f32[8,4,128]{2,1,0:T(4,128)S(1)}, u32[]{:S(2)}, u32[]{:S(2)}) async-start(f32[8,4,128]{2,1,0:T(4,128)} %get-tuple-element.25), calls=%async_computation.1 | async-start | bytes 32768 | tf_op jit(solution)/shard_map/all_to_all | solution.py:514
  57.8 0.6 pad_maximum_fusion.refs
  58.4 8.3 %all-to-all-done.1.received = f32[8,4,128]{2,1,0:T(4,128)S(1)} async-done(((f32[8,4,128]{2,1,0:T(4,128)}), f32[8,4,128]{2,1,0:T(4,128)S(1)}, u32[]{:S(2)}, u32[]{:S(2)}) %all-to-all-start.1) | async-done | bytes 16416 | tf_op jit(solution)/shard_map/all_to_all | solution.py:514
  66.7 0.6 copy-done.1
  67.3 12.7 %weight_gradients.1 = (f32[8,128]{1,0:T(8,128)}, f32[8,128]{1,0:T(8,128)}, f32[64,16,128]{2,1,0:T(8,128)}) custom-call(s32[3]{0:T(128)} %pad_add_fusion.scalars, f32[10]{0:T(128)} %pad_maximum_fusion.refs, f32[64,16,128]{2,1,0:T(8,128)} %copy-done, f32[8,128]{1,0:T(8,128)} %maximum_maximum_fusion.own, f32[8,128]{1,0:T(8,128)} %broadcast_select_fusion.ghost, ...), custom_call_target="tpu_custom_call" | custom-call | tf_op jit(solution)/shard_map/weight_gradients/pallas_call | solution.py:431
  80.0 13.3 %all-to-all-start.2 = ((f32[64,16,128]{2,1,0:T(8,128)}), f32[64,16,128]{2,1,0:T(8,128)S(1)}, u32[]{:S(2)}, u32[]{:S(2)}) async-start(f32[64,16,128]{2,1,0:T(8,128)} %get-tuple-element.41), calls=%async_computation.2 | async-start | bytes 1048576 | tf_op jit(solution)/shard_map/all_to_all | solution.py:517
  93.3 1.3 %slice.79 = f32[1,1]{1,0:T(1,128)} slice(f32[8,128]{1,0:T(8,128)} %get-tuple-element.43), slice={[3:4], [9:10]} | slice | bytes 8 | tf_op jit(solution)/shard_map/slice | solution.py:526
  94.6 0.7 multiply_reduce_fusion
  95.3 0.6 div.27
  95.9 14.5 %all-to-all-done.2 = f32[64,16,128]{2,1,0:T(8,128)S(1)} async-done(((f32[64,16,128]{2,1,0:T(8,128)}), f32[64,16,128]{2,1,0:T(8,128)S(1)}, u32[]{:S(2)}, u32[]{:S(2)}) %all-to-all-start.2) | async-done | bytes 524320 | tf_op jit(solution)/shard_map/all_to_all | solution.py:517
  110.5 0.6 broadcast_in_dim.38
  111.2 3.5 %all-to-all-start.3 = ((f32[8,16,128]{2,1,0:T(8,128)}), f32[8,16,128]{2,1,0:T(8,128)S(1)}, u32[]{:S(2)}, u32[]{:S(2)}) async-start(f32[8,16,128]{2,1,0:T(8,128)} %broadcast_in_dim.38), calls=%async_computation.3 | async-start | bytes 131072 | tf_op jit(solution)/shard_map/all_to_all | solution.py:519
  114.7 0.6 copy.55
  115.2 8.5 %all-to-all-done.3 = f32[8,16,128]{2,1,0:T(8,128)S(1)} async-done(((f32[8,16,128]{2,1,0:T(8,128)}), f32[8,16,128]{2,1,0:T(8,128)S(1)}, u32[]{:S(2)}, u32[]{:S(2)}) %all-to-all-start.3) | async-done | bytes 65568 | tf_op jit(solution)/shard_map/all_to_all | solution.py:519
  124.6 0.4 copy-done.4
  125.2 0.6 multiply_subtract_fusion
  (56 shorter events, 2.1 us)
Async XLA Ops:
  2.3 0.7 slice-start
  3.2 0.7 copy-start.11
  5.0 15.6 %copy-start.12 = (s32[1,1,128]{2,1,0:T(1,128)S(1)}, s32[1,1,128]{2,1,0:T(1,128)}, u32[]{:S(2)}) copy-start(s32[1,1,128]{2,1,0:T(1,128)} %param.14) | copy-start | bytes 1540
  5.0 15.7 %copy-start.9 = (s32[1,1,32]{2,1,0:T(1,128)S(1)}, s32[1,1,32]{2,1,0:T(1,128)}, u32[]{:S(2)}) copy-start(s32[1,1,32]{2,1,0:T(1,128)} %param.18) | copy-start | bytes 388
  5.0 15.7 %copy-start.10 = (s32[1,1,32]{2,1,0:T(1,128)S(1)}, s32[1,1,32]{2,1,0:T(1,128)}, u32[]{:S(2)}) copy-start(s32[1,1,32]{2,1,0:T(1,128)} %param.19) | copy-start | bytes 388
  5.0 36.6 %all-to-all-start = ((f32[64,16,128]{2,1,0:T(8,128)}), f32[64,16,128]{2,1,0:T(8,128)S(1)}, u32[]{:S(2)}, u32[]{:S(2)}) async-start(f32[64,16,128]{2,1,0:T(8,128)} %broadcast_in_dim.33), calls=%async_computation | async-start | bytes 1048576 | tf_op jit(solution)/shard_map/all_to_all | solution.py:509
  20.7 0.7 copy-start.5
  20.7 0.7 copy-start.6
  23.5 11.2 %collective-permute-start.1 = (f32[8,128]{1,0:T(8,128)}, f32[8,128]{1,0:T(8,128)S(1)}, u32[]{:S(2)}, u32[]{:S(2)}) collective-permute-start(f32[8,128]{1,0:T(8,128)} %halo_send.1), channel_id=1, source_target_pairs={{1,0},{2,1},{3,2},{4,3},{5,4},{6,5},{7,6},{0,7},{9,8},{10,9},{11,1... | collective-permute-start | bytes 12296 | tf_op jit(solution)/shard_map/ppermute | solution.py:507
  30.4 10.6 %collective-permute-start = (f32[8,128]{1,0:T(8,128)}, f32[8,128]{1,0:T(8,128)S(1)}, u32[]{:S(2)}, u32[]{:S(2)}) collective-permute-start(f32[8,128]{1,0:T(8,128)} %halo_send.1), channel_id=1, source_target_pairs={{0,1},{1,2},{2,3},{3,4},{4,5},{5,6},{6,7},{7,0},{8,9},{9,10},{10,1... | collective-permute-start | bytes 12296 | tf_op jit(solution)/shard_map/ppermute | solution.py:506
  33.3 1.3 copy-start.7
  41.6 0.8 copy-start
  54.5 12.2 %all-to-all-start.1 = ((f32[8,4,128]{2,1,0:T(4,128)}), f32[8,4,128]{2,1,0:T(4,128)S(1)}, u32[]{:S(2)}, u32[]{:S(2)}) async-start(f32[8,4,128]{2,1,0:T(4,128)} %get-tuple-element.25), calls=%async_computation.1 | async-start | bytes 32768 | tf_op jit(solution)/shard_map/all_to_all | solution.py:514
  66.7 0.6 copy-start.1
  80.0 30.5 %all-to-all-start.2 = ((f32[64,16,128]{2,1,0:T(8,128)}), f32[64,16,128]{2,1,0:T(8,128)S(1)}, u32[]{:S(2)}, u32[]{:S(2)}) async-start(f32[64,16,128]{2,1,0:T(8,128)} %get-tuple-element.41), calls=%async_computation.2 | async-start | bytes 1048576 | tf_op jit(solution)/shard_map/all_to_all | solution.py:517
  111.2 3.5 %copy-start.8 = (f32[8,128]{1,0:T(8,128)S(1)}, f32[8,128]{1,0:T(8,128)}, u32[]{:S(2)}) copy-start(f32[8,128]{1,0:T(8,128)} %get-tuple-element.42) | copy-start | bytes 12292
  111.2 12.5 %all-to-all-start.3 = ((f32[8,16,128]{2,1,0:T(8,128)}), f32[8,16,128]{2,1,0:T(8,128)S(1)}, u32[]{:S(2)}, u32[]{:S(2)}) async-start(f32[8,16,128]{2,1,0:T(8,128)} %broadcast_in_dim.38), calls=%async_computation.3 | async-start | bytes 131072 | tf_op jit(solution)/shard_map/all_to_all | solution.py:519
  124.3 0.7 copy-start.4
  124.4 0.7 copy-start.2
  124.5 0.7 copy-start.3

commit v2 on v1

v2 whole, which is shorter than its diff:
```python
import functools
import jax
import jax.numpy as jnp
from jax import lax
from jax.experimental import pallas as pl
from jax.experimental.pallas import tpu as pltpu
from jax.sharding import PartitionSpec as P

C = 128
FF = 512
K = 64
NS = 100
A = 128
G = 32
DEG = 16
STEP = 100
E = A * DEG
N = A + 2 * G
EC = 1024
CHUNKS = E // EC
BLOCKS = 16
KEPT = [8, 8, C, C, C]

highest = lax.Precision.HIGHEST
cutoff = 6.0
slab_width = 20.0
cross_area = 36.0
force_weight = 10.0
stress_weight = 100.0
spread = 0.5 * ((K - 1) / cutoff) ** 2

f32 = jnp.float32
bf16 = jnp.bfloat16
NN = ((1,), (0,))
NT = ((1,), (1,))


def split(x):
    high = x.astype(bf16)
    return high, (x - high.astype(f32)).astype(bf16)


def mm(a, b, dims):
    return lax.dot_general(a, b, (dims, ((), ())), preferred_element_type=f32)


def stack(x):
    return jnp.concatenate(split(x), axis=0)


def fold_rows(x):
    half = x.shape[0] // 2
    return x[:half] + x[half:]


def fold(x):
    half = x.shape[1] // 2
    x = fold_rows(x)
    return x[:, :half] + x[:, half:]


def lhs(w):
    high, low = split(w)
    return jnp.concatenate(
        [jnp.concatenate([high, high], axis=1), jnp.concatenate([low, jnp.zeros_like(low)], axis=1)], axis=0
    )


def wdot(w, x):
    return fold_rows(mm(w, x, NN))


def wide(x):
    return jnp.concatenate(split(x), axis=1)


def twice(x):
    return jnp.concatenate([x, x], axis=0)


def exact(x):
    one = x.astype(bf16).astype(f32)
    two = (x - one).astype(bf16).astype(f32)
    return jnp.concatenate([one, two, x - one - two], axis=0).astype(bf16)


def whole(x):
    return x[0:8] + x[8:16] + x[16:24]


def full_dot(a, b, dims):
    return lax.dot_general(a, b, (dims, ((), ())), precision=highest, preferred_element_type=f32)


def iota(shape, dim):
    return lax.broadcasted_iota(jnp.int32, shape, dim)


def select_lists(lists):
    return (iota((A, 128), 0) == lists).astype(f32)


def place(pieces, stride, offset, first, last):
    lane = iota((8, 128), 1)
    row = iota((8, 128), 0)
    column = iota((128, 128), 0)
    slot = iota((128, 128), 1)
    lefts, rights = [], []
    for i in range(first, last + 1):
        chosen = [jnp.where(lane % stride == row, p[:, 128 * i : 128 * i + 128], 0.0) for p in pieces]
        lefts.append(jnp.concatenate(chosen, axis=0))
        rights.append((column // stride + (128 // stride) * i == slot + offset).astype(f32))
    return whole(
        mm(
            jnp.concatenate(lefts, axis=1).astype(bf16),
            jnp.concatenate(rights, axis=0).astype(bf16),
            NN,
        )
    )


def prepare_kernel(positions, species, force_ref, send_left, send_right, shard, own, lists, outgoing, blocks):
    own[...] = jnp.concatenate(
        [positions[...], species[...].astype(f32), force_ref[...], jnp.zeros((1, A), f32)], axis=0
    )
    lists[...] = jnp.concatenate(
        [send_right[...], send_left[...], jnp.full((1, 128 - 2 * G), -1, jnp.int32)], axis=1
    )
    outgoing[...] = full_dot(own[...], select_lists(lists[...]), NN)
    x = shard[...]
    one = x.astype(bf16).astype(f32)
    two = (x - one).astype(bf16).astype(f32)
    pieces = [one, two, x - one - two]
    table = place(pieces, 2, 0, 0, 1)
    radial = place(pieces, 2, 100, 1, 2)
    lane = iota((1, 128), 1)
    block = jnp.concatenate(
        [
            table[:2],
            jnp.where(lane < K, radial[:1], pltpu.roll(radial[1:2], K, 1)),
            place(pieces, 2, 164, 2, 4)[:2],
            place(pieces, 2, 292, 4, 6)[:2],
            place(pieces, 8, 105, 6, 14),
            jnp.where(lane < 56, pltpu.roll(x[:, 14 * 128 :], 56, 1), 0.0),
        ],
        axis=0,
    )
    for j in range(blocks.shape[0]):
        blocks[j] = block


def weight(wg, first):
    return jnp.concatenate([wg[:, first, :], wg[:, first + 1, :]], axis=0)


def update_weight_t(wg):
    return jnp.concatenate([wg[:, 7 + h, :] for h in range(8)], axis=0)


def readout_column(wg):
    block = wg[:, 15, :]
    return jnp.concatenate([block[:, h : h + 1] for h in range(8)], axis=0)


def radial_one_t(wg):
    block = wg[:, 2, :]
    return jnp.concatenate([block[:, :K], block[:, K:]], axis=0)


def silu_parts(a):
    sig = 0.5 * jnp.tanh(0.5 * a) + 0.5
    first = sig * (1.0 + a * (1.0 - sig))
    return sig, first


def silu_second(a, sig):
    return sig * (1.0 - sig) * (2.0 + a * (1.0 - 2.0 * sig))


def one_hots(s, t):
    s = jnp.where(s < G, s + A, jnp.where(s < G + A, s - G, s))
    hot_s = (iota((N, EC), 0) == s).astype(f32).astype(bf16)
    hot_t = (iota((A, EC), 0) == t).astype(f32).astype(bf16)
    return hot_s, hot_t


def forward_kernel(
    slabs, count_ref, scalars, wg, own, from_left, from_right, src, dst, lists,
    message, contrib_out, h_out, dn_out, dh_out, z_out, emb_out, *rest,
):
    large = len(KEPT)
    far, near = rest[:large], rest[large : 2 * large]
    src_hot, dst_hot, total, force_total, sems = rest[2 * large :]
    rows_out, vec_out, dfilt_out, q_out, filt_out = near
    copies = []

    count = count_ref[0, 0]
    rank = scalars[0]
    box = slab_width * slabs
    table_t = weight(wg, 0)
    one_t = lhs(radial_one_t(wg))
    two_t = lhs(weight(wg, 3))
    message_t = lhs(weight(wg, 5))
    update_f = update_weight_t(wg)
    update_t = lhs(update_f)
    update = lhs(update_f.T)
    readout = readout_column(wg)

    own_rows = own[...]
    lane = iota((8, 128), 1)
    row = iota((8, 128), 0)
    ghost_rows = jnp.where(lane < G, from_left[...], from_right[...])
    shift = jnp.where(lane < G, jnp.where(rank == 0, -box, 0.0), 0.0)
    shift = shift + jnp.where((lane >= G) & (lane < 2 * G), jnp.where(rank == slabs - 1, box, 0.0), 0.0)
    ghost_pos = ghost_rows + jnp.where(row == 0, shift, 0.0)
    ext = jnp.concatenate([own_rows, ghost_pos], axis=1)
    pieces = exact(jnp.where(iota((8, 256), 0) < 3, ext, 0.0))
    kinds = ext[3:4, :].astype(jnp.int32)
    kind_hot = (iota((128, 256), 0) == kinds).astype(f32)
    table_hi, table_rest = split(table_t)
    table_lo = (table_t - table_hi.astype(f32) - table_rest.astype(f32)).astype(bf16)
    kind_bf = kind_hot.astype(bf16)
    emb = mm(table_hi, kind_bf, NN) + mm(table_rest, kind_bf, NN) + mm(table_lo, kind_bf, NN)
    emb_out[...] = emb
    projected = stack(wdot(message_t, stack(emb)))[:, :N]
    total[...] = jnp.zeros_like(total)
    centers = iota((K, EC), 0).astype(f32) * (cutoff / (K - 1))

    for i in range(CHUNKS):
        at = pl.ds(i * EC, EC)
        t = dst[:, at]
        hot_s, hot_t = one_hots(src[:, at], t)
        src_hot[:, at] = hot_s
        dst_hot[:, at] = hot_t
        vec = whole(mm(pieces[:, :N], hot_s, NN) - mm(pieces[:, :A], hot_t, NN))
        vec_out[:, at] = vec
        square = jnp.sum(vec * vec, axis=0, keepdims=True)
        dist = jnp.sqrt(square)
        inverse = jnp.where(square > 0.0, 1.0 / jnp.where(square > 0.0, dist, 1.0), 0.0)
        ratio = jnp.minimum(dist / cutoff, 1.0)
        live = (t < count).astype(f32)
        inside = 1.0 - ratio * ratio
        gate = inside * inside * live
        dgate = inside * ratio * (-4.0 / cutoff) * live
        rows_out[0:1, at] = dist
        rows_out[1:2, at] = inverse
        rows_out[2:3, at] = gate
        rows_out[3:4, at] = dgate
        delta = dist - centers
        basis = jnp.exp(-spread * delta * delta)
        dbasis = (-2.0 * spread) * delta * basis
        a = wdot(one_t, stack(basis))
        da = wdot(one_t, stack(dbasis))
        sig, slope = silu_parts(a)
        f = wdot(two_t, stack(a * sig))
        df = wdot(two_t, stack(slope * da))
        filt = f * gate
        dfilt = df * gate + f * dgate
        q = fold_rows(mm(projected, hot_s, NN))
        filt_out[:, at] = filt
        dfilt_out[:, at] = dfilt
        q_out[:, at] = q
        total[...] += mm(stack(filt * q), hot_t, NT)
        for k in range(large):
            copy = pltpu.make_async_copy(near[k].at[:, at], far[k].at[:, at], sems.at[k, i])
            copy.start()
            copies.append(copy)

    hidden = emb[:, :A] + fold_rows(total[...]) * (1.0 / DEG)
    h_out[...] = hidden
    rms = lax.rsqrt(jnp.mean(hidden * hidden, axis=0, keepdims=True) + 1e-05)
    z = wdot(update_t, stack(hidden * rms))
    z_out[...] = z
    sig, slope = silu_parts(z)
    live_atom = (iota((1, A), 1) < count).astype(f32)
    weighted = readout * live_atom
    energy = jnp.sum(jnp.sum(weighted * (z * sig), axis=0, keepdims=True), axis=1, keepdims=True)
    dn = wdot(update, stack(weighted * slope))
    dn_out[...] = dn
    cube = rms * rms * rms * (1.0 / C)
    dh = rms * dn - hidden * (cube * jnp.sum(dn * hidden, axis=0, keepdims=True))
    dh_out[...] = dh
    dh_pieces = wide(dh * (1.0 / DEG))
    force_total[...] = jnp.zeros_like(force_total)

    stress = jnp.zeros((8, 8), f32)
    for i in range(CHUNKS):
        at = pl.ds(i * EC, EC)
        hot_s = src_hot[:, at]
        hot_t = dst_hot[:, at]
        back = mm(dh_pieces, twice(hot_t), NN)
        along = jnp.sum(back * (dfilt_out[:, at] * q_out[:, at]), axis=0, keepdims=True)
        vec = vec_out[:, at]
        slopes = vec * (along * rows_out[1:2, at])
        three = exact(slopes)
        force_total[:, :N] += mm(three, hot_s, NT)
        force_total[:, :A] -= mm(three, hot_t, NT)
        stress = stress + full_dot(slopes, vec, NT)

    contrib = whole(force_total[...])
    contrib_out[...] = contrib
    lists_hot = select_lists(lists[...])
    outgoing = full_dot(contrib[:, :A], lists_hot, NN) + pltpu.roll(contrib[:, A:], 64, 1)
    to_right = (lane < G) | (lane >= 96)
    sums = jnp.zeros((8, 128), f32)
    for i in range(3):
        for j in range(3):
            sums = sums + jnp.where(lane == 3 * i + j, stress[i : i + 1, j : j + 1], 0.0)
    sums = sums + jnp.where(lane == 9, energy, 0.0)
    right = lax.rem(rank + 1, slabs)
    left = lax.rem(rank + slabs - 1, slabs)
    for d in range(8):
        keep = (to_right & (right == d)) | (jnp.logical_not(to_right) & (left == d))
        message[d] = jnp.where(row == 3, sums, jnp.where(keep, outgoing, 0.0))[:4]
    for copy in copies:
        copy.wait()


def backward_kernel(
    slabs, count_ref, scalars, energy_ref, stress_ref, wg, own, from_left, from_right, src, dst, lists, received, contrib_in, h_in, dn_in, dh_in, z_in, emb_in, *rest,
):
    large = len(KEPT)
    far, near = rest[:large], rest[large + 4 : 2 * large + 4]
    forces_out, sums_out, keep, give = rest[large : large + 4]
    src_hot, dst_hot, grad, step_row, total, source_total, one_total, two_total, sems = rest[2 * large + 4 :]
    rows_in, vec_in, dfilt_in, q_in, filt_in = near
    copies = [pltpu.make_async_copy(far[k], near[k], sems.at[k]) for k in range(large)]
    for copy in copies:
        copy.start()

    count = count_ref[0, 0]
    core = scalars[1]
    volume = slab_width * cross_area * slabs
    scale = 2.0 / (slabs * A)
    one_t = lhs(radial_one_t(wg))
    two = lhs(weight(wg, 3).T)
    message_w = lhs(weight(wg, 5).T)
    update_f = update_weight_t(wg)
    update_t = lhs(update_f)
    update = lhs(update_f.T)
    readout = readout_column(wg)
    lists_hot = select_lists(lists[...])
    lane = iota((8, 128), 1)
    row = iota((8, 128), 0)
    ghost = jnp.where(lane < G, from_left[...], from_right[...])

    got = jnp.sum(received[...], axis=0)
    got = jnp.concatenate([got, jnp.zeros_like(got)], axis=0)
    moved = jnp.where(row < 3, got, 0.0)
    energy = got[3:4, 9:10]
    inner = jnp.where(lane < 2 * G, pltpu.roll(moved, 64, 1), 0.0)
    contrib = contrib_in[...]
    force_own = -(contrib[:, :A] + full_dot(inner, lists_hot, NT))
    force_ghost = -(contrib[:, A:] + jnp.where(lane < 2 * G, moved, 0.0))
    forces_out[...] = force_own
    sums_out[...] = got
    own_ref = jnp.concatenate([own[4:8], jnp.zeros((4, 128), f32)], axis=0)
    ghost_ref = jnp.concatenate([ghost[4:8], jnp.zeros((4, 128), f32)], axis=0)
    factor = force_weight * scale
    cot_own = jnp.where((lane < count) & (row < 3), factor * (force_own - own_ref), 0.0)
    cot_ghost = jnp.where((lane < 2 * G) & (row < 3), factor * (force_ghost - ghost_ref), 0.0)
    cot = exact(jnp.concatenate([cot_own, cot_ghost], axis=1))
    stress_cot = [
        [
            (2.0 * stress_weight / volume) * (got[3:4, 3 * i + j : 3 * i + j + 1] / volume - stress_ref[0, i, j])
            for j in range(3)
        ]
        for i in range(3)
    ]
    energy_cot = (energy - energy_ref[0]) * scale
    total[...] = jnp.zeros_like(total)

    for copy in copies[:2]:
        copy.wait()
    for i in range(CHUNKS):
        at = pl.ds(i * EC, EC)
        hot_s, hot_t = one_hots(src[:, at], dst[:, at])
        src_hot[:, at] = hot_s
        dst_hot[:, at] = hot_t
        vec = vec_in[:, at]
        delta = whole(mm(cot[:, :A], hot_t, NN) - mm(cot[:, :N], hot_s, NN))
        along = jnp.sum(vec * delta, axis=0, keepdims=True)
        for r in range(3):
            inner_row = sum(stress_cot[r][j] * vec[j : j + 1] for j in range(3))
            along = along + vec[r : r + 1] * inner_row
        step = along * rows_in[1:2, at]
        step_row[:, at] = step
    for copy in copies[2:4]:
        copy.wait()
    for i in range(CHUNKS):
        at = pl.ds(i * EC, EC)
        step = step_row[:, at]
        hot_t = dst_hot[:, at]
        total[...] += mm(stack(dfilt_in[:, at] * q_in[:, at] * step), hot_t, NT)

    hidden = h_in[...]
    dn = dn_in[...]
    dh = dh_in[...]
    z = z_in[...]
    moved_h = fold_rows(total[...]) * (1.0 / DEG)
    rms = lax.rsqrt(jnp.mean(hidden * hidden, axis=0, keepdims=True) + 1e-05)
    cube = rms * rms * rms
    cross = jnp.mean(hidden * moved_h, axis=0, keepdims=True)
    normed = hidden * rms
    moved_n = rms * moved_h - (cube * cross) * hidden
    moved_n2 = stack(moved_n)
    moved_z = wdot(update_t, moved_n2)
    sig, slope = silu_parts(z)
    live_atom = (iota((1, A), 1) < count).astype(f32)
    weighted = readout * live_atom
    z_bar = weighted * (energy_cot * slope + silu_second(z, sig) * moved_z)
    z_bar = stack(z_bar)
    update_grad = fold(
        mm(
            jnp.concatenate([z_bar, stack(weighted * slope)], axis=1),
            jnp.concatenate([stack(normed), moved_n2], axis=1),
            NT,
        )
    )
    readout_grad = jnp.sum(live_atom * (energy_cot * (z * sig) + slope * moved_z), axis=1, keepdims=True)
    n_bar = wdot(update, z_bar)
    dn_h = jnp.sum(dn * hidden, axis=0, keepdims=True) * (1.0 / C)
    mix = (jnp.sum(n_bar * hidden, axis=0, keepdims=True) + jnp.sum(dn * moved_h, axis=0, keepdims=True)) * (1.0 / C)
    h_bar = (
        rms * n_bar
        + hidden * (3.0 * cube * rms * rms * cross * dn_h - cube * mix)
        - moved_h * (cube * dn_h)
        - dn * (cube * cross)
    )
    for h in range(8):
        grad[:, 7 + h, :] = update_grad[64 * h : 64 * h + 64]
    lane64 = iota((64, 128), 1)
    block = jnp.zeros((64, 128), f32)
    for h in range(8):
        block = block + jnp.where(lane64 == h, readout_grad[64 * h : 64 * h + 64], 0.0)
    grad[:, 15, :] = block

    both_pieces = jnp.concatenate([wide(h_bar * (1.0 / DEG)), wide(dh * (1.0 / DEG))], axis=0)
    source_total[...] = jnp.zeros_like(source_total)
    one_total[...] = jnp.zeros_like(one_total)
    two_total[...] = jnp.zeros_like(two_total)
    centers = iota((K, EC), 0).astype(f32) * (cutoff / (K - 1))

    copies[4].wait()
    for i in range(CHUNKS):
        at = pl.ds(i * EC, EC)
        hot_s = src_hot[:, at]
        hot_t = dst_hot[:, at]
        step = step_row[:, at]
        gate = rows_in[2:3, at]
        dgate = rows_in[3:4, at]
        both = mm(both_pieces, twice(hot_t), NN)
        m_bar = both[:C]
        dm_bar = both[C:]
        q = q_in[:, at]
        source_total[...] += mm(
            stack(m_bar * filt_in[:, at] + dm_bar * (dfilt_in[:, at] * step)), hot_s, NT
        )
        dq = dm_bar * q
        f_bar = stack(m_bar * q * gate + dq * (dgate * step))
        df_bar = stack(dq * gate)
        s_bar = wdot(two, f_bar)
        ds_bar = wdot(two, df_bar)
        delta = rows_in[0:1, at] - centers
        basis = jnp.exp(-spread * delta * delta)
        moved_basis = (-2.0 * spread) * delta * basis * step
        basis = stack(basis)
        moved_basis = stack(moved_basis)
        a = wdot(one_t, basis)
        moved_a = wdot(one_t, moved_basis)
        sig, slope = silu_parts(a)
        two_total[...] += mm(f_bar, stack(a * sig), NT) + mm(df_bar, stack(slope * moved_a), NT)
        a_bar = stack(s_bar * slope + ds_bar * (silu_second(a, sig) * moved_a))
        da_bar = stack(ds_bar * slope)
        one_total[...] += mm(a_bar, basis, NT) + mm(da_bar, moved_basis, NT)

    one_grad = fold(one_total[...])
    grad[:, 2, :] = jnp.concatenate([one_grad[:64], one_grad[64:]], axis=1)
    two_grad = fold(two_total[...])
    grad[:, 3, :] = two_grad[:64]
    grad[:, 4, :] = two_grad[64:]
    p_bar = fold_rows(source_total[...])
    p_bar = jnp.concatenate([p_bar, jnp.zeros((C, 256 - N), f32)], axis=1)
    p_pieces = stack(p_bar)
    emb = emb_in[...]
    message_grad = fold(mm(p_pieces, stack(emb), NT))
    grad[:, 5, :] = message_grad[:64]
    grad[:, 6, :] = message_grad[64:]
    emb_bar = wdot(message_w, p_pieces)
    emb_bar = jnp.concatenate([emb_bar[:, :A] + h_bar, emb_bar[:, A:]], axis=1)
    kinds = jnp.concatenate([own[3:4], ghost[3:4]], axis=1).astype(jnp.int32)
    kind_hot = (iota((128, 256), 0) == kinds).astype(f32).astype(bf16)
    table_grad = fold_rows(mm(stack(emb_bar), kind_hot, NT))
    grad[:, 0, :] = table_grad[:64]
    grad[:, 1, :] = table_grad[64:]
    for j in range(32):
        keep[j] = grad[2 * j + core]
        give[j] = grad[2 * j + 1 - core]


vmem = pl.BlockSpec(memory_space=pltpu.VMEM)
smem = pl.BlockSpec(memory_space=pltpu.SMEM)
far = pl.BlockSpec(memory_space=pl.ANY)
params_vmem = pltpu.CompilerParams(vmem_limit_bytes=56 * 1024 * 1024)
edge_scratch = [pltpu.VMEM((rows, E), f32) for rows in KEPT]


def shape(*dims, dtype=jnp.float32):
    return jax.ShapeDtypeStruct(dims, dtype)


def prepare(positions, species, force_ref, send_left, send_right, shard, shards):
    return pl.pallas_call(
        prepare_kernel,
        out_shape=[shape(8, 128), shape(1, 128, dtype=jnp.int32), shape(8, 128), shape(shards, BLOCKS, 128)],
        in_specs=[vmem] * 6,
        out_specs=[vmem] * 4,
        compiler_params=params_vmem,
        name="prepare",
    )(positions, species, force_ref, send_left, send_right, shard)


def forward(slabs, counts, scalars, wg, own, from_left, from_right, src, dst, lists):
    outs = [
        shape(8, 4, 128), shape(8, 256), shape(C, A), shape(C, A), shape(C, A), shape(FF, A), shape(C, 256),
    ]
    return pl.pallas_call(
        functools.partial(forward_kernel, slabs),
        out_shape=outs + [shape(rows, E) for rows in KEPT],
        in_specs=[smem] * 2 + [vmem] * 7,
        out_specs=[vmem] * len(outs) + [far] * len(KEPT),
        scratch_shapes=edge_scratch
        + [
            pltpu.VMEM((N, E), bf16),
            pltpu.VMEM((A, E), bf16),
            pltpu.VMEM((2 * C, A), f32),
            pltpu.VMEM((24, 256), f32),
            pltpu.SemaphoreType.DMA((len(KEPT), CHUNKS)),
        ],
        compiler_params=params_vmem,
        name="energy_slopes",
    )(counts, scalars, wg, own, from_left, from_right, src, dst, lists)


def backward(slabs, counts, scalars, energy_ref, stress_ref, wg, own, from_left, from_right, src, dst, lists, received, kept):
    outs = [shape(8, 128), shape(8, 128), shape(32, BLOCKS, 128), shape(32, BLOCKS, 128)]
    return pl.pallas_call(
        functools.partial(backward_kernel, slabs),
        out_shape=outs,
        in_specs=[smem] * 4 + [vmem] * (8 + len(kept) - len(KEPT)) + [far] * len(KEPT),
        out_specs=[vmem] * 4,
        scratch_shapes=edge_scratch
        + [
            pltpu.VMEM((N, E), bf16),
            pltpu.VMEM((A, E), bf16),
            pltpu.VMEM((64, BLOCKS, 128), f32),
            pltpu.VMEM((1, E), f32),
            pltpu.VMEM((2 * C, A), f32),
            pltpu.VMEM((2 * C, N), f32),
            pltpu.VMEM((2 * C, 2 * K), f32),
            pltpu.VMEM((2 * C, 2 * C), f32),
            pltpu.SemaphoreType.DMA((len(KEPT),)),
        ],
        compiler_params=params_vmem,
        name="weight_gradients",
    )(counts, scalars, energy_ref, stress_ref, wg, own, from_left, from_right, src, dst, lists, received, *kept)


def from_blocks(y):
    two = jnp.concatenate([y[0:2, :100], y[2].reshape(2, 64), y[3:5], y[5:7]], axis=1)
    return jnp.concatenate([two.T.reshape(-1), y[7:15].T.reshape(-1), y[15, :56]])


def adam(params, moment_one, moment_two, grad):
    new_moment_one = 0.9 * moment_one + 0.1 * grad
    new_moment_two = 0.999 * moment_two + 0.001 * grad * grad
    corrected_one = new_moment_one / (1.0 - 0.9**STEP)
    corrected_two = new_moment_two / (1.0 - 0.999**STEP)
    new_params = params - 0.001 * (
        corrected_one / (jnp.sqrt(corrected_two) + 1e-08) + 0.01 * params
    )
    return new_params, new_moment_one, new_moment_two


def body(
    positions,
    species,
    counts,
    source,
    target,
    send_left,
    send_right,
    energy_ref,
    force_ref,
    stress_ref,
    params,
    moment_one,
    moment_two,
):
    shards = lax.axis_size("dp")
    slabs = lax.axis_size("graph")
    rank = lax.axis_index("graph")
    index = lax.axis_index("dp")
    core = index % 2
    scalars = jnp.stack([rank, core]).astype(jnp.int32)
    own, lists, outgoing, blocks = prepare(
        positions[0, 0], species[0], force_ref[0, 0], send_left[0], send_right[0], params[None], shards
    )
    wg = lax.all_to_all(blocks, "dp", 0, 0, tiled=True)
    from_left = lax.ppermute(outgoing, "graph", [(i, (i + 1) % slabs) for i in range(slabs)])
    from_right = lax.ppermute(outgoing, "graph", [((i + 1) % slabs, i) for i in range(slabs)])
    message, *kept = forward(
        slabs, counts, scalars, wg, own, from_left, from_right, source[0], target[0], lists
    )
    received = lax.all_to_all(message, "graph", 0, 0, tiled=True)
    forces, sums, keep, give = backward(
        slabs, counts, scalars, energy_ref, stress_ref, wg, own, from_left, from_right, source[0], target[0], lists, received, kept
    )
    volume = slabs * slab_width * cross_area
    pair = keep + lax.ppermute(give, "dp", [(i, i ^ 1) for i in range(shards)])
    chips = [list(range(c, shards, 2)) for c in range(2)]
    within = jnp.sum(
        lax.all_to_all(pair, "dp", 0, 0, tiled=True, axis_index_groups=chips), axis=0
    )
    copies = jnp.broadcast_to(within[None], (slabs, BLOCKS, 128))
    grad = from_blocks(jnp.sum(lax.all_to_all(copies, "graph", 0, 0, tiled=True), axis=0))
    new_params, new_moment_one, new_moment_two = adam(params, moment_one, moment_two, grad)
    return (
        new_params,
        new_moment_one,
        new_moment_two,
        forces[:3][None, None],
        sums[3, 9][None],
        (sums[3, :9] / volume).reshape(1, 3, 3),
    )


def solution(mesh):
    in_specs = (
        P("dp", "graph", None, None),
        P("dp", "graph", None),
        P("dp", "graph"),
        P("dp", "graph", None),
        P("dp", "graph", None),
        P("dp", "graph", None),
        P("dp", "graph", None),
        P("dp"),
        P("dp", "graph", None, None),
        P("dp", None, None),
        P("dp"),
        P("dp"),
        P("dp"),
    )
    out_specs = (
        P("dp"),
        P("dp"),
        P("dp"),
        P("dp", "graph", None, None),
        P("dp"),
        P("dp", None, None),
    )
    return jax.shard_map(body, mesh=mesh, in_specs=in_specs, out_specs=out_specs, check_vma=False)
```

time: 127 us -> 114 us (0.90)
  Pallas kernels: 26.2 us -> 19 us
  waiting for transfers between devices: 37.6 us -> 32.8 us
  local copies, waits for them, and re-layouts: 10.3 us -> 8.31 us
  starting transfers between devices: 44.8 us -> 46.2 us
    pallas_call x3, Pallas kernels: 26.2 us -> 19 us  [the longest x1 9.47 us: backward(): pl.pallas_call(functools.partial(backward_kernel, slabs), out_shape=outs,...]
    all_to_all x2, waiting for transfers between devices: 23 us -> 16.9 us  [the longest x1 8.44 us: body(): lax.all_to_all(copies, 'graph', 0, 0, tiled=True)]
    all_to_all x2, starting transfers between devices: 16.8 us -> 11.2 us  [the longest x1 7.68 us: body(): lax.all_to_all(pair, 'dp', 0, 0, tiled=True, axis_index_groups=chips)]
    ppermute x0 -> x1, starting transfers between devices: none -> 3.78 us  [body(): pair = keep + lax.ppermute(give, 'dp', [(i, i ^ 1) for i in range(shards)])]
    all_to_all x1, starting transfers between devices: 3.33 us -> 6.54 us  [body(): received = lax.all_to_all(message, 'graph', 0, 0, tiled=True)]
    slice x5 -> x0, local copies, waits for them, and re-layouts: 2.23 us -> none  [the longest x1 0.77 us: to_blocks(): x[840:1864].reshape(128, 8)]
    add x0 -> x1, other arithmetic: none -> 1.67 us  [body(): pair = keep + lax.ppermute(give, 'dp', [(i, i ^ 1) for i in range(shards)])]
    ppermute x0 -> x1, waiting for transfers between devices: none -> 1.35 us  [body(): pair = keep + lax.ppermute(give, 'dp', [(i, i ^ 1) for i in range(shards)])]
  transfers between devices with their start and end apart: 6 -> 7, of which waited for: 4 -> 6; matrix products, arithmetic and copies ran while one was open for 5% -> 4% of each run, Pallas kernels for 1% -> 0%
where the time goes in v2:
time: 114 us; the launch traced here: 112 us
  starting transfers between devices  46.2 us (41%)
  waiting for transfers between devices  32.8 us (29%)
  Pallas kernels  19 us (17%)
  local copies, waits for them, and re-layouts  8.31 us (7%)
  other arithmetic  3.7 us (3%)
  between operations  2.16 us (2%)
    all_to_all x1, starting transfers between devices, body(): wg = lax.all_to_all(blocks, 'dp', 0, 0, tiled=True)  15.5 us
    pallas_call x1, Pallas kernels, backward(): pl.pallas_call(functools.partial(backward_kernel, slabs), out_shape=outs,...  9.47 us
    all_to_all x1, waiting for transfers between devices, body(): lax.all_to_all(copies, 'graph', 0, 0, tiled=True)  8.44 us
    all_to_all x1, waiting for transfers between devices, body(): lax.all_to_all(pair, 'dp', 0, 0, tiled=True, axis_index_groups=chips)  8.42 us
    all_to_all x1, waiting for transfers between devices, body(): received = lax.all_to_all(message, 'graph', 0, 0, tiled=True)  7.7 us
    all_to_all x1, starting transfers between devices, body(): lax.all_to_all(pair, 'dp', 0, 0, tiled=True, axis_index_groups=chips)  7.68 us
    pallas_call x1, Pallas kernels, forward(): pl.pallas_call(functools.partial(forward_kernel, slabs), out_shape=outs +...  7.6 us
    ppermute x1, starting transfers between devices, body(): lax.ppermute(outgoing, 'graph', [((i + 1) % slabs, i) for i in range(slab...  6.95 us
  transfers between devices with their start and end apart: 7, of which 6 were waited for; matrix products, arithmetic and copies ran while one was open for 4% of the time, Pallas kernels for 0%

profile of v2, /device:TPU:1, one launch (start us, length us, event | category | flops | bytes accessed | tf_op | source)
XLA Modules:
  0.0 112.2 jit_solution(2276575072014506355)
XLA Ops:
  0.7 1.3 %broadcast_in_dim.12.shard = f32[1,1920]{1,0:T(1,128)} reshape(f32[1920]{0:T(1024)} %param.23) | data formatting | bytes 15360 | tf_op jit(solution)/shard_map/broadcast_in_dim | solution.py:607
  2.0 0.6 copy_bitcast_fusion
  2.5 1.9 %prepare.1 = (f32[8,128]{1,0:T(8,128)}, s32[1,128]{1,0:T(1,128)}, f32[8,128]{1,0:T(8,128)}, f32[64,16,128]{2,1,0:T(8,128)}) custom-call(f32[3,128]{1,0:T(4,128)} %get-tuple-element.70.positions, s32[1,128]{1,0:T(1,128)} %bitcast.24, f32[3,128]{1,0:T(4,128)} %get-tuple-element.69.force_ref, s32[1,32]{1,0:T(1,128)} %bitcast.25, s32[1,32]{1,0:T(1,128)} %bitcast.26, ...), custom_call_target="tpu_custom_call" | custom-call | tf_op jit(solution)/shard_map/prepare/pallas_call | solution.py:513
  4.5 15.5 %all-to-all-start = ((f32[64,16,128]{2,1,0:T(8,128)}), f32[64,16,128]{2,1,0:T(8,128)S(1)}, u32[]{:S(2)}, u32[]{:S(2)}) async-start(f32[64,16,128]{2,1,0:T(8,128)} %get-tuple-element.26), calls=%async_computation | async-start | bytes 1048576 | tf_op jit(solution)/shard_map/all_to_all | solution.py:609
  20.0 7.0 %collective-permute-start.1 = (f32[8,128]{1,0:T(8,128)S(1)}, f32[8,128]{1,0:T(8,128)S(1)}, u32[]{:S(2)}, u32[]{:S(2)}) collective-permute-start(f32[8,128]{1,0:T(8,128)S(1)} %copy-done.11), channel_id=1, source_target_pairs={{1,0},{2,1},{3,2},{4,3},{5,4},{6,5},{7,6},{0,7},{9,8},{10,9},{11,1... | collective-permute-start | bytes 12296 | tf_op jit(solution)/shard_map/ppermute | solution.py:611
  27.0 2.2 %collective-permute-start = (f32[8,128]{1,0:T(8,128)S(1)}, f32[8,128]{1,0:T(8,128)S(1)}, u32[]{:S(2)}, u32[]{:S(2)}) collective-permute-start(f32[8,128]{1,0:T(8,128)S(1)} %copy-done.11), channel_id=1, source_target_pairs={{0,1},{1,2},{2,3},{3,4},{4,5},{5,6},{6,7},{7,0},{8,9},{9,10},{10,1... | collective-permute-start | bytes 12296 | tf_op jit(solution)/shard_map/ppermute | solution.py:610
  29.2 0.6 pad_add_fusion.scalars
  30.5 1.2 %collective-permute-done.1.from_right = f32[8,128]{1,0:T(8,128)S(1)} collective-permute-done((f32[8,128]{1,0:T(8,128)S(1)}, f32[8,128]{1,0:T(8,128)S(1)}, u32[]{:S(2)}, u32[]{:S(2)}) %collective-permute-start.1) | collective-permute-done | bytes 4128 | tf_op jit(solution)/shard_map/ppermute | solution.py:611
  31.7 5.7 %collective-permute-done.from_left = f32[8,128]{1,0:T(8,128)S(1)} collective-permute-done((f32[8,128]{1,0:T(8,128)S(1)}, f32[8,128]{1,0:T(8,128)S(1)}, u32[]{:S(2)}, u32[]{:S(2)}) %collective-permute-start) | collective-permute-done | bytes 4128 | tf_op jit(solution)/shard_map/ppermute | solution.py:610
  37.4 0.6 copy-done.4
  38.0 0.2 copy-done
  38.2 7.6 %energy_slopes.1 = (f32[8,4,128]{2,1,0:T(4,128)}, f32[8,256]{1,0:T(8,128)}, f32[128,128]{1,0:T(8,128)}, f32[128,128]{1,0:T(8,128)}, f32[128,128]{1,0:T(8,128)}, ...) custom-call(s32[1,1]{1,0:T(1,128)S(6)} %copy.36.count_ref, ...), custom_call_target="tpu_custom_call" | custom-call | tf_op jit(solution)/shard_map/energy_slopes/pallas_call | solution.py:527
  45.8 6.5 %all-to-all-start.1 = ((f32[8,4,128]{2,1,0:T(4,128)}), f32[8,4,128]{2,1,0:T(4,128)S(1)}, u32[]{:S(2)}, u32[]{:S(2)}) async-start(f32[8,4,128]{2,1,0:T(4,128)} %get-tuple-element.30), calls=%async_computation.1 | async-start | bytes 32768 | tf_op jit(solution)/shard_map/all_to_all | solution.py:615
  53.0 0.6 copy.27.stress_ref
  53.6 7.7 %all-to-all-done.1.received = f32[8,4,128]{2,1,0:T(4,128)S(1)} async-done(((f32[8,4,128]{2,1,0:T(4,128)}), f32[8,4,128]{2,1,0:T(4,128)S(1)}, u32[]{:S(2)}, u32[]{:S(2)}) %all-to-all-start.1) | async-done | bytes 16416 | tf_op jit(solution)/shard_map/all_to_all | solution.py:615
  61.3 0.6 copy-done.1
  61.9 9.5 %weight_gradients.1 = (f32[8,128]{1,0:T(8,128)}, f32[8,128]{1,0:T(8,128)}, f32[32,16,128]{2,1,0:T(8,128)}, f32[32,16,128]{2,1,0:T(8,128)}) custom-call(s32[1,1]{1,0:T(1,128)S(6)} %copy.36.count_ref, s32[2]{0:T(128)} %pad_add_fusion.scalars, f32[1]{0:T(128)S(6)} %copy.37.energy_ref, f32[1,3,3]{2,1,0:T(4,128)} %copy.27.stress_ref, f32[64,16,128]{2,1,0:T(8,128)} %copy-done, ...), custom_call_target="tpu_custom_call" | custom-call | tf_op jit(solution)/shard_map/weight_gradients/pallas_call | solution.py:547
  71.4 3.8 %collective-permute-start.2 = (f32[32,16,128]{2,1,0:T(8,128)}, f32[32,16,128]{2,1,0:T(8,128)S(1)}, u32[]{:S(2)}, u32[]{:S(2)}) collective-permute-start(f32[32,16,128]{2,1,0:T(8,128)} %get-tuple-element.43), channel_id=1, source_target_pairs={{0,8},{8,0},{16,24},{24,16},{32,40},{40,32},{48,56},{56,48},{64,72... | collective-permute-start | bytes 786440 | tf_op jit(solution)/shard_map/ppermute | solution.py:620
  75.2 1.4 %collective-permute-done.2 = f32[32,16,128]{2,1,0:T(8,128)S(1)} collective-permute-done((f32[32,16,128]{2,1,0:T(8,128)}, f32[32,16,128]{2,1,0:T(8,128)S(1)}, u32[]{:S(2)}, u32[]{:S(2)}) %collective-permute-start.2) | collective-permute-done | bytes 262176 | tf_op jit(solution)/shard_map/ppermute | solution.py:620
  76.5 1.7 %add.23 = f32[32,16,128]{2,1,0:T(8,128)} add(f32[32,16,128]{2,1,0:T(8,128)} %get-tuple-element.42, f32[32,16,128]{2,1,0:T(8,128)S(1)} %collective-permute-done.2) | non-fusion elementwise | flops 65536 | bytes 786432 | tf_op jit(solution)/shard_map/add | solution.py:620
  78.2 7.7 %all-to-all-start.2 = ((f32[32,16,128]{2,1,0:T(8,128)}), f32[32,16,128]{2,1,0:T(8,128)S(1)}, u32[]{:S(2)}, u32[]{:S(2)}) async-start(f32[32,16,128]{2,1,0:T(8,128)} %add.23), calls=%async_computation.2 | async-start | bytes 524288 | tf_op jit(solution)/shard_map/all_to_all | solution.py:623
  85.9 1.3 %slice.34 = f32[1,1]{1,0:T(1,128)} slice(f32[8,128]{1,0:T(8,128)} %get-tuple-element.45), slice={[3:4], [9:10]} | slice | bytes 8 | tf_op jit(solution)/shard_map/slice | solution.py:633
  87.2 0.7 multiply_reduce_fusion
  87.9 0.6 div.27
  88.5 8.4 %all-to-all-done.2 = f32[32,16,128]{2,1,0:T(8,128)S(1)} async-done(((f32[32,16,128]{2,1,0:T(8,128)}), f32[32,16,128]{2,1,0:T(8,128)S(1)}, u32[]{:S(2)}, u32[]{:S(2)}) %all-to-all-start.2) | async-done | bytes 262176 | tf_op jit(solution)/shard_map/all_to_all | solution.py:623
  97.0 0.6 broadcast_in_dim.13
  97.6 3.5 %all-to-all-start.3 = ((f32[8,16,128]{2,1,0:T(8,128)}), f32[8,16,128]{2,1,0:T(8,128)S(1)}, u32[]{:S(2)}, u32[]{:S(2)}) async-start(f32[8,16,128]{2,1,0:T(8,128)} %broadcast_in_dim.13), calls=%async_computation.3 | async-start | bytes 131072 | tf_op jit(solution)/shard_map/all_to_all | solution.py:626
  101.1 0.6 copy.30
  101.7 8.4 %all-to-all-done.3 = f32[8,16,128]{2,1,0:T(8,128)S(1)} async-done(((f32[8,16,128]{2,1,0:T(8,128)}), f32[8,16,128]{2,1,0:T(8,128)S(1)}, u32[]{:S(2)}, u32[]{:S(2)}) %all-to-all-start.3) | async-done | bytes 65568 | tf_op jit(solution)/shard_map/all_to_all | solution.py:626
  111.0 0.4 copy-done.6
  111.4 0.2 copy-done.2
  111.6 0.6 multiply_subtract_fusion
  (35 shorter events, 0.9 us)
Async XLA Ops:
  0.6 1.3 %copy-start.7 = (f32[1,1,3,128]{3,1,2,0:T(1,128)S(1)}, f32[1,1,3,128]{3,1,2,0:T(1,128)}, u32[]{:S(2)}) copy-start(f32[1,1,3,128]{3,1,2,0:T(1,128)} %param.21) | copy-start | bytes 4612
  0.6 1.3 %copy-start.8 = (f32[1,1,3,128]{3,1,2,0:T(1,128)S(1)}, f32[1,1,3,128]{3,1,2,0:T(1,128)}, u32[]{:S(2)}) copy-start(f32[1,1,3,128]{3,1,2,0:T(1,128)} %param.13) | copy-start | bytes 4612
  4.5 15.6 %copy-start.11 = (f32[8,128]{1,0:T(8,128)S(1)}, f32[8,128]{1,0:T(8,128)}, u32[]{:S(2)}) copy-start(f32[8,128]{1,0:T(8,128)} %get-tuple-element.28) | copy-start | bytes 12292
  4.5 32.9 %all-to-all-start = ((f32[64,16,128]{2,1,0:T(8,128)}), f32[64,16,128]{2,1,0:T(8,128)S(1)}, u32[]{:S(2)}, u32[]{:S(2)}) async-start(f32[64,16,128]{2,1,0:T(8,128)} %get-tuple-element.26), calls=%async_computation | async-start | bytes 1048576 | tf_op jit(solution)/shard_map/all_to_all | solution.py:609
  20.0 11.7 %collective-permute-start.1 = (f32[8,128]{1,0:T(8,128)S(1)}, f32[8,128]{1,0:T(8,128)S(1)}, u32[]{:S(2)}, u32[]{:S(2)}) collective-permute-start(f32[8,128]{1,0:T(8,128)S(1)} %copy-done.11), channel_id=1, source_target_pairs={{1,0},{2,1},{3,2},{4,3},{5,4},{6,5},{7,6},{0,7},{9,8},{10,9},{11,1... | collective-permute-start | bytes 12296 | tf_op jit(solution)/shard_map/ppermute | solution.py:611
  27.0 10.4 %collective-permute-start = (f32[8,128]{1,0:T(8,128)S(1)}, f32[8,128]{1,0:T(8,128)S(1)}, u32[]{:S(2)}, u32[]{:S(2)}) collective-permute-start(f32[8,128]{1,0:T(8,128)S(1)} %copy-done.11), channel_id=1, source_target_pairs={{0,1},{1,2},{2,3},{3,4},{4,5},{5,6},{6,7},{7,0},{8,9},{9,10},{10,1... | collective-permute-start | bytes 12296 | tf_op jit(solution)/shard_map/ppermute | solution.py:610
  31.7 5.7 %copy-start.3 = (f32[8,128]{1,0:T(8,128)}, f32[8,128]{1,0:T(8,128)S(1)}, u32[]{:S(2)}) copy-start(f32[8,128]{1,0:T(8,128)S(1)} %collective-permute-done.1.from_right) | copy-start | bytes 12292
  37.4 0.6 copy-start.4
  37.4 0.8 copy-start
  45.8 15.5 %all-to-all-start.1 = ((f32[8,4,128]{2,1,0:T(4,128)}), f32[8,4,128]{2,1,0:T(4,128)S(1)}, u32[]{:S(2)}, u32[]{:S(2)}) async-start(f32[8,4,128]{2,1,0:T(4,128)} %get-tuple-element.30), calls=%async_computation.1 | async-start | bytes 32768 | tf_op jit(solution)/shard_map/all_to_all | solution.py:615
  52.3 0.7 copy-start.9
  61.3 0.6 copy-start.1
  71.4 5.1 %collective-permute-start.2 = (f32[32,16,128]{2,1,0:T(8,128)}, f32[32,16,128]{2,1,0:T(8,128)S(1)}, u32[]{:S(2)}, u32[]{:S(2)}) collective-permute-start(f32[32,16,128]{2,1,0:T(8,128)} %get-tuple-element.43), channel_id=1, source_target_pairs={{0,8},{8,0},{16,24},{24,16},{32,40},{40,32},{48,56},{56,48},{64,72... | collective-permute-start | bytes 786440 | tf_op jit(solution)/shard_map/ppermute | solution.py:620
  78.2 18.7 %all-to-all-start.2 = ((f32[32,16,128]{2,1,0:T(8,128)}), f32[32,16,128]{2,1,0:T(8,128)S(1)}, u32[]{:S(2)}, u32[]{:S(2)}) async-start(f32[32,16,128]{2,1,0:T(8,128)} %add.23), calls=%async_computation.2 | async-start | bytes 524288 | tf_op jit(solution)/shard_map/all_to_all | solution.py:623
  97.6 3.5 %copy-start.10 = (f32[8,128]{1,0:T(8,128)S(1)}, f32[8,128]{1,0:T(8,128)}, u32[]{:S(2)}) copy-start(f32[8,128]{1,0:T(8,128)} %get-tuple-element.44) | copy-start | bytes 12292
  97.6 12.5 %all-to-all-start.3 = ((f32[8,16,128]{2,1,0:T(8,128)}), f32[8,16,128]{2,1,0:T(8,128)S(1)}, u32[]{:S(2)}, u32[]{:S(2)}) async-start(f32[8,16,128]{2,1,0:T(8,128)} %broadcast_in_dim.13), calls=%async_computation.3 | async-start | bytes 131072 | tf_op jit(solution)/shard_map/all_to_all | solution.py:626
  110.7 0.7 copy-start.6
  110.9 0.7 copy-start.2
  110.9 0.7 copy-start.5

commit v3 on v2

--- a/solution.py
+++ b/solution.py
@@ -19,7 +19,10 @@
 EC = 1024
 CHUNKS = E // EC
 BLOCKS = 16
-KEPT = [8, 8, C, C, C]
+HIDDEN, DN, DH, EMB_OWN, EMB_GHOST = (slice(C * i, C * i + C) for i in range(5))
+Z = slice(5 * C, 5 * C + FF)
+OWN, GHOST, CONTRIB_OWN, CONTRIB_GHOST = (slice(9 * C + 8 * i, 9 * C + 8 * i + 8) for i in range(4))
+KEPT = [(9 * C + 32, A), (8, E), (8, E), (C, E), (C, E)]
 
 highest = lax.Precision.HIGHEST
 cutoff = 6.0
@@ -96,8 +99,17 @@
     return lax.broadcasted_iota(jnp.int32, shape, dim)
 
 
-def select_lists(lists):
+def select_lists(send_left, send_right):
+    lists = jnp.concatenate(
+        [send_right[...], send_left[...], jnp.full((1, 128 - 2 * G), -1, jnp.int32)], axis=1
+    )
     return (iota((A, 128), 0) == lists).astype(f32)
+
+
+def pack_own(positions, species, force_ref):
+    rows = [positions[i] for i in range(3)] + [species[...].astype(f32)]
+    rows = rows + [force_ref[i] for i in range(3)] + [jnp.zeros((1, A), f32)]
+    return jnp.concatenate(rows, axis=0)
 
 
 def place(pieces, stride, offset, first, last):
@@ -119,15 +131,10 @@
     )
 
 
-def prepare_kernel(positions, species, force_ref, send_left, send_right, shard, own, lists, outgoing, blocks):
-    own[...] = jnp.concatenate(
-        [positions[...], species[...].astype(f32), force_ref[...], jnp.zeros((1, A), f32)], axis=0
-    )
-    lists[...] = jnp.concatenate(
-        [send_right[...], send_left[...], jnp.full((1, 128 - 2 * G), -1, jnp.int32)], axis=1
-    )
-    outgoing[...] = full_dot(own[...], select_lists(lists[...]), NN)
-    x = shard[...]
+def prepare_kernel(positions, species, force_ref, send_left, send_right, shard, outgoing, blocks):
+    own = pack_own(positions, species, force_ref)
+    outgoing[...] = full_dot(own, select_lists(send_left, send_right), NN)
+    x = shard[...].reshape(1, 1920)
     one = x.astype(bf16).astype(f32)
     two = (x - one).astype(bf16).astype(f32)
     pieces = [one, two, x - one - two]
@@ -185,14 +192,10 @@
 
 
 def forward_kernel(
-    slabs, count_ref, scalars, wg, own, from_left, from_right, src, dst, lists,
-    message, contrib_out, h_out, dn_out, dh_out, z_out, emb_out, *rest,
+    slabs, count_ref, scalars, wg, positions, species, force_ref, first_ghost, second_ghost, src, dst,
+    send_left, send_right, message, atoms, rows_out, vec_out, dfilt_out, q_out,
+    src_hot, dst_hot, total, force_total,
 ):
-    large = len(KEPT)
-    far, near = rest[:large], rest[large : 2 * large]
-    src_hot, dst_hot, total, force_total, sems = rest[2 * large :]
-    rows_out, vec_out, dfilt_out, q_out, filt_out = near
-    copies = []
 
     count = count_ref[0, 0]
     rank = scalars[0]
@@ -206,10 +209,12 @@
     update = lhs(update_f.T)
     readout = readout_column(wg)
 
-    own_rows = own[...]
+    own_rows = pack_own(positions, species, force_ref)
     lane = iota((8, 128), 1)
     row = iota((8, 128), 0)
-    ghost_rows = jnp.where(lane < G, from_left[...], from_right[...])
+    ghost_rows = jnp.where((lane < G) == (rank % 2 == 1), first_ghost[...], second_ghost[...])
+    atoms[OWN] = own_rows
+    atoms[GHOST] = ghost_rows
     shift = jnp.where(lane < G, jnp.where(rank == 0, -box, 0.0), 0.0)
     shift = shift + jnp.where((lane >= G) & (lane < 2 * G), jnp.where(rank == slabs - 1, box, 0.0), 0.0)
     ghost_pos = ghost_rows + jnp.where(row == 0, shift, 0.0)
@@ -221,7 +226,8 @@
     table_lo = (table_t - table_hi.astype(f32) - table_rest.astype(f32)).astype(bf16)
     kind_bf = kind_hot.astype(bf16)
     emb = mm(table_hi, kind_bf, NN) + mm(table_rest, kind_bf, NN) + mm(table_lo, kind_bf, NN)
-    emb_out[...] = emb
+    atoms[EMB_OWN] = emb[:, :A]
+    atoms[EMB_GHOST] = emb[:, A:]
     projected = stack(wdot(message_t, stack(emb)))[:, :N]
     total[...] = jnp.zeros_like(total)
     centers = iota((K, EC), 0).astype(f32) * (cutoff / (K - 1))
@@ -257,33 +263,28 @@
         filt = f * gate
         dfilt = df * gate + f * dgate
         q = fold_rows(mm(projected, hot_s, NN))
-        filt_out[:, at] = filt
         dfilt_out[:, at] = dfilt
         q_out[:, at] = q
         total[...] += mm(stack(filt * q), hot_t, NT)
-        for k in range(large):
-            copy = pltpu.make_async_copy(near[k].at[:, at], far[k].at[:, at], sems.at[k, i])
-            copy.start()
-            copies.append(copy)
 
     hidden = emb[:, :A] + fold_rows(total[...]) * (1.0 / DEG)
-    h_out[...] = hidden
+    atoms[HIDDEN] = hidden
     rms = lax.rsqrt(jnp.mean(hidden * hidden, axis=0, keepdims=True) + 1e-05)
     z = wdot(update_t, stack(hidden * rms))
-    z_out[...] = z
+    atoms[Z] = z
     sig, slope = silu_parts(z)
     live_atom = (iota((1, A), 1) < count).astype(f32)
     weighted = readout * live_atom
     energy = jnp.sum(jnp.sum(weighted * (z * sig), axis=0, keepdims=True), axis=1, keepdims=True)
     dn = wdot(update, stack(weighted * slope))
-    dn_out[...] = dn
+    atoms[DN] = dn
     cube = rms * rms * rms * (1.0 / C)
     dh = rms * dn - hidden * (cube * jnp.sum(dn * hidden, axis=0, keepdims=True))
-    dh_out[...] = dh
+    atoms[DH] = dh
     dh_pieces = wide(dh * (1.0 / DEG))
     force_total[...] = jnp.zeros_like(force_total)
 
-    stress = jnp.zeros((8, 8), f32)
+    stress = [jnp.zeros((8, 1), f32) for _ in range(3)]
     for i in range(CHUNKS):
         at = pl.ds(i * EC, EC)
         hot_s = src_hot[:, at]
@@ -295,63 +296,60 @@
         three = exact(slopes)
         force_total[:, :N] += mm(three, hot_s, NT)
         force_total[:, :A] -= mm(three, hot_t, NT)
-        stress = stress + full_dot(slopes, vec, NT)
+        stress = [
+            stress[j] + jnp.sum(slopes * vec[j : j + 1], axis=1, keepdims=True) for j in range(3)
+        ]
 
     contrib = whole(force_total[...])
-    contrib_out[...] = contrib
-    lists_hot = select_lists(lists[...])
+    atoms[CONTRIB_OWN] = contrib[:, :A]
+    atoms[CONTRIB_GHOST] = contrib[:, A:]
+    lists_hot = select_lists(send_left, send_right)
     outgoing = full_dot(contrib[:, :A], lists_hot, NN) + pltpu.roll(contrib[:, A:], 64, 1)
     to_right = (lane < G) | (lane >= 96)
     sums = jnp.zeros((8, 128), f32)
     for i in range(3):
         for j in range(3):
-            sums = sums + jnp.where(lane == 3 * i + j, stress[i : i + 1, j : j + 1], 0.0)
+            sums = sums + jnp.where(lane == 3 * i + j, stress[j][i : i + 1], 0.0)
     sums = sums + jnp.where(lane == 9, energy, 0.0)
     right = lax.rem(rank + 1, slabs)
     left = lax.rem(rank + slabs - 1, slabs)
     for d in range(8):
         keep = (to_right & (right == d)) | (jnp.logical_not(to_right) & (left == d))
         message[d] = jnp.where(row == 3, sums, jnp.where(keep, outgoing, 0.0))[:4]
-    for copy in copies:
-        copy.wait()
 
 
 def backward_kernel(
-    slabs, count_ref, scalars, energy_ref, stress_ref, wg, own, from_left, from_right, src, dst, lists, received, contrib_in, h_in, dn_in, dh_in, z_in, emb_in, *rest,
+    slabs, count_ref, scalars, energy_ref, stress_ref, wg, src, dst, send_left, send_right, received, atoms, rows_in, vec_in, dfilt_in, q_in,
+    forces_out, sums_out, keep, give,
+    src_hot, dst_hot, grad, step_row, total, source_total, one_total, two_total,
 ):
-    large = len(KEPT)
-    far, near = rest[:large], rest[large + 4 : 2 * large + 4]
-    forces_out, sums_out, keep, give = rest[large : large + 4]
-    src_hot, dst_hot, grad, step_row, total, source_total, one_total, two_total, sems = rest[2 * large + 4 :]
-    rows_in, vec_in, dfilt_in, q_in, filt_in = near
-    copies = [pltpu.make_async_copy(far[k], near[k], sems.at[k]) for k in range(large)]
-    for copy in copies:
-        copy.start()
 
     count = count_ref[0, 0]
     core = scalars[1]
     volume = slab_width * cross_area * slabs
     scale = 2.0 / (slabs * A)
     one_t = lhs(radial_one_t(wg))
-    two = lhs(weight(wg, 3).T)
+    two_f = weight(wg, 3)
+    two_t = lhs(two_f)
+    two = lhs(two_f.T)
     message_w = lhs(weight(wg, 5).T)
     update_f = update_weight_t(wg)
     update_t = lhs(update_f)
     update = lhs(update_f.T)
     readout = readout_column(wg)
-    lists_hot = select_lists(lists[...])
+    lists_hot = select_lists(send_left, send_right)
     lane = iota((8, 128), 1)
     row = iota((8, 128), 0)
-    ghost = jnp.where(lane < G, from_left[...], from_right[...])
+    own = atoms[OWN]
+    ghost = atoms[GHOST]
 
     got = jnp.sum(received[...], axis=0)
     got = jnp.concatenate([got, jnp.zeros_like(got)], axis=0)
     moved = jnp.where(row < 3, got, 0.0)
     energy = got[3:4, 9:10]
     inner = jnp.where(lane < 2 * G, pltpu.roll(moved, 64, 1), 0.0)
-    contrib = contrib_in[...]
-    force_own = -(contrib[:, :A] + full_dot(inner, lists_hot, NT))
-    force_ghost = -(contrib[:, A:] + jnp.where(lane < 2 * G, moved, 0.0))
+    force_own = -(atoms[CONTRIB_OWN] + full_dot(inner, lists_hot, NT))
+    force_ghost = -(atoms[CONTRIB_GHOST] + jnp.where(lane < 2 * G, moved, 0.0))
     forces_out[...] = force_own
     sums_out[...] = got
     own_ref = jnp.concatenate([own[4:8], jnp.zeros((4, 128), f32)], axis=0)
@@ -362,7 +360,7 @@
     cot = exact(jnp.concatenate([cot_own, cot_ghost], axis=1))
     stress_cot = [
         [
-            (2.0 * stress_weight / volume) * (got[3:4, 3 * i + j : 3 * i + j + 1] / volume - stress_ref[0, i, j])
+            (2.0 * stress_weight / volume) * (got[3:4, 3 * i + j : 3 * i + j + 1] / volume - stress_ref[i, 0, j])
             for j in range(3)
         ]
         for i in range(3)
@@ -370,8 +368,6 @@
     energy_cot = (energy - energy_ref[0]) * scale
     total[...] = jnp.zeros_like(total)
 
-    for copy in copies[:2]:
-        copy.wait()
     for i in range(CHUNKS):
         at = pl.ds(i * EC, EC)
         hot_s, hot_t = one_hots(src[:, at], dst[:, at])
@@ -385,18 +381,12 @@
             along = along + vec[r : r + 1] * inner_row
         step = along * rows_in[1:2, at]
         step_row[:, at] = step
-    for copy in copies[2:4]:
-        copy.wait()
-    for i in range(CHUNKS):
-        at = pl.ds(i * EC, EC)
-        step = step_row[:, at]
-        hot_t = dst_hot[:, at]
         total[...] += mm(stack(dfilt_in[:, at] * q_in[:, at] * step), hot_t, NT)
 
-    hidden = h_in[...]
-    dn = dn_in[...]
-    dh = dh_in[...]
-    z = z_in[...]
+    hidden = atoms[HIDDEN]
+    dn = atoms[DN]
+    dh = atoms[DH]
+    z = atoms[Z]
     moved_h = fold_rows(total[...]) * (1.0 / DEG)
     rms = lax.rsqrt(jnp.mean(hidden * hidden, axis=0, keepdims=True) + 1e-05)
     cube = rms * rms * rms
@@ -441,7 +431,6 @@
     two_total[...] = jnp.zeros_like(two_total)
     centers = iota((K, EC), 0).astype(f32) * (cutoff / (K - 1))
 
-    copies[4].wait()
     for i in range(CHUNKS):
         at = pl.ds(i * EC, EC)
         hot_s = src_hot[:, at]
@@ -453,9 +442,6 @@
         m_bar = both[:C]
         dm_bar = both[C:]
         q = q_in[:, at]
-        source_total[...] += mm(
-            stack(m_bar * filt_in[:, at] + dm_bar * (dfilt_in[:, at] * step)), hot_s, NT
-        )
         dq = dm_bar * q
         f_bar = stack(m_bar * q * gate + dq * (dgate * step))
         df_bar = stack(dq * gate)
@@ -469,7 +455,10 @@
         a = wdot(one_t, basis)
         moved_a = wdot(one_t, moved_basis)
         sig, slope = silu_parts(a)
-        two_total[...] += mm(f_bar, stack(a * sig), NT) + mm(df_bar, stack(slope * moved_a), NT)
+        inner = stack(a * sig)
+        filt = wdot(two_t, inner) * gate
+        source_total[...] += mm(stack(m_bar * filt + dm_bar * (dfilt_in[:, at] * step)), hot_s, NT)
+        two_total[...] += mm(f_bar, inner, NT) + mm(df_bar, stack(slope * moved_a), NT)
         a_bar = stack(s_bar * slope + ds_bar * (silu_second(a, sig) * moved_a))
         da_bar = stack(ds_bar * slope)
         one_total[...] += mm(a_bar, basis, NT) + mm(da_bar, moved_basis, NT)
@@ -482,7 +471,7 @@
     p_bar = fold_rows(source_total[...])
     p_bar = jnp.concatenate([p_bar, jnp.zeros((C, 256 - N), f32)], axis=1)
     p_pieces = stack(p_bar)
-    emb = emb_in[...]
+    emb = jnp.concatenate([atoms[EMB_OWN], atoms[EMB_GHOST]], axis=1)
     message_grad = fold(mm(p_pieces, stack(emb), NT))
     grad[:, 5, :] = message_grad[:64]
     grad[:, 6, :] = message_grad[64:]
@@ -500,9 +489,7 @@
 
 vmem = pl.BlockSpec(memory_space=pltpu.VMEM)
 smem = pl.BlockSpec(memory_space=pltpu.SMEM)
-far = pl.BlockSpec(memory_space=pl.ANY)
-params_vmem = pltpu.CompilerParams(vmem_limit_bytes=56 * 1024 * 1024)
-edge_scratch = [pltpu.VMEM((rows, E), f32) for rows in KEPT]
+params_vmem = pltpu.CompilerParams(vmem_limit_bytes=32 * 1024 * 1024)
 
 
 def shape(*dims, dtype=jnp.float32):
@@ -512,45 +499,39 @@
 def prepare(positions, species, force_ref, send_left, send_right, shard, shards):
     return pl.pallas_call(
         prepare_kernel,
-        out_shape=[shape(8, 128), shape(1, 128, dtype=jnp.int32), shape(8, 128), shape(shards, BLOCKS, 128)],
+        out_shape=[shape(8, 128), shape(shards, BLOCKS, 128)],
         in_specs=[vmem] * 6,
-        out_specs=[vmem] * 4,
+        out_specs=[vmem] * 2,
         compiler_params=params_vmem,
         name="prepare",
     )(positions, species, force_ref, send_left, send_right, shard)
 
 
-def forward(slabs, counts, scalars, wg, own, from_left, from_right, src, dst, lists):
-    outs = [
-        shape(8, 4, 128), shape(8, 256), shape(C, A), shape(C, A), shape(C, A), shape(FF, A), shape(C, 256),
-    ]
+def forward(slabs, counts, scalars, wg, *arrays):
     return pl.pallas_call(
         functools.partial(forward_kernel, slabs),
-        out_shape=outs + [shape(rows, E) for rows in KEPT],
-        in_specs=[smem] * 2 + [vmem] * 7,
-        out_specs=[vmem] * len(outs) + [far] * len(KEPT),
-        scratch_shapes=edge_scratch
-        + [
+        out_shape=[shape(8, 4, 128)] + [shape(*dims) for dims in KEPT],
+        in_specs=[smem] * 2 + [vmem] * (1 + len(arrays)),
+        out_specs=[vmem] * (1 + len(KEPT)),
+        scratch_shapes=[
             pltpu.VMEM((N, E), bf16),
             pltpu.VMEM((A, E), bf16),
             pltpu.VMEM((2 * C, A), f32),
             pltpu.VMEM((24, 256), f32),
-            pltpu.SemaphoreType.DMA((len(KEPT), CHUNKS)),
         ],
         compiler_params=params_vmem,
         name="energy_slopes",
-    )(counts, scalars, wg, own, from_left, from_right, src, dst, lists)
-
-
-def backward(slabs, counts, scalars, energy_ref, stress_ref, wg, own, from_left, from_right, src, dst, lists, received, kept):
+    )(counts, scalars, wg, *arrays)
+
+
+def backward(slabs, counts, scalars, energy_ref, stress_ref, *arrays):
     outs = [shape(8, 128), shape(8, 128), shape(32, BLOCKS, 128), shape(32, BLOCKS, 128)]
     return pl.pallas_call(
         functools.partial(backward_kernel, slabs),
         out_shape=outs,
-        in_specs=[smem] * 4 + [vmem] * (8 + len(kept) - len(KEPT)) + [far] * len(KEPT),
+        in_specs=[smem] * 4 + [vmem] * len(arrays),
         out_specs=[vmem] * 4,
-        scratch_shapes=edge_scratch
-        + [
+        scratch_shapes=[
             pltpu.VMEM((N, E), bf16),
             pltpu.VMEM((A, E), bf16),
             pltpu.VMEM((64, BLOCKS, 128), f32),
@@ -559,11 +540,10 @@
             pltpu.VMEM((2 * C, N), f32),
             pltpu.VMEM((2 * C, 2 * K), f32),
             pltpu.VMEM((2 * C, 2 * C), f32),
-            pltpu.SemaphoreType.DMA((len(KEPT),)),
         ],
         compiler_params=params_vmem,
         name="weight_gradients",
-    )(counts, scalars, energy_ref, stress_ref, wg, own, from_left, from_right, src, dst, lists, received, *kept)
+    )(counts, scalars, energy_ref, stress_ref, *arrays)
 
 
 def from_blocks(y):
@@ -603,18 +583,20 @@
     index = lax.axis_index("dp")
     core = index % 2
     scalars = jnp.stack([rank, core]).astype(jnp.int32)
-    own, lists, outgoing, blocks = prepare(
-        positions[0, 0], species[0], force_ref[0, 0], send_left[0], send_right[0], params[None], shards
-    )
+    atoms = (positions.reshape(3, 1, A), species[0], force_ref.reshape(3, 1, A))
+    lists = (send_left[0], send_right[0])
+    outgoing, blocks = prepare(*atoms, *lists, params, shards)
     wg = lax.all_to_all(blocks, "dp", 0, 0, tiled=True)
-    from_left = lax.ppermute(outgoing, "graph", [(i, (i + 1) % slabs) for i in range(slabs)])
-    from_right = lax.ppermute(outgoing, "graph", [((i + 1) % slabs, i) for i in range(slabs)])
+    first = lax.ppermute(outgoing, "graph", [(i, i ^ 1) for i in range(slabs)])
+    second = lax.ppermute(
+        outgoing, "graph", [(i, (i + (1 if i % 2 else slabs - 1)) % slabs) for i in range(slabs)]
+    )
     message, *kept = forward(
-        slabs, counts, scalars, wg, own, from_left, from_right, source[0], target[0], lists
+        slabs, counts, scalars, wg, *atoms, first, second, source[0], target[0], *lists
     )
     received = lax.all_to_all(message, "graph", 0, 0, tiled=True)
     forces, sums, keep, give = backward(
-        slabs, counts, scalars, energy_ref, stress_ref, wg, own, from_left, from_right, source[0], target[0], lists, received, kept
+        slabs, counts, scalars, energy_ref, stress_ref.reshape(3, 1, 3), wg, source[0], target[0], *lists, received, *kept
     )
     volume = slabs * slab_width * cross_area
     pair = keep + lax.ppermute(give, "dp", [(i, i ^ 1) for i in range(shards)])

time: 114 us -> 108 us (0.947)
  Pallas kernels: 19 us -> 14 us
  other arithmetic: 3.7 us -> 1.58 us
  waiting for transfers between devices: 32.8 us -> 34.1 us
    ppermute x2, waiting for transfers between devices: 6.91 us -> 4.3 us  [the longest x1 2.98 us: body(): lax.ppermute(outgoing, 'graph', [(i, (i + (1 if i % 2 else slabs - 1)) %...]
    pallas_call x2, Pallas kernels: 9.51 us -> 6.91 us  [the longest x1 5.74 us: forward(): pl.pallas_call(functools.partial(forward_kernel, slabs), out_shape=[shape...]
    pallas_call x1, Pallas kernels: 9.47 us -> 7.13 us  [backward(): pl.pallas_call(functools.partial(backward_kernel, slabs), out_shape=outs,...]
    all_to_all x1, waiting for transfers between devices: 0.01 us -> 2.1 us  [body(): wg = lax.all_to_all(blocks, 'dp', 0, 0, tiled=True)]
    unnamed x27 -> x29, local copies, waits for them, and re-layouts: 3.78 us -> 5.22 us
    all_to_all x1, waiting for transfers between devices: 8.42 us -> 9.78 us  [body(): lax.all_to_all(pair, 'dp', 0, 0, tiled=True, axis_index_groups=chips)]
    broadcast_in_dim x1 -> x0, local copies, waits for them, and re-layouts: 1.31 us -> none  [body(): params[None]]
  transfers between devices with their start and end apart: 7 -> 7, of which waited for: 6 -> 7; matrix products, arithmetic and copies ran while one was open for 4% -> 2% of each run, Pallas kernels for 0% -> 0%
where the time goes in v3:
time: 108 us; the launch traced here: 106 us
  starting transfers between devices  46.5 us (43%)
  waiting for transfers between devices  34.1 us (32%)
  Pallas kernels  14 us (13%)
  local copies, waits for them, and re-layouts  7.77 us (7%)
  between operations  2.16 us (2%)
  other arithmetic  1.58 us (1%)
    all_to_all x1, starting transfers between devices, body(): wg = lax.all_to_all(blocks, 'dp', 0, 0, tiled=True)  15.4 us
    all_to_all x1, waiting for transfers between devices, body(): lax.all_to_all(pair, 'dp', 0, 0, tiled=True, axis_index_groups=chips)  9.78 us
    all_to_all x1, waiting for transfers between devices, body(): lax.all_to_all(copies, 'graph', 0, 0, tiled=True)  8.45 us
    all_to_all x1, waiting for transfers between devices, body(): received = lax.all_to_all(message, 'graph', 0, 0, tiled=True)  8.32 us
    all_to_all x1, starting transfers between devices, body(): lax.all_to_all(pair, 'dp', 0, 0, tiled=True, axis_index_groups=chips)  7.28 us
    pallas_call x1, Pallas kernels, backward(): pl.pallas_call(functools.partial(backward_kernel, slabs), out_shape=outs,...  7.13 us
    ppermute x1, starting transfers between devices, body(): lax.ppermute(outgoing, 'graph', [(i, (i + (1 if i % 2 else slabs - 1)) %...  6.95 us
    all_to_all x1, starting transfers between devices, body(): received = lax.all_to_all(message, 'graph', 0, 0, tiled=True)  6.6 us
  transfers between devices with their start and end apart: 7, of which 7 were waited for; matrix products, arithmetic and copies ran while one was open for 2% of the time, Pallas kernels for 0%

profile of v3, /device:TPU:1, one launch (start us, length us, event | category | flops | bytes accessed | tf_op | source)
XLA Modules:
  0.0 106.2 jit_solution(11163321471183606767)
XLA Ops:
  0.7 0.7 copy-done.2
  1.3 0.7 copy-done.3
  2.0 0.7 copy-done.5
  2.7 0.7 copy-done.9
  3.4 1.2 %prepare.1 = (f32[8,128]{1,0:T(8,128)S(1)}, f32[64,16,128]{2,1,0:T(8,128)}) custom-call(f32[3,1,128]{2,1,0:T(1,128)S(1)} %bitcast.23, s32[1,128]{1,0:T(1,128)S(1)} %bitcast.33, f32[3,1,128]{2,1,0:T(1,128)S(1)} %bitcast.25, s32[1,32]{1,0:T(1,128)S(1)} %bitcast.27, s32[1,32]{1,0:T(1,128)S(1)} %bitcast.30, f32[1920]{0:T(1024)S(1)} %copy-done.2), custom_call_target="tpu_custom_call" | custom-call | tf_op jit(solution)/shard_map/prepare/pallas_call | solution.py:500
  4.5 15.4 %all-to-all-start = ((f32[64,16,128]{2,1,0:T(8,128)}), f32[64,16,128]{2,1,0:T(8,128)S(1)}, u32[]{:S(2)}, u32[]{:S(2)}) async-start(f32[64,16,128]{2,1,0:T(8,128)} %get-tuple-element.18), calls=%async_computation | async-start | bytes 1048576 | tf_op jit(solution)/shard_map/all_to_all | solution.py:589
  20.0 7.0 %collective-permute-start.1 = (f32[8,128]{1,0:T(8,128)S(1)}, f32[8,128]{1,0:T(8,128)S(1)}, u32[]{:S(2)}, u32[]{:S(2)}) collective-permute-start(f32[8,128]{1,0:T(8,128)S(1)} %get-tuple-element.19), channel_id=1, source_target_pairs={{0,7},{1,2},{2,1},{3,4},{4,3},{5,6},{6,5},{7,0},{8,15},{9,10},{10,... | collective-permute-start | bytes 12296 | tf_op jit(solution)/shard_map/ppermute | solution.py:591
  26.9 3.2 %collective-permute-start = (f32[8,128]{1,0:T(8,128)S(1)}, f32[8,128]{1,0:T(8,128)S(1)}, u32[]{:S(2)}, u32[]{:S(2)}) collective-permute-start(f32[8,128]{1,0:T(8,128)S(1)} %get-tuple-element.19), channel_id=1, source_target_pairs={{0,1},{1,0},{2,3},{3,2},{4,5},{5,4},{6,7},{7,6},{8,9},{9,8},{10,11... | collective-permute-start | bytes 12296 | tf_op jit(solution)/shard_map/ppermute | solution.py:590
  30.9 3.0 %collective-permute-done.1.second_ghost = f32[8,128]{1,0:T(8,128)S(1)} collective-permute-done((f32[8,128]{1,0:T(8,128)S(1)}, f32[8,128]{1,0:T(8,128)S(1)}, u32[]{:S(2)}, u32[]{:S(2)}) %collective-permute-start.1) | collective-permute-done | bytes 4128 | tf_op jit(solution)/shard_map/ppermute | solution.py:591
  33.9 1.3 %collective-permute-done.first_ghost = f32[8,128]{1,0:T(8,128)S(1)} collective-permute-done((f32[8,128]{1,0:T(8,128)S(1)}, f32[8,128]{1,0:T(8,128)S(1)}, u32[]{:S(2)}, u32[]{:S(2)}) %collective-permute-start) | collective-permute-done | bytes 4128 | tf_op jit(solution)/shard_map/ppermute | solution.py:590
  35.2 2.1 %all-to-all-done.wg = f32[64,16,128]{2,1,0:T(8,128)S(1)} async-done(((f32[64,16,128]{2,1,0:T(8,128)}), f32[64,16,128]{2,1,0:T(8,128)S(1)}, u32[]{:S(2)}, u32[]{:S(2)}) %all-to-all-start) | async-done | bytes 524320 | tf_op jit(solution)/shard_map/all_to_all | solution.py:589
  37.3 0.6 copy-done.10
  37.9 5.7 %energy_slopes.1 = (f32[8,4,128]{2,1,0:T(4,128)}, f32[1184,128]{1,0:T(8,128)S(1)}, f32[8,2048]{1,0:T(8,128)S(1)}, f32[8,2048]{1,0:T(8,128)S(1)}, f32[128,2048]{1,0:T(8,128)S(1)}, /*index=5*/f32[128,2048]{1,0:T(8,128)S(1)}) custom-call(s32[1,1]{1,0:T(1,128)S(6)} %copy.29.count_ref, s32[2]{0:T(128)S(1)} %pad_add_fusion.scalars, ...), custom_call_target="tpu_custom_call" | custom-call | tf_op jit(solution)/shard_map/energy_slopes/pallas_call | solution.py:511
  43.7 6.6 %all-to-all-start.1 = ((f32[8,4,128]{2,1,0:T(4,128)}), f32[8,4,128]{2,1,0:T(4,128)S(1)}, u32[]{:S(2)}, u32[]{:S(2)}) async-start(f32[8,4,128]{2,1,0:T(4,128)} %get-tuple-element.20), calls=%async_computation.1 | async-start | bytes 32768 | tf_op jit(solution)/shard_map/all_to_all | solution.py:597
  50.9 8.3 %all-to-all-done.1.received = f32[8,4,128]{2,1,0:T(4,128)S(1)} async-done(((f32[8,4,128]{2,1,0:T(4,128)}), f32[8,4,128]{2,1,0:T(4,128)S(1)}, u32[]{:S(2)}, u32[]{:S(2)}) %all-to-all-start.1) | async-done | bytes 16416 | tf_op jit(solution)/shard_map/all_to_all | solution.py:597
  59.2 0.7 copy-done.11
  59.9 7.1 %weight_gradients.1 = (f32[8,128]{1,0:T(8,128)S(1)}, f32[8,128]{1,0:T(8,128)S(1)}, f32[32,16,128]{2,1,0:T(8,128)S(1)}, f32[32,16,128]{2,1,0:T(8,128)S(1)}) custom-call(s32[1,1]{1,0:T(1,128)S(6)} %copy.29.count_ref, s32[2]{0:T(128)S(1)} %pad_add_fusion.scalars, f32[1]{0:T(128)S(6)} %copy.30.energy_ref, f32[3,1,3]{2,1,0:T(1,128)S(1)} %bitcast.35, ...), custom_call_target="tpu_custom_call" | custom-call | tf_op jit(solution)/shard_map/weight_gradients/pallas_call | solution.py:529
  67.1 3.8 %collective-permute-start.2 = (f32[32,16,128]{2,1,0:T(8,128)S(1)}, f32[32,16,128]{2,1,0:T(8,128)S(1)}, u32[]{:S(2)}, u32[]{:S(2)}) collective-permute-start(f32[32,16,128]{2,1,0:T(8,128)S(1)} %get-tuple-element.27), channel_id=1, source_target_pairs={{0,8},{8,0},{16,24},{24,16},{32,40},{40,32},{48,56},{56,48},{64,72... | collective-permute-start | bytes 786440 | tf_op jit(solution)/shard_map/ppermute | solution.py:602
  70.8 1.1 %collective-permute-done.2 = f32[32,16,128]{2,1,0:T(8,128)S(1)} collective-permute-done((f32[32,16,128]{2,1,0:T(8,128)S(1)}, f32[32,16,128]{2,1,0:T(8,128)S(1)}, u32[]{:S(2)}, u32[]{:S(2)}) %collective-permute-start.2) | collective-permute-done | bytes 262176 | tf_op jit(solution)/shard_map/ppermute | solution.py:602
  72.0 0.7 add.23
  72.7 7.3 %all-to-all-start.2 = ((f32[32,16,128]{2,1,0:T(8,128)}), f32[32,16,128]{2,1,0:T(8,128)S(1)}, u32[]{:S(2)}, u32[]{:S(2)}) async-start(f32[32,16,128]{2,1,0:T(8,128)} %add.23), calls=%async_computation.2 | async-start | bytes 524288 | tf_op jit(solution)/shard_map/all_to_all | solution.py:605
  80.0 0.6 slice.34
  80.6 0.6 div.27
  81.3 9.8 %all-to-all-done.2 = f32[32,16,128]{2,1,0:T(8,128)S(1)} async-done(((f32[32,16,128]{2,1,0:T(8,128)}), f32[32,16,128]{2,1,0:T(8,128)S(1)}, u32[]{:S(2)}, u32[]{:S(2)}) %all-to-all-start.2) | async-done | bytes 262176 | tf_op jit(solution)/shard_map/all_to_all | solution.py:605
  91.1 0.6 broadcast_in_dim.4
  91.7 3.3 %all-to-all-start.3 = ((f32[8,16,128]{2,1,0:T(8,128)}), f32[8,16,128]{2,1,0:T(8,128)S(1)}, u32[]{:S(2)}, u32[]{:S(2)}) async-start(f32[8,16,128]{2,1,0:T(8,128)} %broadcast_in_dim.4), calls=%async_computation.3 | async-start | bytes 131072 | tf_op jit(solution)/shard_map/all_to_all | solution.py:608
  95.1 0.6 copy.27
  95.7 8.5 %all-to-all-done.3 = f32[8,16,128]{2,1,0:T(8,128)S(1)} async-done(((f32[8,16,128]{2,1,0:T(8,128)}), f32[8,16,128]{2,1,0:T(8,128)S(1)}, u32[]{:S(2)}, u32[]{:S(2)}) %all-to-all-start.3) | async-done | bytes 65568 | tf_op jit(solution)/shard_map/all_to_all | solution.py:608
  104.5 0.1 copy.25
  104.7 0.2 reshape.44
  104.9 0.6 copy-done.12
  105.6 0.6 multiply_subtract_fusion
  (36 shorter events, 0.7 us)
Async XLA Ops:
  0.6 0.7 copy-start.2
  0.6 0.7 copy-start.7
  0.7 0.7 copy-start.8
  1.3 0.7 copy-start.3
  2.0 0.7 copy-start.5
  2.7 0.7 copy-start.9
  4.5 32.7 %all-to-all-start = ((f32[64,16,128]{2,1,0:T(8,128)}), f32[64,16,128]{2,1,0:T(8,128)S(1)}, u32[]{:S(2)}, u32[]{:S(2)}) async-start(f32[64,16,128]{2,1,0:T(8,128)} %get-tuple-element.18), calls=%async_computation | async-start | bytes 1048576 | tf_op jit(solution)/shard_map/all_to_all | solution.py:589
  20.0 13.9 %collective-permute-start.1 = (f32[8,128]{1,0:T(8,128)S(1)}, f32[8,128]{1,0:T(8,128)S(1)}, u32[]{:S(2)}, u32[]{:S(2)}) collective-permute-start(f32[8,128]{1,0:T(8,128)S(1)} %get-tuple-element.19), channel_id=1, source_target_pairs={{0,7},{1,2},{2,1},{3,4},{4,3},{5,6},{6,5},{7,0},{8,15},{9,10},{10,... | collective-permute-start | bytes 12296 | tf_op jit(solution)/shard_map/ppermute | solution.py:591
  26.9 8.3 %collective-permute-start = (f32[8,128]{1,0:T(8,128)S(1)}, f32[8,128]{1,0:T(8,128)S(1)}, u32[]{:S(2)}, u32[]{:S(2)}) collective-permute-start(f32[8,128]{1,0:T(8,128)S(1)} %get-tuple-element.19), channel_id=1, source_target_pairs={{0,1},{1,0},{2,3},{3,2},{4,5},{5,4},{6,7},{7,6},{8,9},{9,8},{10,11... | collective-permute-start | bytes 12296 | tf_op jit(solution)/shard_map/ppermute | solution.py:590
  30.1 7.2 %copy-start.4 = (f32[1,1,3,128]{3,1,2,0:T(1,128)S(1)}, f32[1,1,3,128]{3,1,2,0:T(1,128)}, u32[]{:S(2)}) copy-start(f32[1,1,3,128]{3,1,2,0:T(1,128)} %param.13) | copy-start | bytes 4612
  30.1 7.2 %copy-start.6 = (f32[1,1,3,128]{3,1,2,0:T(1,128)S(1)}, f32[1,1,3,128]{3,1,2,0:T(1,128)}, u32[]{:S(2)}) copy-start(f32[1,1,3,128]{3,1,2,0:T(1,128)} %param.21) | copy-start | bytes 4612
  30.1 7.2 %copy-start.1 = (s32[1,1,2048]{2,1,0:T(1,128)S(1)}, s32[1,1,2048]{2,1,0:T(1,128)}, u32[]{:S(2)}) copy-start(s32[1,1,2048]{2,1,0:T(1,128)} %param.17) | copy-start | bytes 24580
  30.1 7.2 %copy-start = (s32[1,1,2048]{2,1,0:T(1,128)S(1)}, s32[1,1,2048]{2,1,0:T(1,128)}, u32[]{:S(2)}) copy-start(s32[1,1,2048]{2,1,0:T(1,128)} %param.16) | copy-start | bytes 24580
  37.3 0.7 copy-start.10
  43.7 15.6 %all-to-all-start.1 = ((f32[8,4,128]{2,1,0:T(4,128)}), f32[8,4,128]{2,1,0:T(4,128)S(1)}, u32[]{:S(2)}, u32[]{:S(2)}) async-start(f32[8,4,128]{2,1,0:T(4,128)} %get-tuple-element.20), calls=%async_computation.1 | async-start | bytes 32768 | tf_op jit(solution)/shard_map/all_to_all | solution.py:597
  59.2 0.7 copy-start.11
  67.1 4.9 %collective-permute-start.2 = (f32[32,16,128]{2,1,0:T(8,128)S(1)}, f32[32,16,128]{2,1,0:T(8,128)S(1)}, u32[]{:S(2)}, u32[]{:S(2)}) collective-permute-start(f32[32,16,128]{2,1,0:T(8,128)S(1)} %get-tuple-element.27), channel_id=1, source_target_pairs={{0,8},{8,0},{16,24},{24,16},{32,40},{40,32},{48,56},{56,48},{64,72... | collective-permute-start | bytes 786440 | tf_op jit(solution)/shard_map/ppermute | solution.py:602
  72.7 18.3 %all-to-all-start.2 = ((f32[32,16,128]{2,1,0:T(8,128)}), f32[32,16,128]{2,1,0:T(8,128)S(1)}, u32[]{:S(2)}, u32[]{:S(2)}) async-start(f32[32,16,128]{2,1,0:T(8,128)} %add.23), calls=%async_computation.2 | async-start | bytes 524288 | tf_op jit(solution)/shard_map/all_to_all | solution.py:605
  91.7 12.4 %all-to-all-start.3 = ((f32[8,16,128]{2,1,0:T(8,128)}), f32[8,16,128]{2,1,0:T(8,128)S(1)}, u32[]{:S(2)}, u32[]{:S(2)}) async-start(f32[8,16,128]{2,1,0:T(8,128)} %broadcast_in_dim.4), calls=%async_computation.3 | async-start | bytes 131072 | tf_op jit(solution)/shard_map/all_to_all | solution.py:608
  104.8 0.7 copy-start.12
  104.9 0.7 copy-start.13

commit v4 on v3

--- a/solution.py
+++ b/solution.py
@@ -21,8 +21,9 @@
 BLOCKS = 16
 HIDDEN, DN, DH, EMB_OWN, EMB_GHOST = (slice(C * i, C * i + C) for i in range(5))
 Z = slice(5 * C, 5 * C + FF)
-OWN, GHOST, CONTRIB_OWN, CONTRIB_GHOST = (slice(9 * C + 8 * i, 9 * C + 8 * i + 8) for i in range(4))
-KEPT = [(9 * C + 32, A), (8, E), (8, E), (C, E), (C, E)]
+GHOST, CONTRIB_OWN, CONTRIB_GHOST = (slice(9 * C + 8 * i, 9 * C + 8 * i + 8) for i in range(3))
+OWN = slice(9 * C + 24, 9 * C + 40)
+KEPT = [(9 * C + 40, A), (8, E), (8, E), (C, E), (C, E)]
 
 highest = lax.Precision.HIGHEST
 cutoff = 6.0
@@ -73,6 +74,15 @@
     return fold_rows(mm(w, x, NN))
 
 
+def lhs_deep(w):
+    high, low = split(w)
+    return jnp.concatenate([high, high, low], axis=1)
+
+
+def deep(pair):
+    return jnp.concatenate([pair, pair[: pair.shape[0] // 2]], axis=0)
+
+
 def wide(x):
     return jnp.concatenate(split(x), axis=1)
 
@@ -99,16 +109,21 @@
     return lax.broadcasted_iota(jnp.int32, shape, dim)
 
 
-def select_lists(send_left, send_right):
+def select_lists(own):
+    return (iota((A, 128), 0) == own[8:9].astype(jnp.int32)).astype(f32)
+
+
+def pack_own(positions, species, force_ref, send_left, send_right, stress_ref):
+    lane = iota((1, A), 1)
+    refs = jnp.zeros((1, A), f32)
+    for i in range(3):
+        for j in range(3):
+            refs = refs + jnp.where(lane == 3 * i + j, stress_ref[i][:, j : j + 1], 0.0)
+    rows = [positions[i] for i in range(3)] + [species[...].astype(f32)]
     lists = jnp.concatenate(
         [send_right[...], send_left[...], jnp.full((1, 128 - 2 * G), -1, jnp.int32)], axis=1
     )
-    return (iota((A, 128), 0) == lists).astype(f32)
-
-
-def pack_own(positions, species, force_ref):
-    rows = [positions[i] for i in range(3)] + [species[...].astype(f32)]
-    rows = rows + [force_ref[i] for i in range(3)] + [jnp.zeros((1, A), f32)]
+    rows = rows + [force_ref[i] for i in range(3)] + [refs, lists.astype(f32), jnp.zeros((7, A), f32)]
     return jnp.concatenate(rows, axis=0)
 
 
@@ -131,9 +146,12 @@
     )
 
 
-def prepare_kernel(positions, species, force_ref, send_left, send_right, shard, outgoing, blocks):
-    own = pack_own(positions, species, force_ref)
-    outgoing[...] = full_dot(own, select_lists(send_left, send_right), NN)
+def prepare_kernel(
+    positions, species, force_ref, send_left, send_right, stress_ref, shard, own_out, outgoing, blocks
+):
+    own = pack_own(positions, species, force_ref, send_left, send_right, stress_ref)
+    own_out[...] = own
+    outgoing[...] = full_dot(own[:8], select_lists(own), NN)
     x = shard[...].reshape(1, 1920)
     one = x.astype(bf16).astype(f32)
     two = (x - one).astype(bf16).astype(f32)
@@ -175,13 +193,10 @@
 
 
 def silu_parts(a):
-    sig = 0.5 * jnp.tanh(0.5 * a) + 0.5
-    first = sig * (1.0 + a * (1.0 - sig))
-    return sig, first
-
-
-def silu_second(a, sig):
-    return sig * (1.0 - sig) * (2.0 + a * (1.0 - 2.0 * sig))
+    t = jnp.tanh(0.5 * a)
+    sig = 0.5 * t + 0.5
+    peak = 0.25 - 0.25 * (t * t)
+    return sig, sig + a * peak, peak * (2.0 - a * t)
 
 
 def one_hots(s, t):
@@ -192,8 +207,8 @@
 
 
 def forward_kernel(
-    slabs, count_ref, scalars, wg, positions, species, force_ref, first_ghost, second_ghost, src, dst,
-    send_left, send_right, message, atoms, rows_out, vec_out, dfilt_out, q_out,
+    slabs, count_ref, scalars, wg, own, first_ghost, second_ghost, src, dst,
+    message, atoms, rows_out, vec_out, dfilt_out, q_out,
     src_hot, dst_hot, total, force_total,
 ):
 
@@ -201,7 +216,7 @@
     rank = scalars[0]
     box = slab_width * slabs
     table_t = weight(wg, 0)
-    one_t = lhs(radial_one_t(wg))
+    one_t = lhs_deep(radial_one_t(wg))
     two_t = lhs(weight(wg, 3))
     message_t = lhs(weight(wg, 5))
     update_f = update_weight_t(wg)
@@ -209,11 +224,12 @@
     update = lhs(update_f.T)
     readout = readout_column(wg)
 
-    own_rows = pack_own(positions, species, force_ref)
+    own = own[...]
+    own_rows = own[:8]
     lane = iota((8, 128), 1)
     row = iota((8, 128), 0)
     ghost_rows = jnp.where((lane < G) == (rank % 2 == 1), first_ghost[...], second_ghost[...])
-    atoms[OWN] = own_rows
+    atoms[OWN] = own
     atoms[GHOST] = ghost_rows
     shift = jnp.where(lane < G, jnp.where(rank == 0, -box, 0.0), 0.0)
     shift = shift + jnp.where((lane >= G) & (lane < 2 * G), jnp.where(rank == slabs - 1, box, 0.0), 0.0)
@@ -255,9 +271,9 @@
         delta = dist - centers
         basis = jnp.exp(-spread * delta * delta)
         dbasis = (-2.0 * spread) * delta * basis
-        a = wdot(one_t, stack(basis))
-        da = wdot(one_t, stack(dbasis))
-        sig, slope = silu_parts(a)
+        a = mm(one_t, deep(stack(basis)), NN)
+        da = mm(one_t, deep(stack(dbasis)), NN)
+        sig, slope, second = silu_parts(a)
         f = wdot(two_t, stack(a * sig))
         df = wdot(two_t, stack(slope * da))
         filt = f * gate
@@ -272,7 +288,7 @@
     rms = lax.rsqrt(jnp.mean(hidden * hidden, axis=0, keepdims=True) + 1e-05)
     z = wdot(update_t, stack(hidden * rms))
     atoms[Z] = z
-    sig, slope = silu_parts(z)
+    sig, slope, second = silu_parts(z)
     live_atom = (iota((1, A), 1) < count).astype(f32)
     weighted = readout * live_atom
     energy = jnp.sum(jnp.sum(weighted * (z * sig), axis=0, keepdims=True), axis=1, keepdims=True)
@@ -303,7 +319,7 @@
     contrib = whole(force_total[...])
     atoms[CONTRIB_OWN] = contrib[:, :A]
     atoms[CONTRIB_GHOST] = contrib[:, A:]
-    lists_hot = select_lists(send_left, send_right)
+    lists_hot = select_lists(own)
     outgoing = full_dot(contrib[:, :A], lists_hot, NN) + pltpu.roll(contrib[:, A:], 64, 1)
     to_right = (lane < G) | (lane >= 96)
     sums = jnp.zeros((8, 128), f32)
@@ -319,7 +335,7 @@
 
 
 def backward_kernel(
-    slabs, count_ref, scalars, energy_ref, stress_ref, wg, src, dst, send_left, send_right, received, atoms, rows_in, vec_in, dfilt_in, q_in,
+    slabs, count_ref, scalars, energy_ref, wg, src, dst, received, atoms, rows_in, vec_in, dfilt_in, q_in,
     forces_out, sums_out, keep, give,
     src_hot, dst_hot, grad, step_row, total, source_total, one_total, two_total,
 ):
@@ -328,7 +344,7 @@
     core = scalars[1]
     volume = slab_width * cross_area * slabs
     scale = 2.0 / (slabs * A)
-    one_t = lhs(radial_one_t(wg))
+    one_t = lhs_deep(radial_one_t(wg))
     two_f = weight(wg, 3)
     two_t = lhs(two_f)
     two = lhs(two_f.T)
@@ -337,10 +353,10 @@
     update_t = lhs(update_f)
     update = lhs(update_f.T)
     readout = readout_column(wg)
-    lists_hot = select_lists(send_left, send_right)
+    own = atoms[OWN]
+    lists_hot = select_lists(own)
     lane = iota((8, 128), 1)
     row = iota((8, 128), 0)
-    own = atoms[OWN]
     ghost = atoms[GHOST]
 
     got = jnp.sum(received[...], axis=0)
@@ -358,13 +374,8 @@
     cot_own = jnp.where((lane < count) & (row < 3), factor * (force_own - own_ref), 0.0)
     cot_ghost = jnp.where((lane < 2 * G) & (row < 3), factor * (force_ghost - ghost_ref), 0.0)
     cot = exact(jnp.concatenate([cot_own, cot_ghost], axis=1))
-    stress_cot = [
-        [
-            (2.0 * stress_weight / volume) * (got[3:4, 3 * i + j : 3 * i + j + 1] / volume - stress_ref[i, 0, j])
-            for j in range(3)
-        ]
-        for i in range(3)
-    ]
+    stress_row = (2.0 * stress_weight / volume) * (got[3:4] / volume - own[7:8])
+    stress_cot = [[stress_row[:, 3 * i + j : 3 * i + j + 1] for j in range(3)] for i in range(3)]
     energy_cot = (energy - energy_ref[0]) * scale
     total[...] = jnp.zeros_like(total)
 
@@ -395,10 +406,10 @@
     moved_n = rms * moved_h - (cube * cross) * hidden
     moved_n2 = stack(moved_n)
     moved_z = wdot(update_t, moved_n2)
-    sig, slope = silu_parts(z)
+    sig, slope, second = silu_parts(z)
     live_atom = (iota((1, A), 1) < count).astype(f32)
     weighted = readout * live_atom
-    z_bar = weighted * (energy_cot * slope + silu_second(z, sig) * moved_z)
+    z_bar = weighted * (energy_cot * slope + second * moved_z)
     z_bar = stack(z_bar)
     update_grad = fold(
         mm(
@@ -452,14 +463,14 @@
         moved_basis = (-2.0 * spread) * delta * basis * step
         basis = stack(basis)
         moved_basis = stack(moved_basis)
-        a = wdot(one_t, basis)
-        moved_a = wdot(one_t, moved_basis)
-        sig, slope = silu_parts(a)
+        a = mm(one_t, deep(basis), NN)
+        moved_a = mm(one_t, deep(moved_basis), NN)
+        sig, slope, second = silu_parts(a)
         inner = stack(a * sig)
         filt = wdot(two_t, inner) * gate
         source_total[...] += mm(stack(m_bar * filt + dm_bar * (dfilt_in[:, at] * step)), hot_s, NT)
         two_total[...] += mm(f_bar, inner, NT) + mm(df_bar, stack(slope * moved_a), NT)
-        a_bar = stack(s_bar * slope + ds_bar * (silu_second(a, sig) * moved_a))
+        a_bar = stack(s_bar * slope + ds_bar * (second * moved_a))
         da_bar = stack(ds_bar * slope)
         one_total[...] += mm(a_bar, basis, NT) + mm(da_bar, moved_basis, NT)
 
@@ -496,15 +507,15 @@
     return jax.ShapeDtypeStruct(dims, dtype)
 
 
-def prepare(positions, species, force_ref, send_left, send_right, shard, shards):
+def prepare(shards, *arrays):
     return pl.pallas_call(
         prepare_kernel,
-        out_shape=[shape(8, 128), shape(shards, BLOCKS, 128)],
-        in_specs=[vmem] * 6,
-        out_specs=[vmem] * 2,
-        compiler_params=params_vmem,
+        out_shape=[shape(16, 128), shape(8, 128), shape(shards, BLOCKS, 128)],
+        in_specs=[vmem] * len(arrays),
+        out_specs=[vmem] * 3,
+        compiler_params=pltpu.CompilerParams(vmem_limit_bytes=60 * 1024 * 1024),
         name="prepare",
-    )(positions, species, force_ref, send_left, send_right, shard)
+    )(*arrays)
 
 
 def forward(slabs, counts, scalars, wg, *arrays):
@@ -524,12 +535,12 @@
     )(counts, scalars, wg, *arrays)
 
 
-def backward(slabs, counts, scalars, energy_ref, stress_ref, *arrays):
+def backward(slabs, counts, scalars, energy_ref, *arrays):
     outs = [shape(8, 128), shape(8, 128), shape(32, BLOCKS, 128), shape(32, BLOCKS, 128)]
     return pl.pallas_call(
         functools.partial(backward_kernel, slabs),
         out_shape=outs,
-        in_specs=[smem] * 4 + [vmem] * len(arrays),
+        in_specs=[smem] * 3 + [vmem] * len(arrays),
         out_specs=[vmem] * 4,
         scratch_shapes=[
             pltpu.VMEM((N, E), bf16),
@@ -543,7 +554,7 @@
         ],
         compiler_params=params_vmem,
         name="weight_gradients",
-    )(counts, scalars, energy_ref, stress_ref, *arrays)
+    )(counts, scalars, energy_ref, *arrays)
 
 
 def from_blocks(y):
@@ -551,14 +562,16 @@
     return jnp.concatenate([two.T.reshape(-1), y[7:15].T.reshape(-1), y[15, :56]])
 
 
+def decay(params, moment_one, moment_two):
+    return params - (0.001 * 0.01) * params, 0.9 * moment_one, 0.999 * moment_two
+
+
 def adam(params, moment_one, moment_two, grad):
-    new_moment_one = 0.9 * moment_one + 0.1 * grad
-    new_moment_two = 0.999 * moment_two + 0.001 * grad * grad
+    new_moment_one = moment_one + 0.1 * grad
+    new_moment_two = moment_two + 0.001 * grad * grad
     corrected_one = new_moment_one / (1.0 - 0.9**STEP)
     corrected_two = new_moment_two / (1.0 - 0.999**STEP)
-    new_params = params - 0.001 * (
-        corrected_one / (jnp.sqrt(corrected_two) + 1e-08) + 0.01 * params
-    )
+    new_params = params - 0.001 * (corrected_one / (jnp.sqrt(corrected_two) + 1e-08))
     return new_params, new_moment_one, new_moment_two
 
 
@@ -583,22 +596,30 @@
     index = lax.axis_index("dp")
     core = index % 2
     scalars = jnp.stack([rank, core]).astype(jnp.int32)
-    atoms = (positions.reshape(3, 1, A), species[0], force_ref.reshape(3, 1, A))
-    lists = (send_left[0], send_right[0])
-    outgoing, blocks = prepare(*atoms, *lists, params, shards)
+    own, outgoing, blocks = prepare(
+        shards,
+        positions.reshape(3, 1, A),
+        species[0],
+        force_ref.reshape(3, 1, A),
+        send_left[0],
+        send_right[0],
+        stress_ref.reshape(3, 1, 3),
+        params,
+    )
     wg = lax.all_to_all(blocks, "dp", 0, 0, tiled=True)
     first = lax.ppermute(outgoing, "graph", [(i, i ^ 1) for i in range(slabs)])
     second = lax.ppermute(
         outgoing, "graph", [(i, (i + (1 if i % 2 else slabs - 1)) % slabs) for i in range(slabs)]
     )
     message, *kept = forward(
-        slabs, counts, scalars, wg, *atoms, first, second, source[0], target[0], *lists
+        slabs, counts, scalars, wg, own, first, second, source[0], target[0]
     )
     received = lax.all_to_all(message, "graph", 0, 0, tiled=True)
     forces, sums, keep, give = backward(
-        slabs, counts, scalars, energy_ref, stress_ref.reshape(3, 1, 3), wg, source[0], target[0], *lists, received, *kept
+        slabs, counts, scalars, energy_ref, wg, source[0], target[0], received, *kept
     )
     volume = slabs * slab_width * cross_area
+    decayed = lax.optimization_barrier(decay(params, moment_one, moment_two))
     pair = keep + lax.ppermute(give, "dp", [(i, i ^ 1) for i in range(shards)])
     chips = [list(range(c, shards, 2)) for c in range(2)]
     within = jnp.sum(
@@ -606,7 +627,7 @@
     )
     copies = jnp.broadcast_to(within[None], (slabs, BLOCKS, 128))
     grad = from_blocks(jnp.sum(lax.all_to_all(copies, "graph", 0, 0, tiled=True), axis=0))
-    new_params, new_moment_one, new_moment_two = adam(params, moment_one, moment_two, grad)
+    new_params, new_moment_one, new_moment_two = adam(*decayed, grad)
     return (
         new_params,
         new_moment_one,

time: 108 us -> 105 us (0.972)
  local copies, waits for them, and re-layouts: 7.77 us -> 3.83 us
  starting transfers between devices: 46.5 us -> 49.3 us
  waiting for transfers between devices: 34.1 us -> 32.1 us
    unnamed x29 -> x15, local copies, waits for them, and re-layouts: 5.22 us -> 1.28 us
    ppermute x1, starting transfers between devices: 3.17 us -> 4.76 us  [body(): first = lax.ppermute(outgoing, 'graph', [(i, i ^ 1) for i in range(slabs)])]
    all_to_all x1, starting transfers between devices: 7.28 us -> 8.65 us  [body(): lax.all_to_all(pair, 'dp', 0, 0, tiled=True, axis_index_groups=chips)]
    ppermute x1, waiting for transfers between devices: 1.31 us -> 0.01 us  [body(): first = lax.ppermute(outgoing, 'graph', [(i, i ^ 1) for i in range(slabs)])]
    all_to_all x1, waiting for transfers between devices: 8.45 us -> 7.2 us  [body(): lax.all_to_all(copies, 'graph', 0, 0, tiled=True)]
  transfers between devices with their start and end apart: 7 -> 7, of which waited for: 7 -> 6; matrix products, arithmetic and copies ran while one was open for 2% -> 2% of each run, Pallas kernels for 0% -> 0%
where the time goes in v4:
time: 105 us; the launch traced here: 104 us
  starting transfers between devices  49.3 us (47%)
  waiting for transfers between devices  32.1 us (31%)
  Pallas kernels  14.6 us (14%)
  local copies, waits for them, and re-layouts  3.83 us (4%)
  between operations  2.15 us (2%)
  other arithmetic  1.59 us (2%)
    all_to_all x1, starting transfers between devices, body(): wg = lax.all_to_all(blocks, 'dp', 0, 0, tiled=True)  15.5 us
    all_to_all x1, waiting for transfers between devices, body(): lax.all_to_all(pair, 'dp', 0, 0, tiled=True, axis_index_groups=chips)  10.3 us
    all_to_all x1, starting transfers between devices, body(): lax.all_to_all(pair, 'dp', 0, 0, tiled=True, axis_index_groups=chips)  8.65 us
    all_to_all x1, waiting for transfers between devices, body(): received = lax.all_to_all(message, 'graph', 0, 0, tiled=True)  8.32 us
    all_to_all x1, waiting for transfers between devices, body(): lax.all_to_all(copies, 'graph', 0, 0, tiled=True)  7.2 us
    pallas_call x1, Pallas kernels, backward(): pl.pallas_call(functools.partial(backward_kernel, slabs), out_shape=outs,...  7.08 us
    ppermute x1, starting transfers between devices, body(): lax.ppermute(outgoing, 'graph', [(i, (i + (1 if i % 2 else slabs - 1)) %...  6.63 us
    all_to_all x1, starting transfers between devices, body(): received = lax.all_to_all(message, 'graph', 0, 0, tiled=True)  6.59 us
  transfers between devices with their start and end apart: 7, of which 6 were waited for; matrix products, arithmetic and copies ran while one was open for 2% of the time, Pallas kernels for 0%

profile of v4, /device:TPU:1, one launch (start us, length us, event | category | flops | bytes accessed | tf_op | source)
XLA Modules:
  0.0 103.6 jit_solution(3154202261614643650)
XLA Ops:
  0.6 2.0 %prepare.1 = (f32[16,128]{1,0:T(8,128)}, f32[8,128]{1,0:T(8,128)}, f32[64,16,128]{2,1,0:T(8,128)}) custom-call(f32[3,1,128]{2,1,0:T(1,128)} %bitcast.23, s32[1,128]{1,0:T(1,128)} %bitcast.26, f32[3,1,128]{2,1,0:T(1,128)} %bitcast.24, s32[1,32]{1,0:T(1,128)} %bitcast.27, s32[1,32]{1,0:T(1,128)} %bitcast.28, f32[3,1,3]{2,1,0:T(1,128)} %bitcast.25, f32[1920]{0:T(1024)} %shard.1), custom_call_target="tpu_custom_call" | custom-call | tf_op jit(solution)/shard_map/prepare/pallas_call | solution.py:511
  2.6 15.5 %all-to-all-start = ((f32[64,16,128]{2,1,0:T(8,128)}), f32[64,16,128]{2,1,0:T(8,128)S(1)}, u32[]{:S(2)}, u32[]{:S(2)}) async-start(f32[64,16,128]{2,1,0:T(8,128)} %get-tuple-element.24), calls=%async_computation | async-start | bytes 1048576 | tf_op jit(solution)/shard_map/all_to_all | solution.py:609
  18.2 4.8 %collective-permute-start = (f32[8,128]{1,0:T(8,128)S(1)}, f32[8,128]{1,0:T(8,128)S(1)}, u32[]{:S(2)}, u32[]{:S(2)}) collective-permute-start(f32[8,128]{1,0:T(8,128)S(1)} %copy-done.6), channel_id=1, source_target_pairs={{0,1},{1,0},{2,3},{3,2},{4,5},{5,4},{6,7},{7,6},{8,9},{9,8},{10,11... | collective-permute-start | bytes 12296 | tf_op jit(solution)/shard_map/ppermute | solution.py:610
  22.9 6.6 %collective-permute-start.1 = (f32[8,128]{1,0:T(8,128)S(1)}, f32[8,128]{1,0:T(8,128)S(1)}, u32[]{:S(2)}, u32[]{:S(2)}) collective-permute-start(f32[8,128]{1,0:T(8,128)S(1)} %copy-done.6), channel_id=1, source_target_pairs={{0,7},{1,2},{2,1},{3,4},{4,3},{5,6},{6,5},{7,0},{8,15},{9,10},{10,... | collective-permute-start | bytes 12296 | tf_op jit(solution)/shard_map/ppermute | solution.py:611
  29.6 0.1 pad_add_fusion.scalars
  30.4 3.1 %collective-permute-done.1.second_ghost = f32[8,128]{1,0:T(8,128)S(1)} collective-permute-done((f32[8,128]{1,0:T(8,128)S(1)}, f32[8,128]{1,0:T(8,128)S(1)}, u32[]{:S(2)}, u32[]{:S(2)}) %collective-permute-start.1) | collective-permute-done | bytes 4128 | tf_op jit(solution)/shard_map/ppermute | solution.py:611
  33.4 2.1 %all-to-all-done.wg = f32[64,16,128]{2,1,0:T(8,128)S(1)} async-done(((f32[64,16,128]{2,1,0:T(8,128)}), f32[64,16,128]{2,1,0:T(8,128)S(1)}, u32[]{:S(2)}, u32[]{:S(2)}) %all-to-all-start) | async-done | bytes 524320 | tf_op jit(solution)/shard_map/all_to_all | solution.py:609
  35.5 5.6 %energy_slopes.1 = (f32[8,4,128]{2,1,0:T(4,128)}, f32[1192,128]{1,0:T(8,128)S(1)}, f32[8,2048]{1,0:T(8,128)S(1)}, f32[8,2048]{1,0:T(8,128)S(1)}, f32[128,2048]{1,0:T(8,128)S(1)}, /*index=5*/f32[128,2048]{1,0:T(8,128)S(1)}) custom-call(s32[1,1]{1,0:T(1,128)S(6)} %copy.29.count_ref, s32[2]{0:T(128)S(1)} %pad_add_fusion.scalars, ...), custom_call_target="tpu_custom_call" | custom-call | tf_op jit(solution)/shard_map/energy_slopes/pallas_call | solution.py:522
  41.1 6.6 %all-to-all-start.1 = ((f32[8,4,128]{2,1,0:T(4,128)}), f32[8,4,128]{2,1,0:T(4,128)S(1)}, u32[]{:S(2)}, u32[]{:S(2)}) async-start(f32[8,4,128]{2,1,0:T(4,128)} %get-tuple-element.27), calls=%async_computation.1 | async-start | bytes 32768 | tf_op jit(solution)/shard_map/all_to_all | solution.py:617
  48.3 8.3 %all-to-all-done.1.received = f32[8,4,128]{2,1,0:T(4,128)S(1)} async-done(((f32[8,4,128]{2,1,0:T(4,128)}), f32[8,4,128]{2,1,0:T(4,128)S(1)}, u32[]{:S(2)}, u32[]{:S(2)}) %all-to-all-start.1) | async-done | bytes 16416 | tf_op jit(solution)/shard_map/all_to_all | solution.py:617
  56.6 7.1 %weight_gradients.1 = (f32[8,128]{1,0:T(8,128)S(1)}, f32[8,128]{1,0:T(8,128)S(1)}, f32[32,16,128]{2,1,0:T(8,128)S(1)}, f32[32,16,128]{2,1,0:T(8,128)S(1)}) custom-call(s32[1,1]{1,0:T(1,128)S(6)} %copy.29.count_ref, s32[2]{0:T(128)S(1)} %pad_add_fusion.scalars, f32[1]{0:T(128)S(6)} %copy.30.energy_ref, f32[64,16,128]{2,1,0:T(8,128)S(1)} %all-to-all-done.wg, ...), custom_call_target="tpu_custom_call" | custom-call | tf_op jit(solution)/shard_map/weight_gradients/pallas_call | solution.py:540
  63.7 3.8 %collective-permute-start.2 = (f32[32,16,128]{2,1,0:T(8,128)S(1)}, f32[32,16,128]{2,1,0:T(8,128)S(1)}, u32[]{:S(2)}, u32[]{:S(2)}) collective-permute-start(f32[32,16,128]{2,1,0:T(8,128)S(1)} %get-tuple-element.34), channel_id=1, source_target_pairs={{0,8},{8,0},{16,24},{24,16},{32,40},{40,32},{48,56},{56,48},{64,72... | collective-permute-start | bytes 786440 | tf_op jit(solution)/shard_map/ppermute | solution.py:623
  67.5 1.1 %collective-permute-done.2 = f32[32,16,128]{2,1,0:T(8,128)S(1)} collective-permute-done((f32[32,16,128]{2,1,0:T(8,128)S(1)}, f32[32,16,128]{2,1,0:T(8,128)S(1)}, u32[]{:S(2)}, u32[]{:S(2)}) %collective-permute-start.2) | collective-permute-done | bytes 262176 | tf_op jit(solution)/shard_map/ppermute | solution.py:623
  68.6 0.7 add.20
  69.4 8.7 %all-to-all-start.2 = ((f32[32,16,128]{2,1,0:T(8,128)}), f32[32,16,128]{2,1,0:T(8,128)S(1)}, u32[]{:S(2)}, u32[]{:S(2)}) async-start(f32[32,16,128]{2,1,0:T(8,128)} %add.20), calls=%async_computation.2 | async-start | bytes 524288 | tf_op jit(solution)/shard_map/all_to_all | solution.py:626
  78.1 0.7 copy-done.4
  78.7 0.0 copy-done.5
  78.8 10.3 %all-to-all-done.2 = f32[32,16,128]{2,1,0:T(8,128)S(1)} async-done(((f32[32,16,128]{2,1,0:T(8,128)}), f32[32,16,128]{2,1,0:T(8,128)S(1)}, u32[]{:S(2)}, u32[]{:S(2)}) %all-to-all-start.2) | async-done | bytes 262176 | tf_op jit(solution)/shard_map/all_to_all | solution.py:626
  89.1 0.6 broadcast_in_dim.4
  89.7 3.3 %all-to-all-start.3 = ((f32[8,16,128]{2,1,0:T(8,128)}), f32[8,16,128]{2,1,0:T(8,128)S(1)}, u32[]{:S(2)}, u32[]{:S(2)}) async-start(f32[8,16,128]{2,1,0:T(8,128)} %broadcast_in_dim.4), calls=%async_computation.3 | async-start | bytes 131072 | tf_op jit(solution)/shard_map/all_to_all | solution.py:629
  93.1 0.6 copy.27
  93.7 0.6 slice.34
  94.3 0.6 div.27
  94.9 7.2 %all-to-all-done.3 = f32[8,16,128]{2,1,0:T(8,128)S(1)} async-done(((f32[8,16,128]{2,1,0:T(8,128)}), f32[8,16,128]{2,1,0:T(8,128)S(1)}, u32[]{:S(2)}, u32[]{:S(2)}) %all-to-all-start.3) | async-done | bytes 65568 | tf_op jit(solution)/shard_map/all_to_all | solution.py:629
  102.2 0.1 reshape_squeeze.3
  102.3 0.1 maximum_bitcast_fusion
  102.4 0.1 copy.25
  102.5 0.2 reshape.44
  102.7 0.1 copy.26
  102.8 0.1 reshape.45
  102.9 0.1 concatenate.7
  102.9 0.6 multiply_subtract_fusion.1
  (24 shorter events, 0.1 us)
Async XLA Ops:
  2.6 15.6 %copy-start.6 = (f32[8,128]{1,0:T(8,128)S(1)}, f32[8,128]{1,0:T(8,128)}, u32[]{:S(2)}) copy-start(f32[8,128]{1,0:T(8,128)} %get-tuple-element.26) | copy-start | bytes 12292
  2.6 32.9 %all-to-all-start = ((f32[64,16,128]{2,1,0:T(8,128)}), f32[64,16,128]{2,1,0:T(8,128)S(1)}, u32[]{:S(2)}, u32[]{:S(2)}) async-start(f32[64,16,128]{2,1,0:T(8,128)} %get-tuple-element.24), calls=%async_computation | async-start | bytes 1048576 | tf_op jit(solution)/shard_map/all_to_all | solution.py:609
  18.2 12.2 %collective-permute-start = (f32[8,128]{1,0:T(8,128)S(1)}, f32[8,128]{1,0:T(8,128)S(1)}, u32[]{:S(2)}, u32[]{:S(2)}) collective-permute-start(f32[8,128]{1,0:T(8,128)S(1)} %copy-done.6), channel_id=1, source_target_pairs={{0,1},{1,0},{2,3},{3,2},{4,5},{5,4},{6,7},{7,6},{8,9},{9,8},{10,11... | collective-permute-start | bytes 12296 | tf_op jit(solution)/shard_map/ppermute | solution.py:610
  22.9 10.5 %collective-permute-start.1 = (f32[8,128]{1,0:T(8,128)S(1)}, f32[8,128]{1,0:T(8,128)S(1)}, u32[]{:S(2)}, u32[]{:S(2)}) collective-permute-start(f32[8,128]{1,0:T(8,128)S(1)} %copy-done.6), channel_id=1, source_target_pairs={{0,7},{1,2},{2,1},{3,4},{4,3},{5,6},{6,5},{7,0},{8,15},{9,10},{10,... | collective-permute-start | bytes 12296 | tf_op jit(solution)/shard_map/ppermute | solution.py:611
  29.6 5.9 %copy-start.2 = (f32[16,128]{1,0:T(8,128)S(1)}, f32[16,128]{1,0:T(8,128)}, u32[]{:S(2)}) copy-start(f32[16,128]{1,0:T(8,128)} %get-tuple-element.25.own) | copy-start | bytes 24580
  29.6 5.9 %copy-start.1 = (s32[1,1,2048]{2,1,0:T(1,128)S(1)}, s32[1,1,2048]{2,1,0:T(1,128)}, u32[]{:S(2)}) copy-start(s32[1,1,2048]{2,1,0:T(1,128)} %param.17) | copy-start | bytes 24580
  29.6 5.9 %copy-start = (s32[1,1,2048]{2,1,0:T(1,128)S(1)}, s32[1,1,2048]{2,1,0:T(1,128)}, u32[]{:S(2)}) copy-start(s32[1,1,2048]{2,1,0:T(1,128)} %param.16) | copy-start | bytes 24580
  41.1 15.6 %all-to-all-start.1 = ((f32[8,4,128]{2,1,0:T(4,128)}), f32[8,4,128]{2,1,0:T(4,128)S(1)}, u32[]{:S(2)}, u32[]{:S(2)}) async-start(f32[8,4,128]{2,1,0:T(4,128)} %get-tuple-element.27), calls=%async_computation.1 | async-start | bytes 32768 | tf_op jit(solution)/shard_map/all_to_all | solution.py:617
  63.7 4.9 %collective-permute-start.2 = (f32[32,16,128]{2,1,0:T(8,128)S(1)}, f32[32,16,128]{2,1,0:T(8,128)S(1)}, u32[]{:S(2)}, u32[]{:S(2)}) collective-permute-start(f32[32,16,128]{2,1,0:T(8,128)S(1)} %get-tuple-element.34), channel_id=1, source_target_pairs={{0,8},{8,0},{16,24},{24,16},{32,40},{40,32},{48,56},{56,48},{64,72... | collective-permute-start | bytes 786440 | tf_op jit(solution)/shard_map/ppermute | solution.py:623
  69.4 8.7 %copy-start.3 = (f32[1920]{0:T(1024)S(1)}, f32[1920]{0:T(1024)}, u32[]{:S(2)}) copy-start(f32[1920]{0:T(1024)} %shard.1) | copy-start | bytes 23044
  69.4 19.7 %all-to-all-start.2 = ((f32[32,16,128]{2,1,0:T(8,128)}), f32[32,16,128]{2,1,0:T(8,128)S(1)}, u32[]{:S(2)}, u32[]{:S(2)}) async-start(f32[32,16,128]{2,1,0:T(8,128)} %add.20), calls=%async_computation.2 | async-start | bytes 524288 | tf_op jit(solution)/shard_map/all_to_all | solution.py:626
  78.0 0.7 copy-start.4
  78.1 0.7 copy-start.5
  89.7 12.4 %all-to-all-start.3 = ((f32[8,16,128]{2,1,0:T(8,128)}), f32[8,16,128]{2,1,0:T(8,128)S(1)}, u32[]{:S(2)}, u32[]{:S(2)}) async-start(f32[8,16,128]{2,1,0:T(8,128)} %broadcast_in_dim.4), calls=%async_computation.3 | async-start | bytes 131072 | tf_op jit(solution)/shard_map/all_to_all | solution.py:629

commit v5 on v4

--- a/solution.py
+++ b/solution.py
@@ -207,7 +207,7 @@
 
 
 def forward_kernel(
-    slabs, count_ref, scalars, wg, own, first_ghost, second_ghost, src, dst,
+    slabs, count_ref, scalars, energy_ref, wg, own, first_ghost, second_ghost, src, dst,
     message, atoms, rows_out, vec_out, dfilt_out, q_out,
     src_hot, dst_hot, total, force_total,
 ):
@@ -229,7 +229,7 @@
     lane = iota((8, 128), 1)
     row = iota((8, 128), 0)
     ghost_rows = jnp.where((lane < G) == (rank % 2 == 1), first_ghost[...], second_ghost[...])
-    atoms[OWN] = own
+    atoms[OWN] = jnp.where((iota(own.shape, 0) == 7) & (iota(own.shape, 1) == 9), energy_ref[0], own)
     atoms[GHOST] = ghost_rows
     shift = jnp.where(lane < G, jnp.where(rank == 0, -box, 0.0), 0.0)
     shift = shift + jnp.where((lane >= G) & (lane < 2 * G), jnp.where(rank == slabs - 1, box, 0.0), 0.0)
@@ -335,8 +335,8 @@
 
 
 def backward_kernel(
-    slabs, count_ref, scalars, energy_ref, wg, src, dst, received, atoms, rows_in, vec_in, dfilt_in, q_in,
-    forces_out, sums_out, keep, give,
+    slabs, count_ref, scalars, wg, src, dst, received, atoms, rows_in, vec_in, dfilt_in, q_in,
+    forces_out, energy_out, stress_out, keep, give,
     src_hot, dst_hot, grad, step_row, total, source_total, one_total, two_total,
 ):
 
@@ -366,8 +366,10 @@
     inner = jnp.where(lane < 2 * G, pltpu.roll(moved, 64, 1), 0.0)
     force_own = -(atoms[CONTRIB_OWN] + full_dot(inner, lists_hot, NT))
     force_ghost = -(atoms[CONTRIB_GHOST] + jnp.where(lane < 2 * G, moved, 0.0))
-    forces_out[...] = force_own
-    sums_out[...] = got
+    for i in range(3):
+        forces_out[i] = force_own[i : i + 1]
+        stress_out[i] = got[3:4, 3 * i : 3 * i + 3] / volume
+    energy_out[...] = energy
     own_ref = jnp.concatenate([own[4:8], jnp.zeros((4, 128), f32)], axis=0)
     ghost_ref = jnp.concatenate([ghost[4:8], jnp.zeros((4, 128), f32)], axis=0)
     factor = force_weight * scale
@@ -376,7 +378,7 @@
     cot = exact(jnp.concatenate([cot_own, cot_ghost], axis=1))
     stress_row = (2.0 * stress_weight / volume) * (got[3:4] / volume - own[7:8])
     stress_cot = [[stress_row[:, 3 * i + j : 3 * i + j + 1] for j in range(3)] for i in range(3)]
-    energy_cot = (energy - energy_ref[0]) * scale
+    energy_cot = (energy - own[7:8, 9:10]) * scale
     total[...] = jnp.zeros_like(total)
 
     for i in range(CHUNKS):
@@ -518,11 +520,11 @@
     )(*arrays)
 
 
-def forward(slabs, counts, scalars, wg, *arrays):
+def forward(slabs, counts, scalars, energy_ref, *arrays):
     return pl.pallas_call(
         functools.partial(forward_kernel, slabs),
         out_shape=[shape(8, 4, 128)] + [shape(*dims) for dims in KEPT],
-        in_specs=[smem] * 2 + [vmem] * (1 + len(arrays)),
+        in_specs=[smem] * 3 + [vmem] * len(arrays),
         out_specs=[vmem] * (1 + len(KEPT)),
         scratch_shapes=[
             pltpu.VMEM((N, E), bf16),
@@ -532,16 +534,16 @@
         ],
         compiler_params=params_vmem,
         name="energy_slopes",
-    )(counts, scalars, wg, *arrays)
-
-
-def backward(slabs, counts, scalars, energy_ref, *arrays):
-    outs = [shape(8, 128), shape(8, 128), shape(32, BLOCKS, 128), shape(32, BLOCKS, 128)]
+    )(counts, scalars, energy_ref, *arrays)
+
+
+def backward(slabs, counts, scalars, *arrays):
+    outs = [shape(3, 1, A), shape(1, 1), shape(3, 1, 3), shape(32, BLOCKS, 128), shape(32, BLOCKS, 128)]
     return pl.pallas_call(
         functools.partial(backward_kernel, slabs),
         out_shape=outs,
-        in_specs=[smem] * 3 + [vmem] * len(arrays),
-        out_specs=[vmem] * 4,
+        in_specs=[smem] * 2 + [vmem] * len(arrays),
+        out_specs=[vmem] * len(outs),
         scratch_shapes=[
             pltpu.VMEM((N, E), bf16),
             pltpu.VMEM((A, E), bf16),
@@ -554,7 +556,7 @@
         ],
         compiler_params=params_vmem,
         name="weight_gradients",
-    )(counts, scalars, energy_ref, *arrays)
+    )(counts, scalars, *arrays)
 
 
 def from_blocks(y):
@@ -611,15 +613,14 @@
     second = lax.ppermute(
         outgoing, "graph", [(i, (i + (1 if i % 2 else slabs - 1)) % slabs) for i in range(slabs)]
     )
+    wg, decayed = lax.optimization_barrier((wg, decay(params, moment_one, moment_two)))
     message, *kept = forward(
-        slabs, counts, scalars, wg, own, first, second, source[0], target[0]
+        slabs, counts, scalars, energy_ref, wg, own, first, second, source[0], target[0]
     )
     received = lax.all_to_all(message, "graph", 0, 0, tiled=True)
-    forces, sums, keep, give = backward(
-        slabs, counts, scalars, energy_ref, wg, source[0], target[0], received, *kept
-    )
-    volume = slabs * slab_width * cross_area
-    decayed = lax.optimization_barrier(decay(params, moment_one, moment_two))
+    forces, energy, stress, keep, give = backward(
+        slabs, counts, scalars, wg, source[0], target[0], received, *kept
+    )
     pair = keep + lax.ppermute(give, "dp", [(i, i ^ 1) for i in range(shards)])
     chips = [list(range(c, shards, 2)) for c in range(2)]
     within = jnp.sum(
@@ -632,9 +633,9 @@
         new_params,
         new_moment_one,
         new_moment_two,
-        forces[:3][None, None],
-        sums[3, 9][None],
-        (sums[3, :9] / volume).reshape(1, 3, 3),
+        forces.reshape(1, 1, 3, A),
+        energy.reshape(1),
+        stress.reshape(1, 3, 3),
     )
 
 

time: 105 us -> 101 us (0.962)
  blocking collectives: 0 us -> 44.9 us
  waiting for transfers between devices: 32.1 us -> 5.5 us
  starting transfers between devices: 49.3 us -> 29.4 us
  local copies, waits for them, and re-layouts: 3.83 us -> 2.1 us
    all_to_all x0 -> x3, blocking collectives: none -> 44.9 us  [the longest x1 18.1 us: body(): lax.all_to_all(pair, 'dp', 0, 0, tiled=True, axis_index_groups=chips)]
    all_to_all x3 -> x0, waiting for transfers between devices: 25.8 us -> none  [the longest x1 10.3 us: body(): lax.all_to_all(pair, 'dp', 0, 0, tiled=True, axis_index_groups=chips)]
    all_to_all x3 -> x0, starting transfers between devices: 18.6 us -> none  [the longest x1 8.65 us: body(): lax.all_to_all(pair, 'dp', 0, 0, tiled=True, axis_index_groups=chips)]
    ppermute x1, waiting for transfers between devices: 3.07 us -> 0.01 us  [body(): lax.ppermute(outgoing, 'graph', [(i, (i + (1 if i % 2 else slabs - 1)) %...]
    all_to_all x1, waiting for transfers between devices: 2.06 us -> 4.36 us  [body(): wg = lax.all_to_all(blocks, 'dp', 0, 0, tiled=True)]
    ppermute x1, starting transfers between devices: 4.76 us -> 3.17 us  [body(): first = lax.ppermute(outgoing, 'graph', [(i, i ^ 1) for i in range(slabs)])]
  transfers between devices with their start and end apart: 7 -> 4, of which waited for: 6 -> 2; matrix products, arithmetic and copies ran while one was open for 2% -> 0% of each run, Pallas kernels for 0% -> 0%
where the time goes in v5:
time: 101 us; the launch traced here: 99.3 us
  blocking collectives  44.9 us (44%)
  starting transfers between devices  29.4 us (29%)
  Pallas kernels  14.4 us (14%)
  waiting for transfers between devices  5.5 us (5%)
  local copies, waits for them, and re-layouts  2.1 us (2%)
  between operations  2.09 us (2%)
    all_to_all x1, blocking collectives, body(): lax.all_to_all(pair, 'dp', 0, 0, tiled=True, axis_index_groups=chips)  18.1 us
    all_to_all x1, starting transfers between devices, body(): wg = lax.all_to_all(blocks, 'dp', 0, 0, tiled=True)  15.5 us
    all_to_all x1, blocking collectives, body(): received = lax.all_to_all(message, 'graph', 0, 0, tiled=True)  15.4 us
    all_to_all x1, blocking collectives, body(): lax.all_to_all(copies, 'graph', 0, 0, tiled=True)  11.5 us
    pallas_call x1, Pallas kernels, backward(): pl.pallas_call(functools.partial(backward_kernel, slabs), out_shape=outs,...  7.49 us
    ppermute x1, starting transfers between devices, body(): lax.ppermute(outgoing, 'graph', [(i, (i + (1 if i % 2 else slabs - 1)) %...  6.95 us
    pallas_call x1, Pallas kernels, forward(): pl.pallas_call(functools.partial(forward_kernel, slabs), out_shape=[shape...  4.94 us
    all_to_all x1, waiting for transfers between devices, body(): wg = lax.all_to_all(blocks, 'dp', 0, 0, tiled=True)  4.36 us
  transfers between devices with their start and end apart: 4, of which 2 were waited for; matrix products, arithmetic and copies ran while one was open for 0% of the time, Pallas kernels for 0%

profile of v5, /device:TPU:1, one launch (start us, length us, event | category | flops | bytes accessed | tf_op | source)
XLA Modules:
  0.0 99.3 jit_solution(3692656659686762987)
XLA Ops:
  0.6 2.0 %prepare.1 = (f32[16,128]{1,0:T(8,128)}, f32[8,128]{1,0:T(8,128)}, f32[64,16,128]{2,1,0:T(8,128)}) custom-call(f32[3,1,128]{2,1,0:T(1,128)} %bitcast.25, s32[1,128]{1,0:T(1,128)} %bitcast.28, f32[3,1,128]{2,1,0:T(1,128)} %bitcast.26, s32[1,32]{1,0:T(1,128)} %bitcast.29, s32[1,32]{1,0:T(1,128)} %bitcast.30, f32[3,1,3]{2,1,0:T(1,128)} %bitcast.27, f32[1920]{0:T(1024)} %shard.1), custom_call_target="tpu_custom_call" | custom-call | tf_op jit(solution)/shard_map/prepare/pallas_call | solution.py:513
  2.6 15.5 %all-to-all-start = ((f32[64,16,128]{2,1,0:T(8,128)}), f32[64,16,128]{2,1,0:T(8,128)S(1)}, u32[]{:S(2)}, u32[]{:S(2)}) async-start(f32[64,16,128]{2,1,0:T(8,128)} %get-tuple-element.24), calls=%async_computation | async-start | bytes 1048576 | tf_op jit(solution)/shard_map/all_to_all | solution.py:611
  18.2 0.0 copy-done.6
  18.2 7.0 %collective-permute-start.1 = (f32[8,128]{1,0:T(8,128)S(1)}, f32[8,128]{1,0:T(8,128)S(1)}, u32[]{:S(2)}, u32[]{:S(2)}) collective-permute-start(f32[8,128]{1,0:T(8,128)S(1)} %copy-done.6), channel_id=1, source_target_pairs={{0,7},{1,2},{2,1},{3,4},{4,3},{5,6},{6,5},{7,0},{8,15},{9,10},{10,... | collective-permute-start | bytes 12296 | tf_op jit(solution)/shard_map/ppermute | solution.py:613
  25.1 3.2 %collective-permute-start = (f32[8,128]{1,0:T(8,128)S(1)}, f32[8,128]{1,0:T(8,128)S(1)}, u32[]{:S(2)}, u32[]{:S(2)}) collective-permute-start(f32[8,128]{1,0:T(8,128)S(1)} %copy-done.6), channel_id=1, source_target_pairs={{0,1},{1,0},{2,3},{3,2},{4,5},{5,4},{6,7},{7,6},{8,9},{9,8},{10,11... | collective-permute-start | bytes 12296 | tf_op jit(solution)/shard_map/ppermute | solution.py:612
  28.3 0.0 copy-start.3
  28.3 0.7 copy-done.3
  29.0 0.7 copy-done.4
  29.7 0.0 copy-done.5
  29.7 0.0 copy-start
  29.7 0.1 pad_add_fusion.scalars
  31.1 4.4 %all-to-all-done.wg = f32[64,16,128]{2,1,0:T(8,128)S(1)} async-done(((f32[64,16,128]{2,1,0:T(8,128)}), f32[64,16,128]{2,1,0:T(8,128)S(1)}, u32[]{:S(2)}, u32[]{:S(2)}) %all-to-all-start) | async-done | bytes 524320 | tf_op jit(solution)/shard_map/all_to_all | solution.py:611
  35.5 0.0 collective-permute-done.1.second_ghost
  35.5 0.0 collective-permute-done.first_ghost
  35.5 0.0 copy-done.2
  35.5 0.0 copy-done.1
  35.5 0.0 copy-done
  35.5 4.9 %energy_slopes.1 = (f32[8,4,128]{2,1,0:T(4,128)S(1)}, f32[1192,128]{1,0:T(8,128)S(1)}, f32[8,2048]{1,0:T(8,128)S(1)}, f32[8,2048]{1,0:T(8,128)S(1)}, f32[128,2048]{1,0:T(8,128)S(1)}, /*index=5*/f32[128,2048]{1,0:T(8,128)S(1)}) custom-call(s32[1,1]{1,0:T(1,128)S(6)} %copy.26.count_ref, s32[2]{0:T(128)S(1)} %pad_add_fusion.scalars, f32[1]{0:T(128)S(6)} %copy.27.energy_ref, ...), custom_call_target="tpu_custom_call" | custom-call | tf_op jit(solution)/shard_map/energy_slopes/pallas_call | solution.py:524
  40.5 15.4 %all_to_all.20.received = f32[8,4,128]{2,1,0:T(4,128)S(1)} all-to-all(f32[8,4,128]{2,1,0:T(4,128)S(1)} %get-tuple-element.30), channel_id=1, replica_groups=mesh['dp'=64,'graph'=8] {'graph'}, dimensions={0} | all-to-all | bytes 32768 | tf_op jit(solution)/shard_map/all_to_all | solution.py:620
  55.8 7.5 %weight_gradients.1 = (f32[3,1,128]{2,1,0:T(1,128)}, f32[1,1]{1,0:T(1,128)}, f32[3,1,3]{2,1,0:T(1,128)}, f32[32,16,128]{2,1,0:T(8,128)S(1)}, f32[32,16,128]{2,1,0:T(8,128)S(1)}) custom-call(s32[1,1]{1,0:T(1,128)S(6)} %copy.26.count_ref, s32[2]{0:T(128)S(1)} %pad_add_fusion.scalars, f32[64,16,128]{2,1,0:T(8,128)S(1)} %all-to-all-done.wg, ...), custom_call_target="tpu_custom_call" | custom-call | tf_op jit(solution)/shard_map/weight_gradients/pallas_call | solution.py:542
  63.3 3.8 %collective-permute-start.2 = (f32[32,16,128]{2,1,0:T(8,128)S(1)}, f32[32,16,128]{2,1,0:T(8,128)S(1)}, u32[]{:S(2)}, u32[]{:S(2)}) collective-permute-start(f32[32,16,128]{2,1,0:T(8,128)S(1)} %get-tuple-element.37), channel_id=1, source_target_pairs={{0,8},{8,0},{16,24},{24,16},{32,40},{40,32},{48,56},{56,48},{64,72... | collective-permute-start | bytes 786440 | tf_op jit(solution)/shard_map/ppermute | solution.py:624
  67.1 1.1 %collective-permute-done.2 = f32[32,16,128]{2,1,0:T(8,128)S(1)} collective-permute-done((f32[32,16,128]{2,1,0:T(8,128)S(1)}, f32[32,16,128]{2,1,0:T(8,128)S(1)}, u32[]{:S(2)}, u32[]{:S(2)}) %collective-permute-start.2) | collective-permute-done | bytes 262176 | tf_op jit(solution)/shard_map/ppermute | solution.py:624
  68.3 18.1 %all_to_all.21 = f32[32,16,128]{2,1,0:T(8,128)S(1)} all-to-all(f32[32,16,128]{2,1,0:T(8,128)S(1)} %add.20), channel_id=1, replica_groups={{0,16,32,48,64,80,96,112,128,144,160,176,192,208,224,240,256,272,288,30..., dimensions={0} | all-to-all | bytes 524288 | tf_op jit(solution)/shard_map/all_to_all | solution.py:627
  86.4 11.5 %all_to_all.22 = f32[8,16,128]{2,1,0:T(8,128)S(1)} all-to-all(f32[8,16,128]{2,1,0:T(8,128)S(1)} %broadcast_in_dim.2), channel_id=1, replica_groups=mesh['dp'=64,'graph'=8] {'graph'}, dimensions={0} | all-to-all | bytes 131072 | tf_op jit(solution)/shard_map/all_to_all | solution.py:630
  97.9 0.1 reshape_squeeze.3
  98.0 0.1 copy.24
  98.1 0.1 reshape.41
  98.2 0.1 maximum_bitcast_fusion
  98.3 0.1 copy.23
  98.4 0.2 reshape.40
  98.6 0.1 concatenate.7
  98.7 0.6 multiply_subtract_fusion.1
  (16 shorter events, 0.1 us)
Async XLA Ops:
  2.6 15.6 %copy-start.6 = (f32[8,128]{1,0:T(8,128)S(1)}, f32[8,128]{1,0:T(8,128)}, u32[]{:S(2)}) copy-start(f32[8,128]{1,0:T(8,128)} %get-tuple-element.29) | copy-start | bytes 12292
  2.6 32.9 %all-to-all-start = ((f32[64,16,128]{2,1,0:T(8,128)}), f32[64,16,128]{2,1,0:T(8,128)S(1)}, u32[]{:S(2)}, u32[]{:S(2)}) async-start(f32[64,16,128]{2,1,0:T(8,128)} %get-tuple-element.24), calls=%async_computation | async-start | bytes 1048576 | tf_op jit(solution)/shard_map/all_to_all | solution.py:611
  18.2 17.3 %collective-permute-start.1 = (f32[8,128]{1,0:T(8,128)S(1)}, f32[8,128]{1,0:T(8,128)S(1)}, u32[]{:S(2)}, u32[]{:S(2)}) collective-permute-start(f32[8,128]{1,0:T(8,128)S(1)} %copy-done.6), channel_id=1, source_target_pairs={{0,7},{1,2},{2,1},{3,4},{4,3},{5,6},{6,5},{7,0},{8,15},{9,10},{10,... | collective-permute-start | bytes 12296 | tf_op jit(solution)/shard_map/ppermute | solution.py:613
  25.1 10.4 %collective-permute-start = (f32[8,128]{1,0:T(8,128)S(1)}, f32[8,128]{1,0:T(8,128)S(1)}, u32[]{:S(2)}, u32[]{:S(2)}) collective-permute-start(f32[8,128]{1,0:T(8,128)S(1)} %copy-done.6), channel_id=1, source_target_pairs={{0,1},{1,0},{2,3},{3,2},{4,5},{5,4},{6,7},{7,6},{8,9},{9,8},{10,11... | collective-permute-start | bytes 12296 | tf_op jit(solution)/shard_map/ppermute | solution.py:612
  28.3 0.7 copy-start.3
  29.0 0.7 copy-start.4
  29.0 0.7 copy-start.5
  29.7 5.8 %copy-start.2 = (f32[16,128]{1,0:T(8,128)S(1)}, f32[16,128]{1,0:T(8,128)}, u32[]{:S(2)}) copy-start(f32[16,128]{1,0:T(8,128)} %get-tuple-element.28.own) | copy-start | bytes 24580
  29.7 5.8 %copy-start.1 = (s32[1,1,2048]{2,1,0:T(1,128)S(1)}, s32[1,1,2048]{2,1,0:T(1,128)}, u32[]{:S(2)}) copy-start(s32[1,1,2048]{2,1,0:T(1,128)} %param.17) | copy-start | bytes 24580
  29.7 5.8 %copy-start = (s32[1,1,2048]{2,1,0:T(1,128)S(1)}, s32[1,1,2048]{2,1,0:T(1,128)}, u32[]{:S(2)}) copy-start(s32[1,1,2048]{2,1,0:T(1,128)} %param.16) | copy-start | bytes 24580
  63.3 4.9 %collective-permute-start.2 = (f32[32,16,128]{2,1,0:T(8,128)S(1)}, f32[32,16,128]{2,1,0:T(8,128)S(1)}, u32[]{:S(2)}, u32[]{:S(2)}) collective-permute-start(f32[32,16,128]{2,1,0:T(8,128)S(1)} %get-tuple-element.37), channel_id=1, source_target_pairs={{0,8},{8,0},{16,24},{24,16},{32,40},{40,32},{48,56},{56,48},{64,72... | collective-permute-start | bytes 786440 | tf_op jit(solution)/shard_map/ppermute | solution.py:624

commit v6 on v5

--- a/solution.py
+++ b/solution.py
@@ -206,10 +206,16 @@
     return hot_s, hot_t
 
 
+def hot_kernel(src, dst, src_hot, dst_hot):
+    for i in range(CHUNKS):
+        at = pl.ds(i * EC, EC)
+        src_hot[:, at], dst_hot[:, at] = one_hots(src[:, at], dst[:, at])
+
+
 def forward_kernel(
-    slabs, count_ref, scalars, energy_ref, wg, own, first_ghost, second_ghost, src, dst,
+    slabs, count_ref, scalars, energy_ref, wg, own, first_ghost, second_ghost, dst, src_hot, dst_hot,
     message, atoms, rows_out, vec_out, dfilt_out, q_out,
-    src_hot, dst_hot, total, force_total,
+    total, force_total,
 ):
 
     count = count_ref[0, 0]
@@ -251,9 +257,8 @@
     for i in range(CHUNKS):
         at = pl.ds(i * EC, EC)
         t = dst[:, at]
-        hot_s, hot_t = one_hots(src[:, at], t)
-        src_hot[:, at] = hot_s
-        dst_hot[:, at] = hot_t
+        hot_s = src_hot[:, at]
+        hot_t = dst_hot[:, at]
         vec = whole(mm(pieces[:, :N], hot_s, NN) - mm(pieces[:, :A], hot_t, NN))
         vec_out[:, at] = vec
         square = jnp.sum(vec * vec, axis=0, keepdims=True)
@@ -336,7 +341,7 @@
 
 def backward_kernel(
     slabs, count_ref, scalars, wg, src, dst, received, atoms, rows_in, vec_in, dfilt_in, q_in,
-    forces_out, energy_out, stress_out, keep, give,
+    forces_far, energy_far, stress_far, keep, give, forces_out, energy_out, stress_out, sems,
     src_hot, dst_hot, grad, step_row, total, source_total, one_total, two_total,
 ):
 
@@ -370,6 +375,10 @@
         forces_out[i] = force_own[i : i + 1]
         stress_out[i] = got[3:4, 3 * i : 3 * i + 3] / volume
     energy_out[...] = energy
+    results = ((forces_out, forces_far), (energy_out, energy_far), (stress_out, stress_far))
+    copies = [pltpu.make_async_copy(near, far, sems.at[k]) for k, (near, far) in enumerate(results)]
+    for copy in copies:
+        copy.start()
     own_ref = jnp.concatenate([own[4:8], jnp.zeros((4, 128), f32)], axis=0)
     ghost_ref = jnp.concatenate([ghost[4:8], jnp.zeros((4, 128), f32)], axis=0)
     factor = force_weight * scale
@@ -498,10 +507,13 @@
     for j in range(32):
         keep[j] = grad[2 * j + core]
         give[j] = grad[2 * j + 1 - core]
+    for copy in copies:
+        copy.wait()
 
 
 vmem = pl.BlockSpec(memory_space=pltpu.VMEM)
 smem = pl.BlockSpec(memory_space=pltpu.SMEM)
+far = pl.BlockSpec(memory_space=pl.ANY)
 params_vmem = pltpu.CompilerParams(vmem_limit_bytes=32 * 1024 * 1024)
 
 
@@ -520,6 +532,17 @@
     )(*arrays)
 
 
+def edge_hots(src, dst):
+    return pl.pallas_call(
+        hot_kernel,
+        out_shape=[shape(N, E, dtype=bf16), shape(A, E, dtype=bf16)],
+        in_specs=[vmem] * 2,
+        out_specs=[vmem] * 2,
+        compiler_params=params_vmem,
+        name="edge_hots",
+    )(src, dst)
+
+
 def forward(slabs, counts, scalars, energy_ref, *arrays):
     return pl.pallas_call(
         functools.partial(forward_kernel, slabs),
@@ -527,8 +550,6 @@
         in_specs=[smem] * 3 + [vmem] * len(arrays),
         out_specs=[vmem] * (1 + len(KEPT)),
         scratch_shapes=[
-            pltpu.VMEM((N, E), bf16),
-            pltpu.VMEM((A, E), bf16),
             pltpu.VMEM((2 * C, A), f32),
             pltpu.VMEM((24, 256), f32),
         ],
@@ -543,8 +564,10 @@
         functools.partial(backward_kernel, slabs),
         out_shape=outs,
         in_specs=[smem] * 2 + [vmem] * len(arrays),
-        out_specs=[vmem] * len(outs),
-        scratch_shapes=[
+        out_specs=[far] * 3 + [vmem] * 2,
+        scratch_shapes=[pltpu.VMEM(out.shape, f32) for out in outs[:3]]
+        + [
+            pltpu.SemaphoreType.DMA((3,)),
             pltpu.VMEM((N, E), bf16),
             pltpu.VMEM((A, E), bf16),
             pltpu.VMEM((64, BLOCKS, 128), f32),
@@ -613,9 +636,11 @@
     second = lax.ppermute(
         outgoing, "graph", [(i, (i + (1 if i % 2 else slabs - 1)) % slabs) for i in range(slabs)]
     )
-    wg, decayed = lax.optimization_barrier((wg, decay(params, moment_one, moment_two)))
+    wg, decayed, hots = lax.optimization_barrier(
+        (wg, decay(params, moment_one, moment_two), edge_hots(source[0], target[0]))
+    )
     message, *kept = forward(
-        slabs, counts, scalars, energy_ref, wg, own, first, second, source[0], target[0]
+        slabs, counts, scalars, energy_ref, wg, own, first, second, target[0], *hots
     )
     received = lax.all_to_all(message, "graph", 0, 0, tiled=True)
     forces, energy, stress, keep, give = backward(

time: 101 us -> 101 us (level)
  no operation moved by 1% of the time
where the time goes in v6:
time: 101 us; the launch traced here: 99.3 us
  blocking collectives  44.9 us (44%)
  starting transfers between devices  29.4 us (29%)
  Pallas kernels  14.6 us (14%)
  waiting for transfers between devices  5.25 us (5%)
  between operations  2.11 us (2%)
  local copies, waits for them, and re-layouts  2.1 us (2%)
    all_to_all x1, blocking collectives, body(): lax.all_to_all(pair, 'dp', 0, 0, tiled=True, axis_index_groups=chips)  18.1 us
    all_to_all x1, starting transfers between devices, body(): wg = lax.all_to_all(blocks, 'dp', 0, 0, tiled=True)  15.5 us
    all_to_all x1, blocking collectives, body(): received = lax.all_to_all(message, 'graph', 0, 0, tiled=True)  15.4 us
    all_to_all x1, blocking collectives, body(): lax.all_to_all(copies, 'graph', 0, 0, tiled=True)  11.5 us
    pallas_call x1, Pallas kernels, backward(): pl.pallas_call(functools.partial(backward_kernel, slabs), out_shape=outs,...  7.51 us
    ppermute x1, starting transfers between devices, body(): lax.ppermute(outgoing, 'graph', [(i, (i + (1 if i % 2 else slabs - 1)) %...  6.95 us
    pallas_call x1, Pallas kernels, forward(): pl.pallas_call(functools.partial(forward_kernel, slabs), out_shape=[shape...  4.88 us
    all_to_all x1, waiting for transfers between devices, body(): wg = lax.all_to_all(blocks, 'dp', 0, 0, tiled=True)  4.11 us
  transfers between devices with their start and end apart: 4, of which 2 were waited for; matrix products, arithmetic and copies ran while one was open for 0% of the time, Pallas kernels for 0%

profile of v6, /device:TPU:1, one launch (start us, length us, event | category | flops | bytes accessed | tf_op | source)
XLA Modules:
  0.0 99.3 jit_solution(16679174484083154722)
XLA Ops:
  0.6 2.0 %prepare.1 = (f32[16,128]{1,0:T(8,128)}, f32[8,128]{1,0:T(8,128)}, f32[64,16,128]{2,1,0:T(8,128)}) custom-call(f32[3,1,128]{2,1,0:T(1,128)} %bitcast.26, s32[1,128]{1,0:T(1,128)} %bitcast.29, f32[3,1,128]{2,1,0:T(1,128)} %bitcast.27, s32[1,32]{1,0:T(1,128)} %bitcast.30, s32[1,32]{1,0:T(1,128)} %bitcast.31, f32[3,1,3]{2,1,0:T(1,128)} %bitcast.28, f32[1920]{0:T(1024)} %shard.1), custom_call_target="tpu_custom_call" | custom-call | tf_op jit(solution)/shard_map/prepare/pallas_call | solution.py:525
  2.6 15.5 %all-to-all-start = ((f32[64,16,128]{2,1,0:T(8,128)}), f32[64,16,128]{2,1,0:T(8,128)S(1)}, u32[]{:S(2)}, u32[]{:S(2)}) async-start(f32[64,16,128]{2,1,0:T(8,128)} %get-tuple-element.28), calls=%async_computation | async-start | bytes 1048576 | tf_op jit(solution)/shard_map/all_to_all | solution.py:634
  18.2 0.0 copy-done.6
  18.2 7.0 %collective-permute-start.1 = (f32[8,128]{1,0:T(8,128)S(1)}, f32[8,128]{1,0:T(8,128)S(1)}, u32[]{:S(2)}, u32[]{:S(2)}) collective-permute-start(f32[8,128]{1,0:T(8,128)S(1)} %copy-done.6), channel_id=1, source_target_pairs={{0,7},{1,2},{2,1},{3,4},{4,3},{5,6},{6,5},{7,0},{8,15},{9,10},{10,... | collective-permute-start | bytes 12296 | tf_op jit(solution)/shard_map/ppermute | solution.py:636
  25.1 3.2 %collective-permute-start = (f32[8,128]{1,0:T(8,128)S(1)}, f32[8,128]{1,0:T(8,128)S(1)}, u32[]{:S(2)}, u32[]{:S(2)}) collective-permute-start(f32[8,128]{1,0:T(8,128)S(1)} %copy-done.6), channel_id=1, source_target_pairs={{0,1},{1,0},{2,3},{3,2},{4,5},{5,4},{6,7},{7,6},{8,9},{9,8},{10,11... | collective-permute-start | bytes 12296 | tf_op jit(solution)/shard_map/ppermute | solution.py:635
  28.3 0.0 copy-start.3
  28.3 0.7 copy-done.3
  29.0 0.7 copy-done.4
  29.7 0.0 copy-done.5
  29.7 0.1 pad_add_fusion.scalars
  31.1 0.0 copy-done.1
  31.1 0.0 copy-done
  31.1 0.2 edge_hots.1
  31.4 0.0 copy-start.2
  31.4 4.1 %all-to-all-done.wg = f32[64,16,128]{2,1,0:T(8,128)S(1)} async-done(((f32[64,16,128]{2,1,0:T(8,128)}), f32[64,16,128]{2,1,0:T(8,128)S(1)}, u32[]{:S(2)}, u32[]{:S(2)}) %all-to-all-start) | async-done | bytes 524320 | tf_op jit(solution)/shard_map/all_to_all | solution.py:634
  35.5 0.0 collective-permute-done.1.second_ghost
  35.5 0.0 collective-permute-done.first_ghost
  35.5 4.9 %energy_slopes.1 = (f32[8,4,128]{2,1,0:T(4,128)S(1)}, f32[1192,128]{1,0:T(8,128)S(1)}, f32[8,2048]{1,0:T(8,128)S(1)}, f32[8,2048]{1,0:T(8,128)S(1)}, f32[128,2048]{1,0:T(8,128)S(1)}, /*index=5*/f32[128,2048]{1,0:T(8,128)S(1)}) custom-call(s32[1,1]{1,0:T(1,128)S(6)} %copy.26.count_ref, s32[2]{0:T(128)S(1)} %pad_add_fusion.scalars, f32[1]{0:T(128)S(6)} %copy.27.energy_ref, ...), custom_call_target="tpu_custom_call" | custom-call | tf_op jit(solution)/shard_map/energy_slopes/pallas_call | solution.py:547
  40.4 15.4 %all_to_all.20.received = f32[8,4,128]{2,1,0:T(4,128)S(1)} all-to-all(f32[8,4,128]{2,1,0:T(4,128)S(1)} %get-tuple-element.38), channel_id=1, replica_groups=mesh['dp'=64,'graph'=8] {'graph'}, dimensions={0} | all-to-all | bytes 32768 | tf_op jit(solution)/shard_map/all_to_all | solution.py:645
  55.7 7.5 %weight_gradients.1 = (f32[3,1,128]{2,1,0:T(1,128)}, f32[1,1]{1,0:T(1,128)}, f32[3,1,3]{2,1,0:T(1,128)}, f32[32,16,128]{2,1,0:T(8,128)S(1)}, f32[32,16,128]{2,1,0:T(8,128)S(1)}) custom-call(s32[1,1]{1,0:T(1,128)S(6)} %copy.26.count_ref, s32[2]{0:T(128)S(1)} %pad_add_fusion.scalars, f32[64,16,128]{2,1,0:T(8,128)S(1)} %all-to-all-done.wg, ...), custom_call_target="tpu_custom_call" | custom-call | tf_op jit(solution)/shard_map/weight_gradients/pallas_call | solution.py:563
  63.2 3.8 %collective-permute-start.2 = (f32[32,16,128]{2,1,0:T(8,128)S(1)}, f32[32,16,128]{2,1,0:T(8,128)S(1)}, u32[]{:S(2)}, u32[]{:S(2)}) collective-permute-start(f32[32,16,128]{2,1,0:T(8,128)S(1)} %get-tuple-element.45), channel_id=1, source_target_pairs={{0,8},{8,0},{16,24},{24,16},{32,40},{40,32},{48,56},{56,48},{64,72... | collective-permute-start | bytes 786440 | tf_op jit(solution)/shard_map/ppermute | solution.py:649
  67.0 1.1 %collective-permute-done.2 = f32[32,16,128]{2,1,0:T(8,128)S(1)} collective-permute-done((f32[32,16,128]{2,1,0:T(8,128)S(1)}, f32[32,16,128]{2,1,0:T(8,128)S(1)}, u32[]{:S(2)}, u32[]{:S(2)}) %collective-permute-start.2) | collective-permute-done | bytes 262176 | tf_op jit(solution)/shard_map/ppermute | solution.py:649
  68.2 18.1 %all_to_all.21 = f32[32,16,128]{2,1,0:T(8,128)S(1)} all-to-all(f32[32,16,128]{2,1,0:T(8,128)S(1)} %add.20), channel_id=1, replica_groups={{0,16,32,48,64,80,96,112,128,144,160,176,192,208,224,240,256,272,288,30..., dimensions={0} | all-to-all | bytes 524288 | tf_op jit(solution)/shard_map/all_to_all | solution.py:652
  86.4 11.5 %all_to_all.22 = f32[8,16,128]{2,1,0:T(8,128)S(1)} all-to-all(f32[8,16,128]{2,1,0:T(8,128)S(1)} %broadcast_in_dim.2), channel_id=1, replica_groups=mesh['dp'=64,'graph'=8] {'graph'}, dimensions={0} | all-to-all | bytes 131072 | tf_op jit(solution)/shard_map/all_to_all | solution.py:655
  97.9 0.1 reshape_squeeze.3
  98.0 0.1 copy.24
  98.1 0.1 reshape.41
  98.2 0.1 maximum_bitcast_fusion
  98.3 0.1 copy.23
  98.4 0.2 reshape.40
  98.6 0.1 concatenate.7
  98.7 0.6 multiply_subtract_fusion.1
  (17 shorter events, 0.1 us)
Async XLA Ops:
  2.6 15.6 %copy-start.6 = (f32[8,128]{1,0:T(8,128)S(1)}, f32[8,128]{1,0:T(8,128)}, u32[]{:S(2)}) copy-start(f32[8,128]{1,0:T(8,128)} %get-tuple-element.35) | copy-start | bytes 12292
  2.6 32.9 %all-to-all-start = ((f32[64,16,128]{2,1,0:T(8,128)}), f32[64,16,128]{2,1,0:T(8,128)S(1)}, u32[]{:S(2)}, u32[]{:S(2)}) async-start(f32[64,16,128]{2,1,0:T(8,128)} %get-tuple-element.28), calls=%async_computation | async-start | bytes 1048576 | tf_op jit(solution)/shard_map/all_to_all | solution.py:634
  18.2 17.3 %collective-permute-start.1 = (f32[8,128]{1,0:T(8,128)S(1)}, f32[8,128]{1,0:T(8,128)S(1)}, u32[]{:S(2)}, u32[]{:S(2)}) collective-permute-start(f32[8,128]{1,0:T(8,128)S(1)} %copy-done.6), channel_id=1, source_target_pairs={{0,7},{1,2},{2,1},{3,4},{4,3},{5,6},{6,5},{7,0},{8,15},{9,10},{10,... | collective-permute-start | bytes 12296 | tf_op jit(solution)/shard_map/ppermute | solution.py:636
  25.1 10.4 %collective-permute-start = (f32[8,128]{1,0:T(8,128)S(1)}, f32[8,128]{1,0:T(8,128)S(1)}, u32[]{:S(2)}, u32[]{:S(2)}) collective-permute-start(f32[8,128]{1,0:T(8,128)S(1)} %copy-done.6), channel_id=1, source_target_pairs={{0,1},{1,0},{2,3},{3,2},{4,5},{5,4},{6,7},{7,6},{8,9},{9,8},{10,11... | collective-permute-start | bytes 12296 | tf_op jit(solution)/shard_map/ppermute | solution.py:635
  28.3 0.7 copy-start.3
  29.0 0.7 copy-start.4
  29.0 0.7 copy-start.5
  29.7 1.4 %copy-start.1 = (s32[1,1,2048]{2,1,0:T(1,128)S(1)}, s32[1,1,2048]{2,1,0:T(1,128)}, u32[]{:S(2)}) copy-start(s32[1,1,2048]{2,1,0:T(1,128)} %param.16) | copy-start | bytes 24580
  29.7 1.4 %copy-start = (s32[1,1,2048]{2,1,0:T(1,128)S(1)}, s32[1,1,2048]{2,1,0:T(1,128)}, u32[]{:S(2)}) copy-start(s32[1,1,2048]{2,1,0:T(1,128)} %param.17) | copy-start | bytes 24580
  31.4 4.1 %copy-start.2 = (f32[16,128]{1,0:T(8,128)S(1)}, f32[16,128]{1,0:T(8,128)}, u32[]{:S(2)}) copy-start(f32[16,128]{1,0:T(8,128)} %get-tuple-element.34.own) | copy-start | bytes 24580
  63.2 4.9 %collective-permute-start.2 = (f32[32,16,128]{2,1,0:T(8,128)S(1)}, f32[32,16,128]{2,1,0:T(8,128)S(1)}, u32[]{:S(2)}, u32[]{:S(2)}) collective-permute-start(f32[32,16,128]{2,1,0:T(8,128)S(1)} %get-tuple-element.45), channel_id=1, source_target_pairs={{0,8},{8,0},{16,24},{24,16},{32,40},{40,32},{48,56},{56,48},{64,72... | collective-permute-start | bytes 786440 | tf_op jit(solution)/shard_map/ppermute | solution.py:649

commit v7 on v6

--- a/solution.py
+++ b/solution.py
@@ -480,10 +480,18 @@
         inner = stack(a * sig)
         filt = wdot(two_t, inner) * gate
         source_total[...] += mm(stack(m_bar * filt + dm_bar * (dfilt_in[:, at] * step)), hot_s, NT)
-        two_total[...] += mm(f_bar, inner, NT) + mm(df_bar, stack(slope * moved_a), NT)
+        two_total[...] += mm(
+            jnp.concatenate([f_bar, df_bar], axis=1),
+            jnp.concatenate([inner, stack(slope * moved_a)], axis=1),
+            NT,
+        )
         a_bar = stack(s_bar * slope + ds_bar * (second * moved_a))
         da_bar = stack(ds_bar * slope)
-        one_total[...] += mm(a_bar, basis, NT) + mm(da_bar, moved_basis, NT)
+        one_total[...] += mm(
+            jnp.concatenate([a_bar, da_bar], axis=1),
+            jnp.concatenate([basis, moved_basis], axis=1),
+            NT,
+        )
 
     one_grad = fold(one_total[...])
     grad[:, 2, :] = jnp.concatenate([one_grad[:64], one_grad[64:]], axis=1)

time: 101 us -> 101 us (level)
  no operation moved by 1% of the time
where the time goes in v7:
time: 101 us; the launch traced here: 99.1 us
  blocking collectives  44.9 us (44%)
  starting transfers between devices  29.4 us (29%)
  Pallas kernels  14.4 us (14%)
  waiting for transfers between devices  5.25 us (5%)
  between operations  2.11 us (2%)
  local copies, waits for them, and re-layouts  2.1 us (2%)
    all_to_all x1, blocking collectives, body(): lax.all_to_all(pair, 'dp', 0, 0, tiled=True, axis_index_groups=chips)  18.1 us
    all_to_all x1, starting transfers between devices, body(): wg = lax.all_to_all(blocks, 'dp', 0, 0, tiled=True)  15.5 us
    all_to_all x1, blocking collectives, body(): received = lax.all_to_all(message, 'graph', 0, 0, tiled=True)  15.4 us
    all_to_all x1, blocking collectives, body(): lax.all_to_all(copies, 'graph', 0, 0, tiled=True)  11.5 us
    pallas_call x1, Pallas kernels, backward(): pl.pallas_call(functools.partial(backward_kernel, slabs), out_shape=outs,...  7.37 us
    ppermute x1, starting transfers between devices, body(): lax.ppermute(outgoing, 'graph', [(i, (i + (1 if i % 2 else slabs - 1)) %...  6.95 us
    pallas_call x1, Pallas kernels, forward(): pl.pallas_call(functools.partial(forward_kernel, slabs), out_shape=[shape...  4.88 us
    all_to_all x1, waiting for transfers between devices, body(): wg = lax.all_to_all(blocks, 'dp', 0, 0, tiled=True)  4.11 us
  transfers between devices with their start and end apart: 4, of which 2 were waited for; matrix products, arithmetic and copies ran while one was open for 0% of the time, Pallas kernels for 0%

profile of v7, /device:TPU:1, one launch (start us, length us, event | category | flops | bytes accessed | tf_op | source)
XLA Modules:
  0.0 99.1 jit_solution(10891314367654430733)
XLA Ops:
  0.6 2.0 %prepare.1 = (f32[16,128]{1,0:T(8,128)}, f32[8,128]{1,0:T(8,128)}, f32[64,16,128]{2,1,0:T(8,128)}) custom-call(f32[3,1,128]{2,1,0:T(1,128)} %bitcast.26, s32[1,128]{1,0:T(1,128)} %bitcast.29, f32[3,1,128]{2,1,0:T(1,128)} %bitcast.27, s32[1,32]{1,0:T(1,128)} %bitcast.30, s32[1,32]{1,0:T(1,128)} %bitcast.31, f32[3,1,3]{2,1,0:T(1,128)} %bitcast.28, f32[1920]{0:T(1024)} %shard.1), custom_call_target="tpu_custom_call" | custom-call | tf_op jit(solution)/shard_map/prepare/pallas_call | solution.py:533
  2.6 15.5 %all-to-all-start = ((f32[64,16,128]{2,1,0:T(8,128)}), f32[64,16,128]{2,1,0:T(8,128)S(1)}, u32[]{:S(2)}, u32[]{:S(2)}) async-start(f32[64,16,128]{2,1,0:T(8,128)} %get-tuple-element.28), calls=%async_computation | async-start | bytes 1048576 | tf_op jit(solution)/shard_map/all_to_all | solution.py:642
  18.2 0.0 copy-done.6
  18.2 7.0 %collective-permute-start.1 = (f32[8,128]{1,0:T(8,128)S(1)}, f32[8,128]{1,0:T(8,128)S(1)}, u32[]{:S(2)}, u32[]{:S(2)}) collective-permute-start(f32[8,128]{1,0:T(8,128)S(1)} %copy-done.6), channel_id=1, source_target_pairs={{0,7},{1,2},{2,1},{3,4},{4,3},{5,6},{6,5},{7,0},{8,15},{9,10},{10,... | collective-permute-start | bytes 12296 | tf_op jit(solution)/shard_map/ppermute | solution.py:644
  25.1 3.2 %collective-permute-start = (f32[8,128]{1,0:T(8,128)S(1)}, f32[8,128]{1,0:T(8,128)S(1)}, u32[]{:S(2)}, u32[]{:S(2)}) collective-permute-start(f32[8,128]{1,0:T(8,128)S(1)} %copy-done.6), channel_id=1, source_target_pairs={{0,1},{1,0},{2,3},{3,2},{4,5},{5,4},{6,7},{7,6},{8,9},{9,8},{10,11... | collective-permute-start | bytes 12296 | tf_op jit(solution)/shard_map/ppermute | solution.py:643
  28.3 0.0 copy-start.3
  28.3 0.7 copy-done.3
  29.0 0.7 copy-done.4
  29.7 0.0 copy-done.5
  29.7 0.1 pad_add_fusion.scalars
  31.1 0.0 copy-done.1
  31.1 0.0 copy-done
  31.1 0.2 edge_hots.1
  31.4 0.0 copy-start.2
  31.4 4.1 %all-to-all-done.wg = f32[64,16,128]{2,1,0:T(8,128)S(1)} async-done(((f32[64,16,128]{2,1,0:T(8,128)}), f32[64,16,128]{2,1,0:T(8,128)S(1)}, u32[]{:S(2)}, u32[]{:S(2)}) %all-to-all-start) | async-done | bytes 524320 | tf_op jit(solution)/shard_map/all_to_all | solution.py:642
  35.5 0.0 collective-permute-done.1.second_ghost
  35.5 0.0 collective-permute-done.first_ghost
  35.5 4.9 %energy_slopes.1 = (f32[8,4,128]{2,1,0:T(4,128)S(1)}, f32[1192,128]{1,0:T(8,128)S(1)}, f32[8,2048]{1,0:T(8,128)S(1)}, f32[8,2048]{1,0:T(8,128)S(1)}, f32[128,2048]{1,0:T(8,128)S(1)}, /*index=5*/f32[128,2048]{1,0:T(8,128)S(1)}) custom-call(s32[1,1]{1,0:T(1,128)S(6)} %copy.26.count_ref, s32[2]{0:T(128)S(1)} %pad_add_fusion.scalars, f32[1]{0:T(128)S(6)} %copy.27.energy_ref, ...), custom_call_target="tpu_custom_call" | custom-call | tf_op jit(solution)/shard_map/energy_slopes/pallas_call | solution.py:555
  40.4 15.4 %all_to_all.20.received = f32[8,4,128]{2,1,0:T(4,128)S(1)} all-to-all(f32[8,4,128]{2,1,0:T(4,128)S(1)} %get-tuple-element.38), channel_id=1, replica_groups=mesh['dp'=64,'graph'=8] {'graph'}, dimensions={0} | all-to-all | bytes 32768 | tf_op jit(solution)/shard_map/all_to_all | solution.py:653
  55.7 7.4 %weight_gradients.1 = (f32[3,1,128]{2,1,0:T(1,128)}, f32[1,1]{1,0:T(1,128)}, f32[3,1,3]{2,1,0:T(1,128)}, f32[32,16,128]{2,1,0:T(8,128)S(1)}, f32[32,16,128]{2,1,0:T(8,128)S(1)}) custom-call(s32[1,1]{1,0:T(1,128)S(6)} %copy.26.count_ref, s32[2]{0:T(128)S(1)} %pad_add_fusion.scalars, f32[64,16,128]{2,1,0:T(8,128)S(1)} %all-to-all-done.wg, ...), custom_call_target="tpu_custom_call" | custom-call | tf_op jit(solution)/shard_map/weight_gradients/pallas_call | solution.py:571
  63.1 3.8 %collective-permute-start.2 = (f32[32,16,128]{2,1,0:T(8,128)S(1)}, f32[32,16,128]{2,1,0:T(8,128)S(1)}, u32[]{:S(2)}, u32[]{:S(2)}) collective-permute-start(f32[32,16,128]{2,1,0:T(8,128)S(1)} %get-tuple-element.45), channel_id=1, source_target_pairs={{0,8},{8,0},{16,24},{24,16},{32,40},{40,32},{48,56},{56,48},{64,72... | collective-permute-start | bytes 786440 | tf_op jit(solution)/shard_map/ppermute | solution.py:657
  66.9 1.1 %collective-permute-done.2 = f32[32,16,128]{2,1,0:T(8,128)S(1)} collective-permute-done((f32[32,16,128]{2,1,0:T(8,128)S(1)}, f32[32,16,128]{2,1,0:T(8,128)S(1)}, u32[]{:S(2)}, u32[]{:S(2)}) %collective-permute-start.2) | collective-permute-done | bytes 262176 | tf_op jit(solution)/shard_map/ppermute | solution.py:657
  68.1 18.1 %all_to_all.21 = f32[32,16,128]{2,1,0:T(8,128)S(1)} all-to-all(f32[32,16,128]{2,1,0:T(8,128)S(1)} %add.20), channel_id=1, replica_groups={{0,16,32,48,64,80,96,112,128,144,160,176,192,208,224,240,256,272,288,30..., dimensions={0} | all-to-all | bytes 524288 | tf_op jit(solution)/shard_map/all_to_all | solution.py:660
  86.2 11.5 %all_to_all.22 = f32[8,16,128]{2,1,0:T(8,128)S(1)} all-to-all(f32[8,16,128]{2,1,0:T(8,128)S(1)} %broadcast_in_dim.2), channel_id=1, replica_groups=mesh['dp'=64,'graph'=8] {'graph'}, dimensions={0} | all-to-all | bytes 131072 | tf_op jit(solution)/shard_map/all_to_all | solution.py:663
  97.8 0.1 reshape_squeeze.3
  97.8 0.1 copy.24
  98.0 0.1 reshape.41
  98.0 0.1 maximum_bitcast_fusion
  98.1 0.1 copy.23
  98.3 0.2 reshape.40
  98.4 0.1 concatenate.7
  98.5 0.6 multiply_subtract_fusion.1
  (17 shorter events, 0.1 us)
Async XLA Ops:
  2.6 15.6 %copy-start.6 = (f32[8,128]{1,0:T(8,128)S(1)}, f32[8,128]{1,0:T(8,128)}, u32[]{:S(2)}) copy-start(f32[8,128]{1,0:T(8,128)} %get-tuple-element.35) | copy-start | bytes 12292
  2.6 32.9 %all-to-all-start = ((f32[64,16,128]{2,1,0:T(8,128)}), f32[64,16,128]{2,1,0:T(8,128)S(1)}, u32[]{:S(2)}, u32[]{:S(2)}) async-start(f32[64,16,128]{2,1,0:T(8,128)} %get-tuple-element.28), calls=%async_computation | async-start | bytes 1048576 | tf_op jit(solution)/shard_map/all_to_all | solution.py:642
  18.2 17.3 %collective-permute-start.1 = (f32[8,128]{1,0:T(8,128)S(1)}, f32[8,128]{1,0:T(8,128)S(1)}, u32[]{:S(2)}, u32[]{:S(2)}) collective-permute-start(f32[8,128]{1,0:T(8,128)S(1)} %copy-done.6), channel_id=1, source_target_pairs={{0,7},{1,2},{2,1},{3,4},{4,3},{5,6},{6,5},{7,0},{8,15},{9,10},{10,... | collective-permute-start | bytes 12296 | tf_op jit(solution)/shard_map/ppermute | solution.py:644
  25.1 10.4 %collective-permute-start = (f32[8,128]{1,0:T(8,128)S(1)}, f32[8,128]{1,0:T(8,128)S(1)}, u32[]{:S(2)}, u32[]{:S(2)}) collective-permute-start(f32[8,128]{1,0:T(8,128)S(1)} %copy-done.6), channel_id=1, source_target_pairs={{0,1},{1,0},{2,3},{3,2},{4,5},{5,4},{6,7},{7,6},{8,9},{9,8},{10,11... | collective-permute-start | bytes 12296 | tf_op jit(solution)/shard_map/ppermute | solution.py:643
  28.3 0.7 copy-start.3
  29.0 0.7 copy-start.4
  29.0 0.7 copy-start.5
  29.7 1.4 %copy-start.1 = (s32[1,1,2048]{2,1,0:T(1,128)S(1)}, s32[1,1,2048]{2,1,0:T(1,128)}, u32[]{:S(2)}) copy-start(s32[1,1,2048]{2,1,0:T(1,128)} %param.16) | copy-start | bytes 24580
  29.7 1.4 %copy-start = (s32[1,1,2048]{2,1,0:T(1,128)S(1)}, s32[1,1,2048]{2,1,0:T(1,128)}, u32[]{:S(2)}) copy-start(s32[1,1,2048]{2,1,0:T(1,128)} %param.17) | copy-start | bytes 24580
  31.4 4.1 %copy-start.2 = (f32[16,128]{1,0:T(8,128)S(1)}, f32[16,128]{1,0:T(8,128)}, u32[]{:S(2)}) copy-start(f32[16,128]{1,0:T(8,128)} %get-tuple-element.34.own) | copy-start | bytes 24580
  63.1 4.9 %collective-permute-start.2 = (f32[32,16,128]{2,1,0:T(8,128)S(1)}, f32[32,16,128]{2,1,0:T(8,128)S(1)}, u32[]{:S(2)}, u32[]{:S(2)}) collective-permute-start(f32[32,16,128]{2,1,0:T(8,128)S(1)} %get-tuple-element.45), channel_id=1, source_target_pairs={{0,8},{8,0},{16,24},{24,16},{32,40},{40,32},{48,56},{56,48},{64,72... | collective-permute-start | bytes 786440 | tf_op jit(solution)/shard_map/ppermute | solution.py:657
